TPU v7x, 32 devices: a whole 2x2x4 slice. The times are simulated.
32 devices in a mesh: groups: 1, ep: 32 (over z, y, x, core).
Axes of the slice: x: 2, y: 2, z: 4, core: 2. Of those that a mesh axis runs over, the one named last changes fastest.
Arguments:
- moe_input: bfloat16 [1024, 3584], P(('groups', 'ep')), may hold values from -6 to 6
- route_ids: int32 [1024, 8], P(('groups', 'ep')), may hold values from 0 to 15, all different within a row; in each aligned block of 32 rows (0 to 31, 32 to 63, ...) at most 16 rows name the same one
- route_weights: float32 [1024, 8], P(('groups', 'ep')), may hold values from 0.05 to 1
- gate_weight: bfloat16 [32, 3584, 512], P('ep'), may hold values from -0.09375 to 0.09375
- up_weight: bfloat16 [32, 3584, 512], P('ep'), may hold values from -0.09375 to 0.09375
- down_weight: bfloat16 [32, 512, 3584], P('ep'), may hold values from -0.1875 to 0.1875
Outputs:
- moe_out: bfloat16 [1024, 3584], P(('groups', 'ep'))
Inputs may be any that keep to these rules, and one draw needn't show every extreme that they name: `route_ids`: each row names 8 different experts; within the 32 rows of one device no expert is named by more than 16 rows.
All inputs are finite; a program needn't handle non-finite values.
Results may differ from a plain program's by a relative error of at most 0.0058.
Values may be sent and summed in bfloat16 or wider, within the bound.
No kernel may reach another device: no remote copies, remote signals or barrier semaphores. Data moves between devices by JAX's collectives and lax.ppermute only.
A program may use at most 64 MiB of HBM per device.

v0:
```python
import jax
import jax.numpy as jnp
from jax import lax
from jax.sharding import PartitionSpec as P


def expert_part(inputs, gate_slice, up_slice, down_slice):
    leading_shape = inputs.shape[:-1]
    flattened = inputs.reshape(-1, inputs.shape[-1])
    gate_value = jnp.dot(flattened, gate_slice, preferred_element_type=jnp.float32)
    up_value = jnp.dot(flattened, up_slice, preferred_element_type=jnp.float32)
    hidden = (jax.nn.silu(gate_value) * up_value).astype(jnp.bfloat16)
    projected = jnp.dot(hidden, down_slice, preferred_element_type=jnp.float32)
    return projected.reshape(leading_shape + (down_slice.shape[1],))


def body(moe_input, route_ids, route_weights, gate_weight, up_weight, down_weight):
    rows_here = moe_input.shape[0]
    width = moe_input.shape[1]
    chosen_count = route_ids.shape[1]
    devices = lax.axis_size("ep")
    experts = devices // 2
    capacity = max(4, 2 * rows_here * chosen_count // devices)
    flat_ids = route_ids.reshape(-1)
    expert_iota = jnp.arange(experts, dtype=jnp.int32)
    member = (flat_ids[:, None] == expert_iota[None, :]).astype(jnp.int32)
    before = jnp.cumsum(member, axis=0) - member
    slot_index = jnp.sum(member * before, axis=1)
    target = flat_ids * capacity + slot_index
    slot_iota = jnp.arange(experts * capacity, dtype=jnp.int32)
    placed = (target[:, None] == slot_iota[None, :]).astype(jnp.float32)
    owners = jnp.arange(flat_ids.shape[0], dtype=jnp.int32) // chosen_count
    row_iota = jnp.arange(rows_here, dtype=jnp.int32)
    owner_table = (owners[:, None] == row_iota[None, :]).astype(jnp.float32)
    picker = jnp.dot(placed.T, owner_table, precision=lax.Precision.HIGHEST).astype(jnp.bfloat16)
    outgoing = jnp.dot(picker, moe_input, preferred_element_type=jnp.float32).astype(jnp.bfloat16)
    gate_slice = gate_weight[0]
    up_slice = up_weight[0]
    down_slice = down_weight[0]
    doubled = jnp.broadcast_to(
        outgoing.reshape(experts, 1, capacity, width), (experts, 2, capacity, width)
    ).reshape(devices, capacity, width)
    partial_sum = expert_part(
        lax.all_to_all(doubled, "ep", split_axis=0, concat_axis=0, tiled=True),
        gate_slice,
        up_slice,
        down_slice,
    )
    returned = lax.all_to_all(partial_sum, "ep", split_axis=0, concat_axis=0, tiled=True)
    halves = returned.reshape(experts, 2, capacity, width)
    merged = (halves[:, 0] + halves[:, 1]).astype(jnp.bfloat16)
    gathered = jnp.take(merged.reshape(experts * capacity, width), target, axis=0)
    weighted = (
        gathered.astype(jnp.float32).reshape(rows_here, chosen_count, width)
        * route_weights[:, :, None]
    )
    moe_out = jnp.sum(weighted, axis=1).astype(jnp.bfloat16)
    return moe_out


def solution(mesh):
    return jax.shard_map(
        body,
        mesh=mesh,
        in_specs=(
            P(("groups", "ep"), None),
            P(("groups", "ep"), None),
            P(("groups", "ep"), None),
            P("ep", None, None),
            P("ep", None, None),
            P("ep", None, None),
        ),
        out_specs=P(("groups", "ep"), None),
        check_vma=False,
    )
```

profile of v0, /device:TPU:0, one launch (start us, length us, event | category | flops | bytes accessed | tf_op | source)
XLA Modules:
  0.0 280.1 jit_solution(11066889480002171457)
XLA Ops:
  0.0 0.0 copy-start
  0.0 0.8 copy.9
  0.8 0.1 eq.52
  0.9 0.1 reshape.99
  1.0 0.6 reduce-window.6
  1.6 0.2 slice_reduce_fusion
  1.8 0.1 fusion.17
  1.9 0.4 convolution_convert_fusion.1
  2.3 0.0 copy-done
  2.3 0.6 convolution_convert_fusion
  2.9 0.4 broadcast_in_dim.25
  3.3 0.0 copy-start.3
  3.3 90.1 %all_to_all.10 = bf16[32,16,3584]{2,1,0:T(8,128)(2,1)S(1)} all-to-all(bf16[32,16,3584]{2,1,0:T(8,128)(2,1)S(1)} %bitcast.51), channel_id=1, replica_groups=mesh['groups'=1,'ep'=32] {'ep'}, dimensions={0} | all-to-all | bytes 7340032 | tf_op jit(solution)/shard_map/all_to_all | solution.py:44
  93.4 0.0 copy-done.3
  93.4 0.0 copy-start.4
  93.4 2.1 fusion.5
  95.5 0.0 copy-done.4
  95.5 0.0 copy-start.1
  95.5 2.1 fusion.10
  97.6 0.0 copy-done.1
  97.6 5.1 %fusion.1 = f32[32,16,3584]{2,1,0:T(8,128)} fusion(bf16[32,16,512]{2,1,0:T(8,128)(2,1)S(1)} %bitcast.55, bf16[1,512,3584]{2,1,0:T(8,128)(2,1)S(1)} %copy-done.1), kind=kOutput, calls=%fused_computation.4 | convolution fusion | flops 1879048192 | bytes 11534336 | tf_op jit(solution)/shard_map/dot_general | solution.py:13
  102.7 0.0 copy-start.2
  102.7 3.8 %all-to-all-start.1 = ((f32[32,16,3584]{2,1,0:T(8,128)}), f32[32,16,3584]{2,1,0:T(8,128)}, u32[]{:S(2)}, u32[]{:S(2)}) async-start(f32[32,16,3584]{2,1,0:T(8,128)} %fusion.1), calls=%async_computation.1 | async-start | bytes 14680064 | tf_op jit(solution)/shard_map/all_to_all | solution.py:49
  106.5 0.1 reduce_sum.23
  106.6 0.1 mul.51
  106.7 0.0 copy-done.2
  106.7 0.1 copy.13
  106.8 162.8 %all-to-all-done.1 = f32[32,16,3584]{2,1,0:T(8,128)} async-done(((f32[32,16,3584]{2,1,0:T(8,128)}), f32[32,16,3584]{2,1,0:T(8,128)}, u32[]{:S(2)}, u32[]{:S(2)}) %all-to-all-start.1) | async-done | bytes 7340064 | tf_op jit(solution)/shard_map/all_to_all | solution.py:49
  269.6 3.6 %fusion = bf16[16,1,16,3584]{3,2,1,0:T(8,128)(2,1)S(1)} fusion(f32[16,2,16,3584]{3,2,1,0:T(8,128)} %bitcast.9), kind=kLoop, calls=%fused_computation.3 | loop fusion | flops 1835008 | bytes 9175040 | tf_op jit(solution)/shard_map/convert_element_type | solution.py:51
  273.2 3.0 %gather_fusion = bf16[256,3584]{1,0:T(8,128)(2,1)} fusion(bf16[256,3584]{1,0:T(8,128)(2,1)S(1)} %bitcast.50, s32[1024]{0:T(1024)S(1)} %pad_clamp_fusion), kind=kCustom, calls=%fused_computation | custom fusion | bytes 3671040 | tf_op jit(solution)/shard_map/jit(_take)/gather | solution.py:52
  276.2 3.9 %multiply_reduce_fusion = bf16[32,3584]{1,0:T(8,128)(2,1)} fusion(bf16[256,3584]{1,0:T(8,128)(2,1)} %gather_fusion, f32[32,8]{1,0:T(8,128)S(1)} %copy.13, pred[32,8]{1,0:T(8,128)(4,1)S(1)} %compare_and_fusion), kind=kLoop, calls=%fused_computation.10 | loop fusion | flops 3555328 | bytes 2065664 | tf_op jit(solution)/shard_map/reduce_sum | solution.py:57
  (8 shorter events, 0.1 us)
Async XLA Ops:
  0.0 2.3 copy-start
  3.3 90.1 %copy-start.3 = (bf16[1,3584,512]{2,1,0:T(8,128)(2,1)S(1)}, bf16[1,3584,512]{2,1,0:T(8,128)(2,1)}, u32[]{:S(2)}) copy-start(bf16[1,3584,512]{2,1,0:T(8,128)(2,1)} %param.9) | copy-start | bytes 11010052
  93.4 2.1 copy-start.4
  95.5 2.2 copy-start.1
  102.7 4.0 %copy-start.2 = (f32[32,8]{0,1:T(8,128)S(1)}, f32[32,8]{0,1:T(8,128)}, u32[]{:S(2)}) copy-start(f32[32,8]{0,1:T(8,128)} %param.8) | copy-start | bytes 3076
  102.7 166.9 %all-to-all-start.1 = ((f32[32,16,3584]{2,1,0:T(8,128)}), f32[32,16,3584]{2,1,0:T(8,128)}, u32[]{:S(2)}, u32[]{:S(2)}) async-start(f32[32,16,3584]{2,1,0:T(8,128)} %fusion.1), calls=%async_computation.1 | async-start | bytes 14680064 | tf_op jit(solution)/shard_map/all_to_all | solution.py:49
where the time goes:
time: 280 us
  waiting for transfers between devices  163 us (58%)
  blocking collectives  90.1 us (32%)
  matrix products  10.3 us (4%)
  other arithmetic  8.23 us (3%)
  local copies, waits for them, and re-layouts  4.83 us (2%)
  starting transfers between devices  3.76 us (1%)
    all_to_all x1, waiting for transfers between devices, body(): lax.all_to_all(partial_sum, 'ep', split_axis=0, concat_axis=0, tiled=True)  163 us
    all_to_all x1, blocking collectives, body(): lax.all_to_all(doubled, 'ep', split_axis=0, concat_axis=0, tiled=True)  90.1 us
  transfers between devices with their start and end apart: 1, of which 1 were waited for; matrix products, arithmetic and copies ran while one was open for 0% of the time, Pallas kernels for 0%

commit v1 on v0

v1 whole, which is shorter than its diff:
```python
import functools

import jax
import jax.numpy as jnp
from jax import lax
from jax.experimental import pallas as pl
from jax.experimental.pallas import tpu as pltpu
from jax.sharding import PartitionSpec as P

F32, BF16 = jnp.float32, jnp.bfloat16
LANES = 128
TILE = 512


def whole_specs(count):
    return [pl.BlockSpec(memory_space=pltpu.VMEM)] * count


def call(kernel, out_shapes, *operands, flops=0):
    moved = sum(o.size * o.dtype.itemsize for o in operands)
    moved += sum(o.size * o.dtype.itemsize for o in out_shapes)
    return pl.pallas_call(
        kernel,
        out_shape=out_shapes,
        in_specs=whole_specs(len(operands)),
        out_specs=whole_specs(len(out_shapes)),
        compiler_params=pltpu.CompilerParams(vmem_limit_bytes=32 << 20),
        cost_estimate=pl.CostEstimate(flops=flops, bytes_accessed=moved, transcendentals=0),
    )(*operands)


def tiles(width):
    return [(start, min(TILE, width - start)) for start in range(0, width, TILE)]


def split3(value):
    high = value.astype(BF16)
    rest = value - high.astype(F32)
    middle = rest.astype(BF16)
    low = (rest - middle.astype(F32)).astype(BF16)
    return high, middle, low


def tag_kernel(experts, x_ref, ids_ref, weights_ref, out_ref):
    rows, width = x_ref.shape
    tag_lanes = out_ref.shape[1] - width
    lane = lax.broadcasted_iota(jnp.int32, (rows, tag_lanes), 1)
    expert = lane % experts
    group = lane // experts
    flags = jnp.zeros((rows, tag_lanes), F32)
    weights = jnp.zeros((rows, tag_lanes), F32)
    for k in range(ids_ref.shape[1]):
        match = ids_ref[:, k : k + 1] == expert
        flags = jnp.where(match, 1.0, flags)
        weights = jnp.where(match, weights_ref[:, k : k + 1], weights)
    high, middle, low = split3(weights)
    tag = jnp.where(
        group == 0,
        flags,
        jnp.where(
            group == 1,
            high.astype(F32),
            jnp.where(group == 2, middle.astype(F32), jnp.where(group == 3, low.astype(F32), 0.0)),
        ),
    )
    out_ref[:, :width] = x_ref[...]
    out_ref[:, width:] = tag.astype(BF16)


def pick_kernel(experts, cap, blocks, planes, e_ref, *refs):
    x_refs, outs = refs[:blocks], refs[blocks : blocks + planes]
    high_ref, middle_ref, low_ref = refs[blocks + planes :]
    rows = x_refs[0].shape[0]
    width = outs[0].shape[1]
    total = blocks * rows
    slots = blocks * cap
    tag = jnp.concatenate([x[:, width:] for x in x_refs], axis=0)
    tag_lanes = tag.shape[1]
    row = lax.broadcasted_iota(jnp.int32, (total, total), 0)
    col = lax.broadcasted_iota(jnp.int32, (total, total), 1)
    before = ((row // rows == col // rows) & (col < row)).astype(F32).astype(BF16)
    rank = jnp.dot(before, tag, preferred_element_type=F32)
    tag = tag.astype(F32)
    lane = lax.broadcasted_iota(jnp.int32, (total, tag_lanes), 1)
    block = lax.broadcasted_iota(jnp.int32, (total, 1), 0) // rows
    slot = lax.broadcasted_iota(jnp.int32, (total, planes * slots), 1)
    picked = jnp.zeros((total, planes * slots), F32)
    weight = jnp.zeros((total, planes * slots), F32)
    for j in range(planes):
        e = e_ref[0, j]
        here = lane == e
        flag = jnp.sum(jnp.where(here, tag, 0.0), axis=1, keepdims=True)
        place = jnp.sum(jnp.where(here, rank, 0.0), axis=1, keepdims=True).astype(jnp.int32)
        parts = (lane % experts == e) & (lane // experts >= 1) & (lane // experts <= 3)
        factor = jnp.sum(jnp.where(parts, tag, 0.0), axis=1, keepdims=True)
        target = jnp.where(flag > 0.0, j * slots + block * cap + place, -1)
        hit = slot == target
        picked = jnp.where(hit, 1.0, picked)
        weight = jnp.where(hit, factor, weight)
    high_ref[...], middle_ref[...], low_ref[...] = split3(weight)
    picker = picked.T.astype(BF16)
    for start, size in tiles(width):
        columns = pl.ds(start, size)
        x = jnp.concatenate([x[:, columns] for x in x_refs], axis=0)
        out = jnp.dot(picker, x, preferred_element_type=F32).astype(BF16)
        for j in range(planes):
            outs[j][:, columns] = out[j * slots : (j + 1) * slots]


def combine_kernel(blocks, planes, *refs):
    ret_refs = refs[:planes]
    high_ref, middle_ref, low_ref = refs[planes : planes + 3]
    outs = refs[planes + 3 :]
    rows, width = outs[0].shape
    for start, size in tiles(width):
        columns = pl.ds(start, size)
        y = jnp.concatenate([r[:, columns] for r in ret_refs], axis=0)
        total = jnp.dot(low_ref[...], y, preferred_element_type=F32)
        total += jnp.dot(middle_ref[...], y, preferred_element_type=F32)
        total += jnp.dot(high_ref[...], y, preferred_element_type=F32)
        for k in range(blocks):
            outs[k][:, columns] = total[k * rows : (k + 1) * rows].astype(outs[k].dtype)


def body(moe_input, route_ids, route_weights, gate_weight, up_weight, down_weight):
    rows, width = moe_input.shape
    top = route_ids.shape[1]
    devices = lax.axis_size("ep")
    experts = devices // 2
    cap = max(4, 2 * rows * top // devices)
    planes = min(4, experts)
    blocks = experts // planes
    slots = blocks * cap

    me = lax.axis_index("ep")
    my_block, my_plane = me // (2 * planes), me // 2 % planes

    def swap(array, mask):
        return lax.ppermute(array, "ep", [(i, i ^ mask) for i in range(devices)])

    tag_lanes = pl.cdiv(4 * experts, LANES) * LANES
    tagged = call(
        functools.partial(tag_kernel, experts),
        [jax.ShapeDtypeStruct((rows, width + tag_lanes), BF16)],
        moe_input, route_ids, route_weights,
    )[0]
    column = [tagged] + [swap(tagged, k * 2 * planes) for k in range(1, blocks)]
    targets = (my_block * planes + (my_plane ^ jnp.arange(planes, dtype=jnp.int32))).reshape(1, planes)
    picked = pl.pallas_call(
        functools.partial(pick_kernel, experts, cap, blocks, planes),
        out_shape=[jax.ShapeDtypeStruct((slots, width), BF16)] * planes
        + [jax.ShapeDtypeStruct((blocks * rows, planes * slots), BF16)] * 3,
        in_specs=[pl.BlockSpec(memory_space=pltpu.SMEM)] + whole_specs(blocks),
        out_specs=whole_specs(planes + 3),
        compiler_params=pltpu.CompilerParams(vmem_limit_bytes=32 << 20),
        cost_estimate=pl.CostEstimate(
            flops=2 * planes * slots * blocks * rows * width, bytes_accessed=6 * slots * planes * width, transcendentals=0
        ),
    )(targets, *column)
    outgoing, factors = picked[:planes], picked[planes:]
    mine = jnp.concatenate([outgoing[0]] + [swap(outgoing[j], 2 * j) for j in range(1, planes)], axis=0)
    others = swap(mine, 1)

    def hidden_of(inputs):
        gate_value = jnp.dot(inputs, gate_weight[0], preferred_element_type=F32)
        up_value = jnp.dot(inputs, up_weight[0], preferred_element_type=F32)
        return (jax.nn.silu(gate_value) * up_value).astype(BF16)

    hidden_mine = hidden_of(mine)
    part_others = jnp.dot(hidden_of(others), down_weight[0], preferred_element_type=F32).astype(BF16)
    from_pair = swap(part_others, 1)
    part_mine = jnp.dot(hidden_mine, down_weight[0], preferred_element_type=F32)
    result = (part_mine + from_pair.astype(F32)).astype(BF16)
    pieces = [result[j * slots : (j + 1) * slots] for j in range(planes)]
    returned = [pieces[0]] + [swap(pieces[j], 2 * j) for j in range(1, planes)]
    sums = call(
        functools.partial(combine_kernel, blocks, planes),
        [jax.ShapeDtypeStruct((rows, width), F32 if k == 0 else BF16) for k in range(blocks)],
        *returned, *factors,
        flops=6 * planes * slots * blocks * rows * width,
    )
    total = sums[0]
    for k in range(1, blocks):
        total = total + swap(sums[k], k * 2 * planes).astype(F32)
    return total.astype(BF16)


def solution(mesh):
    return jax.shard_map(
        body,
        mesh=mesh,
        in_specs=(
            P(("groups", "ep"), None),
            P(("groups", "ep"), None),
            P(("groups", "ep"), None),
            P("ep", None, None),
            P("ep", None, None),
            P("ep", None, None),
        ),
        out_specs=P(("groups", "ep"), None),
        check_vma=False,
    )
```

time: 280 us -> 123 us (0.44)
  blocking collectives: 90.1 us -> 0 us
  waiting for transfers between devices: 163 us -> 75.8 us
  starting transfers between devices: 3.76 us -> 21.1 us
  matrix products: 10.3 us -> 17.8 us
  other arithmetic: 8.23 us -> 0.79 us
    all_to_all x1 -> x0, waiting for transfers between devices: 163 us -> none  [body(): lax.all_to_all(partial_sum, 'ep', split_axis=0, concat_axis=0, tiled=True)]
    all_to_all x1 -> x0, blocking collectives: 90.1 us -> none  [body(): lax.all_to_all(doubled, 'ep', split_axis=0, concat_axis=0, tiled=True)]
    ppermute x0 -> x14, waiting for transfers between devices: none -> 75.8 us  [swap(): return lax.ppermute(array, 'ep', [(i, i ^ mask) for i in range(devices)])]
    ppermute x0 -> x14, starting transfers between devices: none -> 21.1 us  [swap(): return lax.ppermute(array, 'ep', [(i, i ^ mask) for i in range(devices)])]
    dot_general x5 -> x4, matrix products: 10.3 us -> 17.8 us  [the longest x1 7.13 us: body(): jnp.dot(hidden_of(others), down_weight[0], preferred_element_type=F32)]
    reduce_sum x2 -> x0, other arithmetic: 3.97 us -> none  [the longest x1 3.88 us: body(): moe_out = jnp.sum(weighted, axis=1).astype(jnp.bfloat16)]
    all_to_all x1 -> x0, starting transfers between devices: 3.76 us -> none  [body(): lax.all_to_all(partial_sum, 'ep', split_axis=0, concat_axis=0, tiled=True)]
    gather x1 -> x0, local copies, waits for them, and re-layouts: 2.98 us -> none  [body(): jnp.take(merged.reshape(experts * capacity, width), target, axis=0)]
  transfers between devices with their start and end apart: 1 -> 14, of which waited for: 1 -> 10; matrix products, arithmetic and copies ran while one was open for 0% -> 3% of each run, Pallas kernels for 0% -> 0%
where the time goes in v1:
time: 123 us; the launch traced here: 122 us
  waiting for transfers between devices  75.8 us (62%)
  starting transfers between devices  21.1 us (17%)
  matrix products  17.8 us (14%)
  local copies, waits for them, and re-layouts  3.98 us (3%)
  Pallas kernels  2.56 us (2%)
    ppermute x14, waiting for transfers between devices, swap(): return lax.ppermute(array, 'ep', [(i, i ^ mask) for i in range(devices)])  75.8 us
    ppermute x14, starting transfers between devices, swap(): return lax.ppermute(array, 'ep', [(i, i ^ mask) for i in range(devices)])  21.1 us
    dot_general x1, matrix products, body(): jnp.dot(hidden_of(others), down_weight[0], preferred_element_type=F32)  7.13 us
    dot_general x1, matrix products, body(): part_mine = jnp.dot(hidden_mine, down_weight[0], preferred_element_type=F32)  6.41 us
    dot_general x2, matrix products, hidden_of(): up_value = jnp.dot(inputs, up_weight[0], preferred_element_type=F32)  4.24 us
    unnamed x13, local copies, waits for them, and re-layouts  3.82 us
  transfers between devices with their start and end apart: 14, of which 10 were waited for; matrix products, arithmetic and copies ran while one was open for 3% of the time, Pallas kernels for 0%

profile of v1, /device:TPU:0, one launch (start us, length us, event | category | flops | bytes accessed | tf_op | source)
XLA Modules:
  0.0 122.1 jit_solution(16434060052596163601)
XLA Ops:
  0.0 0.8 copy.7.ids_ref
  0.8 0.8 copy.8.weights_ref
  1.5 0.0 copy-start
  1.5 0.9 copy-done
  2.5 0.2 shard_map.64.refs_0_
  2.6 3.1 %collective-permute-start = (bf16[32,3712]{1,0:T(8,128)(2,1)S(1)}, bf16[32,3712]{1,0:T(8,128)(2,1)S(1)}, u32[]{:S(2)}, u32[]{:S(2)}) collective-permute-start(bf16[32,3712]{1,0:T(8,128)(2,1)S(1)} %shard_map.64.refs_0_), channel_id=1, source_target_pairs={{0,8},{1,9},{2,10},{3,11},{4,12},{5,13},{6,14},{7,15},{8,0},{9,1},... | collective-permute-start | bytes 712712 | tf_op jit(solution)/shard_map/ppermute | solution.py:139
  5.7 2.6 %collective-permute-start.1 = (bf16[32,3712]{1,0:T(8,128)(2,1)S(1)}, bf16[32,3712]{1,0:T(8,128)(2,1)S(1)}, u32[]{:S(2)}, u32[]{:S(2)}) collective-permute-start(bf16[32,3712]{1,0:T(8,128)(2,1)S(1)} %shard_map.64.refs_0_), channel_id=1, source_target_pairs={{0,16},{1,17},{2,18},{3,19},{4,20},{5,21},{6,22},{7,23},{8,24},{9,... | collective-permute-start | bytes 712712 | tf_op jit(solution)/shard_map/ppermute | solution.py:139
  8.3 0.0 collective-permute-start.2
  8.3 7.5 %collective-permute-done.refs_1_ = bf16[32,3712]{1,0:T(8,128)(2,1)S(1)} collective-permute-done((bf16[32,3712]{1,0:T(8,128)(2,1)S(1)}, bf16[32,3712]{1,0:T(8,128)(2,1)S(1)}, u32[]{:S(2)}, u32[]{:S(2)}) %collective-permute-start) | collective-permute-done | bytes 237600 | tf_op jit(solution)/shard_map/ppermute | solution.py:139
  15.8 9.7 %collective-permute-done.1.refs_2_ = bf16[32,3712]{1,0:T(8,128)(2,1)S(1)} collective-permute-done((bf16[32,3712]{1,0:T(8,128)(2,1)S(1)}, bf16[32,3712]{1,0:T(8,128)(2,1)S(1)}, u32[]{:S(2)}, u32[]{:S(2)}) %collective-permute-start.1) | collective-permute-done | bytes 237600 | tf_op jit(solution)/shard_map/ppermute | solution.py:139
  25.5 0.0 collective-permute-done.2.refs_3_
  25.5 1.5 %shard_map.65 = (bf16[64,3584]{1,0:T(8,128)(2,1)S(1)}, bf16[64,3584]{1,0:T(8,128)(2,1)S(1)}, bf16[64,3584]{1,0:T(8,128)(2,1)S(1)}, bf16[64,3584]{1,0:T(8,128)(2,...) custom-call(s32[1,4]{1,0:T(1,128)S(1)} %xor_add_fusion.e_ref, ...), custom_call_target="tpu_custom_call" | custom-call | flops 234881024 | bytes 5505024 | tf_op jit(solution)/shard_map/pallas_call | solution.py:149
  27.0 1.6 %collective-permute-start.3 = (bf16[64,3584]{1,0:T(8,128)(2,1)S(1)}, bf16[64,3584]{1,0:T(8,128)(2,1)S(1)}, u32[]{:S(2)}, u32[]{:S(2)}) collective-permute-start(bf16[64,3584]{1,0:T(8,128)(2,1)S(1)} %get-tuple-element.17), channel_id=1, source_target_pairs={{0,2},{1,3},{2,0},{3,1},{4,6},{5,7},{6,4},{7,5},{8,10},{9,11},{10,... | collective-permute-start | bytes 1376264 | tf_op jit(solution)/shard_map/ppermute | solution.py:139
  28.6 1.5 %collective-permute-start.4 = (bf16[64,3584]{1,0:T(8,128)(2,1)S(1)}, bf16[64,3584]{1,0:T(8,128)(2,1)S(1)}, u32[]{:S(2)}, u32[]{:S(2)}) collective-permute-start(bf16[64,3584]{1,0:T(8,128)(2,1)S(1)} %get-tuple-element.18), channel_id=1, source_target_pairs={{0,4},{1,5},{2,6},{3,7},{4,0},{5,1},{6,2},{7,3},{8,12},{9,13},{10,... | collective-permute-start | bytes 1376264 | tf_op jit(solution)/shard_map/ppermute | solution.py:139
  30.1 0.5 collective-permute-start.5
  30.6 0.0 copy-start.2
  30.6 9.9 %collective-permute-done.3 = bf16[64,3584]{1,0:T(8,128)(2,1)S(1)} collective-permute-done((bf16[64,3584]{1,0:T(8,128)(2,1)S(1)}, bf16[64,3584]{1,0:T(8,128)(2,1)S(1)}, u32[]{:S(2)}, u32[]{:S(2)}) %collective-permute-start.3) | collective-permute-done | bytes 458784 | tf_op jit(solution)/shard_map/ppermute | solution.py:139
  40.6 7.3 %collective-permute-done.4 = bf16[64,3584]{1,0:T(8,128)(2,1)S(1)} collective-permute-done((bf16[64,3584]{1,0:T(8,128)(2,1)S(1)}, bf16[64,3584]{1,0:T(8,128)(2,1)S(1)}, u32[]{:S(2)}, u32[]{:S(2)}) %collective-permute-start.4) | collective-permute-done | bytes 458784 | tf_op jit(solution)/shard_map/ppermute | solution.py:139
  48.0 0.0 collective-permute-done.5
  48.0 0.0 copy-start.1
  48.0 0.1 collective-permute-start.6
  48.1 3.8 %collective-permute-done.6 = bf16[256,3584]{1,0:T(8,128)(2,1)S(1)} collective-permute-done((bf16[256,3584]{1,0:T(8,128)(2,1)S(1)}, bf16[256,3584]{1,0:T(8,128)(2,1)S(1)}, u32[]{:S(2)}, u32[]{:S(2)}) %collective-permute-start.6) | collective-permute-done | bytes 1835040 | tf_op jit(solution)/shard_map/ppermute | solution.py:139
  51.9 0.0 copy-start.3
  51.9 1.3 %copy-done.3 = bf16[256,3584]{1,0:T(8,128)(2,1)} copy-done((bf16[256,3584]{1,0:T(8,128)(2,1)}, bf16[256,3584]{1,0:T(8,128)(2,1)S(1)}, u32[]{:S(2)}) %copy-start.3) | copy-done | bytes 1835032
  53.1 0.0 copy-done.2
  53.1 1.1 fusion.3
  54.3 7.1 %convolution_convert_fusion = bf16[256,3584]{1,0:T(8,128)(2,1)} fusion(bf16[1,512,3584]{2,1,0:T(8,128)(2,1)} %param.11, f32[256,512]{1,0:T(8,128)S(1)} %fusion.3, bf16[256,3584]{1,0:T(8,128)(2,1)} %copy-done.3, bf16[1,3584,512]{2,1,0:T(8,128)(2,1)} %param.9), kind=kOutput, calls=%fused_computation | convolution fusion | flops 1880752128 | bytes 11534336 | tf_op jit(solution)/shard_map/dot_general | solution.py:170
  61.4 0.1 collective-permute-start.7
  61.5 0.0 copy-done.1
  61.5 3.1 %fusion.5 = f32[256,512]{1,0:T(8,128)S(1)} fusion(bf16[256,3584]{1,0:T(8,128)(2,1)S(1)} %constant_dynamic-update-slice_fusion, bf16[1,3584,512]{2,1,0:T(8,128)(2,1)} %param.10), kind=kOutput, calls=%fused_computation.6 | convolution fusion | flops 939524096 | bytes 6029312 | tf_op jit(solution)/shard_map/dot_general | solution.py:166
  64.7 0.8 collective-permute-done.7
  65.5 6.4 %add_convert_fusion = bf16[256,3584]{1,0:T(8,128)(2,1)S(1)} fusion(bf16[256,3584]{1,0:T(8,128)(2,1)} %collective-permute-done.7, bf16[1,512,3584]{2,1,0:T(8,128)(2,1)} %param.11, f32[256,512]{1,0:T(8,128)S(1)} %fusion.5, bf16[256,3584]{1,0:T(8,128)(2,1)} %copy-done.1, bf16[1,3584,512]{2,1,0:T(8,128)(2,1)} %param.9), kind=kOutput, calls=%fused_computation.12 | convolution fusion | flops 1882587136 | bytes 13369344 | tf_op jit(solution)/shard_map/dot_general | solution.py:172
  71.9 0.1 fusion.25
  72.1 1.6 %collective-permute-start.10 = (bf16[64,3584]{1,0:T(8,128)(2,1)S(1)}, bf16[64,3584]{1,0:T(8,128)(2,1)S(1)}, u32[]{:S(2)}, u32[]{:S(2)}) collective-permute-start(bf16[64,3584]{1,0:T(8,128)(2,1)S(1)} %get-tuple-element.27), channel_id=1, source_target_pairs={{0,6},{1,7},{2,4},{3,5},{4,2},{5,3},{6,0},{7,1},{8,14},{9,15},{10,... | collective-permute-start | bytes 1376264 | tf_op jit(solution)/shard_map/ppermute | solution.py:139
  73.6 1.5 %collective-permute-start.8 = (bf16[64,3584]{1,0:T(8,128)(2,1)S(1)}, bf16[64,3584]{1,0:T(8,128)(2,1)S(1)}, u32[]{:S(2)}, u32[]{:S(2)}) collective-permute-start(bf16[64,3584]{1,0:T(8,128)(2,1)S(1)} %get-tuple-element.29), channel_id=1, source_target_pairs={{0,2},{1,3},{2,0},{3,1},{4,6},{5,7},{6,4},{7,5},{8,10},{9,11},{10,... | collective-permute-start | bytes 1376264 | tf_op jit(solution)/shard_map/ppermute | solution.py:139
  75.1 0.5 collective-permute-start.9
  75.6 10.8 %collective-permute-done.10.refs_3_ = bf16[64,3584]{1,0:T(8,128)(2,1)S(1)} collective-permute-done((bf16[64,3584]{1,0:T(8,128)(2,1)S(1)}, bf16[64,3584]{1,0:T(8,128)(2,1)S(1)}, u32[]{:S(2)}, u32[]{:S(2)}) %collective-permute-start.10) | collective-permute-done | bytes 458784 | tf_op jit(solution)/shard_map/ppermute | solution.py:139
  86.4 9.1 %collective-permute-done.8.refs_1_ = bf16[64,3584]{1,0:T(8,128)(2,1)S(1)} collective-permute-done((bf16[64,3584]{1,0:T(8,128)(2,1)S(1)}, bf16[64,3584]{1,0:T(8,128)(2,1)S(1)}, u32[]{:S(2)}, u32[]{:S(2)}) %collective-permute-start.8) | collective-permute-done | bytes 458784 | tf_op jit(solution)/shard_map/ppermute | solution.py:139
  95.5 0.0 collective-permute-done.9.refs_2_
  95.5 0.9 shard_map.66
  96.4 5.6 %collective-permute-start.11 = (bf16[32,3584]{1,0:T(8,128)(2,1)S(1)}, bf16[32,3584]{1,0:T(8,128)(2,1)S(1)}, u32[]{:S(2)}, u32[]{:S(2)}) collective-permute-start(bf16[32,3584]{1,0:T(8,128)(2,1)S(1)} %get-tuple-element.24), channel_id=1, source_target_pairs={{0,8},{1,9},{2,10},{3,11},{4,12},{5,13},{6,14},{7,15},{8,0},{9,1},... | collective-permute-start | bytes 688136 | tf_op jit(solution)/shard_map/ppermute | solution.py:139
  102.0 1.1 collective-permute-start.12
  103.1 1.4 %collective-permute-start.13 = (bf16[32,3584]{1,0:T(8,128)(2,1)S(1)}, bf16[32,3584]{1,0:T(8,128)(2,1)S(1)}, u32[]{:S(2)}, u32[]{:S(2)}) collective-permute-start(bf16[32,3584]{1,0:T(8,128)(2,1)S(1)} %get-tuple-element.26), channel_id=1, source_target_pairs={{0,24},{1,25},{2,26},{3,27},{4,28},{5,29},{6,30},{7,31},{8,16},{9,... | collective-permute-start | bytes 688136 | tf_op jit(solution)/shard_map/ppermute | solution.py:139
  104.5 7.4 %collective-permute-done.11 = bf16[32,3584]{1,0:T(8,128)(2,1)S(1)} collective-permute-done((bf16[32,3584]{1,0:T(8,128)(2,1)S(1)}, bf16[32,3584]{1,0:T(8,128)(2,1)S(1)}, u32[]{:S(2)}, u32[]{:S(2)}) %collective-permute-start.11) | collective-permute-done | bytes 229408 | tf_op jit(solution)/shard_map/ppermute | solution.py:139
  111.9 9.4 %collective-permute-done.12 = bf16[32,3584]{1,0:T(8,128)(2,1)S(1)} collective-permute-done((bf16[32,3584]{1,0:T(8,128)(2,1)S(1)}, bf16[32,3584]{1,0:T(8,128)(2,1)S(1)}, u32[]{:S(2)}, u32[]{:S(2)}) %collective-permute-start.12) | collective-permute-done | bytes 229408 | tf_op jit(solution)/shard_map/ppermute | solution.py:139
  121.3 0.0 collective-permute-done.13
  121.3 0.8 add_convert_fusion.1
  (5 shorter events, 0.1 us)
Async XLA Ops:
  1.5 0.9 copy-start
  2.6 13.2 %collective-permute-start = (bf16[32,3712]{1,0:T(8,128)(2,1)S(1)}, bf16[32,3712]{1,0:T(8,128)(2,1)S(1)}, u32[]{:S(2)}, u32[]{:S(2)}) collective-permute-start(bf16[32,3712]{1,0:T(8,128)(2,1)S(1)} %shard_map.64.refs_0_), channel_id=1, source_target_pairs={{0,8},{1,9},{2,10},{3,11},{4,12},{5,13},{6,14},{7,15},{8,0},{9,1},... | collective-permute-start | bytes 712712 | tf_op jit(solution)/shard_map/ppermute | solution.py:139
  5.7 19.8 %collective-permute-start.1 = (bf16[32,3712]{1,0:T(8,128)(2,1)S(1)}, bf16[32,3712]{1,0:T(8,128)(2,1)S(1)}, u32[]{:S(2)}, u32[]{:S(2)}) collective-permute-start(bf16[32,3712]{1,0:T(8,128)(2,1)S(1)} %shard_map.64.refs_0_), channel_id=1, source_target_pairs={{0,16},{1,17},{2,18},{3,19},{4,20},{5,21},{6,22},{7,23},{8,24},{9,... | collective-permute-start | bytes 712712 | tf_op jit(solution)/shard_map/ppermute | solution.py:139
  8.3 17.2 %collective-permute-start.2 = (bf16[32,3712]{1,0:T(8,128)(2,1)S(1)}, bf16[32,3712]{1,0:T(8,128)(2,1)S(1)}, u32[]{:S(2)}, u32[]{:S(2)}) collective-permute-start(bf16[32,3712]{1,0:T(8,128)(2,1)S(1)} %shard_map.64.refs_0_), channel_id=1, source_target_pairs={{0,24},{1,25},{2,26},{3,27},{4,28},{5,29},{6,30},{7,31},{8,16},{9,... | collective-permute-start | bytes 712712 | tf_op jit(solution)/shard_map/ppermute | solution.py:139
  27.0 13.5 %collective-permute-start.3 = (bf16[64,3584]{1,0:T(8,128)(2,1)S(1)}, bf16[64,3584]{1,0:T(8,128)(2,1)S(1)}, u32[]{:S(2)}, u32[]{:S(2)}) collective-permute-start(bf16[64,3584]{1,0:T(8,128)(2,1)S(1)} %get-tuple-element.17), channel_id=1, source_target_pairs={{0,2},{1,3},{2,0},{3,1},{4,6},{5,7},{6,4},{7,5},{8,10},{9,11},{10,... | collective-permute-start | bytes 1376264 | tf_op jit(solution)/shard_map/ppermute | solution.py:139
  28.6 19.3 %collective-permute-start.4 = (bf16[64,3584]{1,0:T(8,128)(2,1)S(1)}, bf16[64,3584]{1,0:T(8,128)(2,1)S(1)}, u32[]{:S(2)}, u32[]{:S(2)}) collective-permute-start(bf16[64,3584]{1,0:T(8,128)(2,1)S(1)} %get-tuple-element.18), channel_id=1, source_target_pairs={{0,4},{1,5},{2,6},{3,7},{4,0},{5,1},{6,2},{7,3},{8,12},{9,13},{10,... | collective-permute-start | bytes 1376264 | tf_op jit(solution)/shard_map/ppermute | solution.py:139
  30.1 17.9 %collective-permute-start.5 = (bf16[64,3584]{1,0:T(8,128)(2,1)S(1)}, bf16[64,3584]{1,0:T(8,128)(2,1)S(1)}, u32[]{:S(2)}, u32[]{:S(2)}) collective-permute-start(bf16[64,3584]{1,0:T(8,128)(2,1)S(1)} %get-tuple-element.19), channel_id=1, source_target_pairs={{0,6},{1,7},{2,4},{3,5},{4,2},{5,3},{6,0},{7,1},{8,14},{9,15},{10,... | collective-permute-start | bytes 1376264 | tf_op jit(solution)/shard_map/ppermute | solution.py:139
  30.6 22.6 %copy-start.2 = (bf16[1,3584,512]{2,1,0:T(8,128)(2,1)S(1)}, bf16[1,3584,512]{2,1,0:T(8,128)(2,1)}, u32[]{:S(2)}) copy-start(bf16[1,3584,512]{2,1,0:T(8,128)(2,1)} %param.10) | copy-start | bytes 11010052
  48.0 13.5 %copy-start.1 = (bf16[256,3584]{1,0:T(8,128)(2,1)}, bf16[256,3584]{1,0:T(8,128)(2,1)S(1)}, u32[]{:S(2)}) copy-start(bf16[256,3584]{1,0:T(8,128)(2,1)S(1)} %constant_dynamic-update-slice_fusion) | copy-start | bytes 5505028
  48.0 3.9 %collective-permute-start.6 = (bf16[256,3584]{1,0:T(8,128)(2,1)S(1)}, bf16[256,3584]{1,0:T(8,128)(2,1)S(1)}, u32[]{:S(2)}, u32[]{:S(2)}) collective-permute-start(bf16[256,3584]{1,0:T(8,128)(2,1)S(1)} %constant_dynamic-update-slice_fusion), channel_id=1, source_target_pairs={{0,1},{1,0},{2,3},{3,2},{4,5},{5,4},{6,7},{7,6},{8,9},{9,8},{10,11... | collective-permute-start | bytes 5505032 | tf_op jit(solution)/shard_map/ppermute | solution.py:139
  51.9 1.3 %copy-start.3 = (bf16[256,3584]{1,0:T(8,128)(2,1)}, bf16[256,3584]{1,0:T(8,128)(2,1)S(1)}, u32[]{:S(2)}) copy-start(bf16[256,3584]{1,0:T(8,128)(2,1)S(1)} %collective-permute-done.6) | copy-start | bytes 5505028
  61.4 4.1 %collective-permute-start.7 = (bf16[256,3584]{1,0:T(8,128)(2,1)}, bf16[256,3584]{1,0:T(8,128)(2,1)}, u32[]{:S(2)}, u32[]{:S(2)}) collective-permute-start(bf16[256,3584]{1,0:T(8,128)(2,1)} %convolution_convert_fusion), channel_id=1, source_target_pairs={{0,1},{1,0},{2,3},{3,2},{4,5},{5,4},{6,7},{7,6},{8,9},{9,8},{10,11... | collective-permute-start | bytes 5505032 | tf_op jit(solution)/shard_map/ppermute | solution.py:139
  72.1 14.4 %collective-permute-start.10 = (bf16[64,3584]{1,0:T(8,128)(2,1)S(1)}, bf16[64,3584]{1,0:T(8,128)(2,1)S(1)}, u32[]{:S(2)}, u32[]{:S(2)}) collective-permute-start(bf16[64,3584]{1,0:T(8,128)(2,1)S(1)} %get-tuple-element.27), channel_id=1, source_target_pairs={{0,6},{1,7},{2,4},{3,5},{4,2},{5,3},{6,0},{7,1},{8,14},{9,15},{10,... | collective-permute-start | bytes 1376264 | tf_op jit(solution)/shard_map/ppermute | solution.py:139
  73.6 21.9 %collective-permute-start.8 = (bf16[64,3584]{1,0:T(8,128)(2,1)S(1)}, bf16[64,3584]{1,0:T(8,128)(2,1)S(1)}, u32[]{:S(2)}, u32[]{:S(2)}) collective-permute-start(bf16[64,3584]{1,0:T(8,128)(2,1)S(1)} %get-tuple-element.29), channel_id=1, source_target_pairs={{0,2},{1,3},{2,0},{3,1},{4,6},{5,7},{6,4},{7,5},{8,10},{9,11},{10,... | collective-permute-start | bytes 1376264 | tf_op jit(solution)/shard_map/ppermute | solution.py:139
  75.1 20.4 %collective-permute-start.9 = (bf16[64,3584]{1,0:T(8,128)(2,1)S(1)}, bf16[64,3584]{1,0:T(8,128)(2,1)S(1)}, u32[]{:S(2)}, u32[]{:S(2)}) collective-permute-start(bf16[64,3584]{1,0:T(8,128)(2,1)S(1)} %get-tuple-element.28), channel_id=1, source_target_pairs={{0,4},{1,5},{2,6},{3,7},{4,0},{5,1},{6,2},{7,3},{8,12},{9,13},{10,... | collective-permute-start | bytes 1376264 | tf_op jit(solution)/shard_map/ppermute | solution.py:139
  96.4 15.4 %collective-permute-start.11 = (bf16[32,3584]{1,0:T(8,128)(2,1)S(1)}, bf16[32,3584]{1,0:T(8,128)(2,1)S(1)}, u32[]{:S(2)}, u32[]{:S(2)}) collective-permute-start(bf16[32,3584]{1,0:T(8,128)(2,1)S(1)} %get-tuple-element.24), channel_id=1, source_target_pairs={{0,8},{1,9},{2,10},{3,11},{4,12},{5,13},{6,14},{7,15},{8,0},{9,1},... | collective-permute-start | bytes 688136 | tf_op jit(solution)/shard_map/ppermute | solution.py:139
  102.0 19.3 %collective-permute-start.12 = (bf16[32,3584]{1,0:T(8,128)(2,1)S(1)}, bf16[32,3584]{1,0:T(8,128)(2,1)S(1)}, u32[]{:S(2)}, u32[]{:S(2)}) collective-permute-start(bf16[32,3584]{1,0:T(8,128)(2,1)S(1)} %get-tuple-element.25), channel_id=1, source_target_pairs={{0,16},{1,17},{2,18},{3,19},{4,20},{5,21},{6,22},{7,23},{8,24},{9,... | collective-permute-start | bytes 688136 | tf_op jit(solution)/shard_map/ppermute | solution.py:139
  103.1 18.2 %collective-permute-start.13 = (bf16[32,3584]{1,0:T(8,128)(2,1)S(1)}, bf16[32,3584]{1,0:T(8,128)(2,1)S(1)}, u32[]{:S(2)}, u32[]{:S(2)}) collective-permute-start(bf16[32,3584]{1,0:T(8,128)(2,1)S(1)} %get-tuple-element.26), channel_id=1, source_target_pairs={{0,24},{1,25},{2,26},{3,27},{4,28},{5,29},{6,30},{7,31},{8,16},{9,... | collective-permute-start | bytes 688136 | tf_op jit(solution)/shard_map/ppermute | solution.py:139

commit v2 on v1

v2 whole, which is shorter than its diff:
```python
import functools

import jax
import jax.numpy as jnp
from jax import lax
from jax.experimental import pallas as pl
from jax.experimental.pallas import tpu as pltpu
from jax.sharding import PartitionSpec as P

F32, BF16 = jnp.float32, jnp.bfloat16
LANES = 128
SHARE = (2, 3)
TILE = 512
VMEM_LIMIT = 24 << 20


def call(kernel, out_shapes, *operands, flops=0, scalars=0):
    moved = sum(o.size * o.dtype.itemsize for o in operands)
    moved += sum(o.size * o.dtype.itemsize for o in out_shapes)
    vmem = pl.BlockSpec(memory_space=pltpu.VMEM)
    smem = pl.BlockSpec(memory_space=pltpu.SMEM)
    return pl.pallas_call(
        kernel,
        out_shape=out_shapes,
        in_specs=[smem] * scalars + [vmem] * (len(operands) - scalars),
        out_specs=[vmem] * len(out_shapes),
        compiler_params=pltpu.CompilerParams(vmem_limit_bytes=VMEM_LIMIT),
        cost_estimate=pl.CostEstimate(flops=flops, bytes_accessed=moved, transcendentals=0),
    )(*operands)


def shaped(count, shape, dtype=BF16):
    return [jax.ShapeDtypeStruct(shape, dtype) for _ in range(count)]


def tiles(width):
    return [(start, min(TILE, width - start)) for start in range(0, width, TILE)]


def split3(value):
    high = value.astype(BF16)
    rest = value - high.astype(F32)
    middle = rest.astype(BF16)
    low = (rest - middle.astype(F32)).astype(BF16)
    return high, middle, low


def tag_kernel(experts, x_ref, ids_ref, weights_ref, first_ref, second_ref):
    rows, width = x_ref.shape
    split = first_ref.shape[1] - (first_ref.shape[1] + second_ref.shape[1] - width) // 2
    tag_lanes = first_ref.shape[1] - split
    lane = lax.broadcasted_iota(jnp.int32, (rows, tag_lanes), 1)
    expert = lane % experts
    group = lane // experts
    flags = jnp.zeros((rows, tag_lanes), F32)
    weights = jnp.zeros((rows, tag_lanes), F32)
    for k in range(ids_ref.shape[1]):
        match = ids_ref[:, k : k + 1] == expert
        flags = jnp.where(match, 1.0, flags)
        weights = jnp.where(match, weights_ref[:, k : k + 1], weights)
    parts = [flags] + [part.astype(F32) for part in split3(weights)]
    tag = jnp.zeros((rows, tag_lanes), F32)
    for number, part in enumerate(parts):
        tag = jnp.where(group == number, part, tag)
    first_ref[:, :split] = x_ref[:, :split]
    first_ref[:, split:] = tag.astype(BF16)
    second_ref[:, : width - split] = x_ref[:, split:]
    second_ref[:, width - split :] = tag.astype(BF16)


def pick_kernel(experts, cap, sources, targets, e_ref, *refs):
    x_refs, outs = refs[:sources], refs[sources : sources + targets]
    high_ref, middle_ref, low_ref = refs[sources + targets :]
    rows = x_refs[0].shape[0]
    width = outs[0].shape[1]
    total = sources * rows
    slots = sources * cap
    tag = jnp.concatenate([x[:, width:] for x in x_refs], axis=0)
    tag_lanes = tag.shape[1]
    row = lax.broadcasted_iota(jnp.int32, (total, total), 0)
    col = lax.broadcasted_iota(jnp.int32, (total, total), 1)
    before = ((row // rows == col // rows) & (col < row)).astype(F32).astype(BF16)
    rank = jnp.dot(before, tag, preferred_element_type=F32)
    tag = tag.astype(F32)
    lane = lax.broadcasted_iota(jnp.int32, (total, tag_lanes), 1)
    source = lax.broadcasted_iota(jnp.int32, (total, 1), 0) // rows
    slot = lax.broadcasted_iota(jnp.int32, (total, targets * slots), 1)
    picked = jnp.zeros((total, targets * slots), F32)
    weight = jnp.zeros((total, targets * slots), F32)
    for t in range(targets):
        e = e_ref[0, t]
        here = lane == e
        flag = jnp.sum(jnp.where(here, tag, 0.0), axis=1, keepdims=True)
        place = jnp.sum(jnp.where(here, rank, 0.0), axis=1, keepdims=True).astype(jnp.int32)
        parts = (lane % experts == e) & (lane // experts >= 1) & (lane // experts <= 3)
        factor = jnp.sum(jnp.where(parts, tag, 0.0), axis=1, keepdims=True)
        hit = slot == jnp.where(flag > 0.0, t * slots + source * cap + place, -1)
        picked = jnp.where(hit, 1.0, picked)
        weight = jnp.where(hit, factor, weight)
    high_ref[...], middle_ref[...], low_ref[...] = split3(weight)
    picker = picked.T.astype(BF16)
    for start, size in tiles(width):
        columns = pl.ds(start, size)
        x = jnp.concatenate([x[:, columns] for x in x_refs], axis=0)
        out = jnp.dot(picker, x, preferred_element_type=F32).astype(BF16)
        for t in range(targets):
            outs[t][:, columns] = out[t * slots : (t + 1) * slots]


def combine_kernel(sources, targets, *refs):
    returned = refs[:targets]
    high_ref, middle_ref, low_ref = refs[targets : targets + 3]
    outs = refs[targets + 3 :]
    rows, width = outs[0].shape
    for start, size in tiles(width):
        columns = pl.ds(start, size)
        y = jnp.concatenate([r[:, columns] for r in returned], axis=0)
        total = jnp.dot(low_ref[...], y, preferred_element_type=F32)
        total += jnp.dot(middle_ref[...], y, preferred_element_type=F32)
        total += jnp.dot(high_ref[...], y, preferred_element_type=F32)
        for s in range(sources):
            outs[s][:, columns] = total[s * rows : (s + 1) * rows].astype(outs[s].dtype)


def reorder(blocks, planes, cap, inverse=False):
    count = blocks * planes * cap
    row = lax.broadcasted_iota(jnp.int32, (count, count), 1 if inverse else 0)
    col = lax.broadcasted_iota(jnp.int32, (count, count), 0 if inverse else 1)
    plane, block, place = row // (blocks * cap), row // cap % blocks, row % cap
    return (col == (block * planes + plane) * cap + place).astype(F32).astype(BF16)


def hidden_kernel(blocks, planes, cap, *refs):
    firsts, seconds = refs[:planes], refs[planes : planes + blocks]
    gate_ref, up_ref, hidden_ref = refs[planes + blocks :]
    split = firsts[0].shape[1]
    first = jnp.concatenate([r[...] for r in firsts], axis=0)
    second = jnp.concatenate([r[...] for r in seconds], axis=0)
    second = jnp.dot(reorder(blocks, planes, cap), second, preferred_element_type=F32).astype(BF16)

    def product(ref, columns):
        value = jnp.dot(first, ref[0, :split, columns], preferred_element_type=F32)
        return value + jnp.dot(second, ref[0, split:, columns], preferred_element_type=F32)

    for start in range(0, hidden_ref.shape[1], 256):
        columns = pl.ds(start, 256)
        gate_value = product(gate_ref, columns)
        up_value = product(up_ref, columns)
        hidden_ref[:, columns] = (gate_value * jax.nn.sigmoid(gate_value) * up_value).astype(BF16)


def down_kernel(blocks, planes, cap, hidden_ref, down_ref, first_ref, second_ref):
    split = first_ref.shape[1]
    hidden = hidden_ref[...]
    for start, size in tiles(split):
        part = jnp.dot(hidden, down_ref[0, :, pl.ds(start, size)], preferred_element_type=F32)
        first_ref[:, pl.ds(start, size)] = part.astype(BF16)
    hidden = jnp.dot(reorder(blocks, planes, cap, True), hidden, preferred_element_type=F32).astype(BF16)
    for start, size in tiles(second_ref.shape[1]):
        part = jnp.dot(hidden, down_ref[0, :, pl.ds(split + start, size)], preferred_element_type=F32)
        second_ref[:, pl.ds(start, size)] = part.astype(BF16)


def add_down_kernel(blocks, planes, cap, hidden_ref, down_ref, first_ref, second_ref, *outs):
    split = first_ref.shape[1]
    hidden = hidden_ref[...]

    def halves(hidden, base, other_ref, outs):
        rows = outs[0].shape[0]
        for start, size in tiles(other_ref.shape[1]):
            columns = pl.ds(start, size)
            part = jnp.dot(hidden, down_ref[0, :, pl.ds(base + start, size)], preferred_element_type=F32)
            both = (part + other_ref[:, columns].astype(F32)).astype(BF16)
            for number, out in enumerate(outs):
                out[:, columns] = both[number * rows : (number + 1) * rows]

    halves(hidden, 0, first_ref, outs[:planes])
    hidden = jnp.dot(reorder(blocks, planes, cap, True), hidden, preferred_element_type=F32).astype(BF16)
    halves(hidden, split, second_ref, outs[planes:])


def body(moe_input, route_ids, route_weights, gate_weight, up_weight, down_weight):
    rows, width = moe_input.shape
    top = route_ids.shape[1]
    devices = lax.axis_size("ep")
    experts = devices // 2
    cap = max(4, 2 * rows * top // devices)
    planes = min(4, experts)
    blocks = experts // planes
    slots = blocks * planes * cap
    split = width * SHARE[0] // (SHARE[1] * LANES) * LANES
    rest = width - split

    me = lax.axis_index("ep")
    my_block, my_plane = me // (2 * planes), me // 2 % planes

    def swap(array, mask):
        return lax.ppermute(array, "ep", [(i, i ^ mask) for i in range(devices)])

    def over_blocks(arrays):
        return [arrays[0]] + [swap(arrays[k], 2 * planes * k) for k in range(1, blocks)]

    def over_planes(arrays):
        return [arrays[0]] + [swap(arrays[j], 2 * j) for j in range(1, planes)]

    tag_lanes = pl.cdiv(4 * experts, LANES) * LANES
    tagged_first, tagged_second = call(
        functools.partial(tag_kernel, experts),
        shaped(1, (rows, split + tag_lanes)) + shaped(1, (rows, rest + tag_lanes)),
        moe_input, route_ids, route_weights,
    )
    plane_ids = my_block * planes + (my_plane ^ jnp.arange(planes, dtype=jnp.int32))
    block_ids = (my_block ^ jnp.arange(blocks, dtype=jnp.int32)) * planes + my_plane
    column = over_blocks([tagged_first] * blocks)
    plane = over_planes([tagged_second] * planes)

    def pick(arrays, targets, ids, columns):
        sources = len(arrays)
        out = call(
            functools.partial(pick_kernel, experts, cap, sources, targets),
            shaped(targets, (sources * cap, columns)) + shaped(3, (sources * rows, slots)),
            ids.reshape(1, targets), *arrays,
            flops=2 * slots * sources * rows * columns, scalars=1,
        )
        return out[:targets], out[targets:]

    first, first_factors = pick(column, planes, plane_ids, split)
    second, second_factors = pick(plane, blocks, block_ids, rest)
    first = over_planes(first)
    second = over_blocks(second)
    first_other = [swap(piece, 1) for piece in first]
    second_other = [swap(piece, 1) for piece in second]

    sizes = (blocks, planes, cap)
    hidden_width = gate_weight.shape[2]

    def hidden_of(first, second):
        return call(
            functools.partial(hidden_kernel, *sizes),
            shaped(1, (slots, hidden_width)),
            *first, *second, gate_weight, up_weight,
            flops=4 * slots * width * hidden_width,
        )[0]

    hidden_mine = hidden_of(first, second)
    hidden_other = hidden_of(first_other, second_other)
    parts = call(
        functools.partial(down_kernel, *sizes),
        shaped(1, (slots, split)) + shaped(1, (slots, rest)),
        hidden_other, down_weight,
        flops=2 * slots * width * hidden_width,
    )
    results = call(
        functools.partial(add_down_kernel, *sizes),
        shaped(planes, (blocks * cap, split)) + shaped(blocks, (planes * cap, rest)),
        hidden_mine, down_weight, swap(parts[0], 1), swap(parts[1], 1),
        flops=2 * slots * width * hidden_width,
    )
    first = over_planes(results[:planes])
    second = over_blocks(results[planes:])

    def combine(arrays, factors, sources, columns):
        return call(
            functools.partial(combine_kernel, sources, len(arrays)),
            shaped(1, (rows, columns), F32) + shaped(sources - 1, (rows, columns)),
            *arrays, *factors,
            flops=6 * slots * sources * rows * columns,
        )

    first = over_blocks(combine(first, first_factors, blocks, split))
    second = over_planes(combine(second, second_factors, planes, rest))

    def total(arrays):
        result = arrays[0]
        for array in arrays[1:]:
            result = result + array.astype(F32)
        return result.astype(BF16)

    return jnp.concatenate([total(first), total(second)], axis=1)


def solution(mesh):
    return jax.shard_map(
        body,
        mesh=mesh,
        in_specs=(
            P(("groups", "ep"), None),
            P(("groups", "ep"), None),
            P(("groups", "ep"), None),
            P("ep", None, None),
            P("ep", None, None),
            P("ep", None, None),
        ),
        out_specs=P(("groups", "ep"), None),
        check_vma=False,
    )
```

time: 123 us -> 94.8 us (0.77)
  waiting for transfers between devices: 75.8 us -> 36.5 us
  starting transfers between devices: 21.1 us -> 39.3 us
  matrix products: 17.8 us -> 0 us
  Pallas kernels: 2.56 us -> 10.9 us
  local copies, waits for them, and re-layouts: 3.98 us -> 6.9 us
    ppermute x14 -> x34, waiting for transfers between devices: 75.8 us -> 36.5 us  [swap(): return lax.ppermute(array, 'ep', [(i, i ^ mask) for i in range(devices)])]
    ppermute x14 -> x34, starting transfers between devices: 21.1 us -> 39.3 us  [swap(): return lax.ppermute(array, 'ep', [(i, i ^ mask) for i in range(devices)])]
    dot_general x4 -> x0, matrix products: 17.8 us -> none  [the longest x1 7.13 us: body(): jnp.dot(hidden_of(others), down_weight[0], preferred_element_type=F32)]
    pallas_call x3 -> x9, Pallas kernels: 2.56 us -> 10.9 us  [call(): pl.pallas_call(kernel, out_shape=out_shapes, in_specs=[smem] * scalars +...]
    unnamed x13 -> x14, local copies, waits for them, and re-layouts: 3.82 us -> 6.9 us
  transfers between devices with their start and end apart: 14 -> 34, of which waited for: 10 -> 10; matrix products, arithmetic and copies ran while one was open for 3% -> 0% of each run, Pallas kernels for 0% -> 6%
where the time goes in v2:
time: 94.8 us; the launch traced here: 94.5 us
  starting transfers between devices  39.3 us (41%)
  waiting for transfers between devices  36.5 us (39%)
  Pallas kernels  10.9 us (11%)
  local copies, waits for them, and re-layouts  6.9 us (7%)
    ppermute x34, starting transfers between devices, swap(): return lax.ppermute(array, 'ep', [(i, i ^ mask) for i in range(devices)])  39.3 us
    ppermute x34, waiting for transfers between devices, swap(): return lax.ppermute(array, 'ep', [(i, i ^ mask) for i in range(devices)])  36.5 us
    pallas_call x9, Pallas kernels, call(): pl.pallas_call(kernel, out_shape=out_shapes, in_specs=[smem] * scalars +...  10.9 us
    unnamed x14, local copies, waits for them, and re-layouts  6.9 us
  transfers between devices with their start and end apart: 34, of which 10 were waited for; matrix products, arithmetic and copies ran while one was open for 0% of the time, Pallas kernels for 6%

profile of v2, /device:TPU:0, one launch (start us, length us, event | category | flops | bytes accessed | tf_op | source)
XLA Modules:
  0.0 94.5 jit_solution(2427675042171030671)
XLA Ops:
  0.0 0.8 copy.7.ids_ref
  0.8 0.8 copy.8.weights_ref
  1.5 0.9 copy-done.5
  2.6 4.0 %collective-permute-start.8 = (bf16[32,1408]{1,0:T(8,128)(2,1)S(1)}, bf16[32,1408]{1,0:T(8,128)(2,1)S(1)}, u32[]{:S(2)}, u32[]{:S(2)}) collective-permute-start(bf16[32,1408]{1,0:T(8,128)(2,1)S(1)} %get-tuple-element.44.refs_0_), channel_id=1, source_target_pairs={{0,6},{1,7},{2,4},{3,5},{4,2},{5,3},{6,0},{7,1},{8,14},{9,15},{10,... | collective-permute-start | bytes 270344 | tf_op jit(solution)/shard_map/ppermute | solution.py:198
  6.6 0.5 collective-permute-start.7
  7.2 4.0 %collective-permute-start.2 = (bf16[32,2432]{1,0:T(8,128)(2,1)S(1)}, bf16[32,2432]{1,0:T(8,128)(2,1)S(1)}, u32[]{:S(2)}, u32[]{:S(2)}) collective-permute-start(bf16[32,2432]{1,0:T(8,128)(2,1)S(1)} %get-tuple-element.39.refs_0_), channel_id=1, source_target_pairs={{0,24},{1,25},{2,26},{3,27},{4,28},{5,29},{6,30},{7,31},{8,16},{9,... | collective-permute-start | bytes 466952 | tf_op jit(solution)/shard_map/ppermute | solution.py:198
  11.2 0.6 collective-permute-start
  11.9 1.2 %shard_map.66 = (bf16[64,1280]{1,0:T(8,128)(2,1)S(1)}, bf16[64,1280]{1,0:T(8,128)(2,1)S(1)}, bf16[64,1280]{1,0:T(8,128)(2,1)S(1)}, bf16[64,1280]{1,0:T(8,128)(2,...) custom-call(s32[1,4]{1,0:T(1,128)S(1)} %multiply_add_fusion.e_ref, ...), custom_call_target="tpu_custom_call" | custom-call | flops 83886080 | bytes 1212432 | tf_op jit(solution)/shard_map/pallas_call | solution.py:22
  13.1 1.5 %collective-permute-start.9 = (bf16[64,1280]{1,0:T(8,128)(2,1)S(1)}, bf16[64,1280]{1,0:T(8,128)(2,1)S(1)}, u32[]{:S(2)}, u32[]{:S(2)}) collective-permute-start(bf16[64,1280]{1,0:T(8,128)(2,1)S(1)} %get-tuple-element.46), channel_id=1, source_target_pairs={{0,8},{1,9},{2,10},{3,11},{4,12},{5,13},{6,14},{7,15},{8,0},{9,1},... | collective-permute-start | bytes 491528 | tf_op jit(solution)/shard_map/ppermute | solution.py:198
  14.6 2.9 %collective-permute-start.10 = (bf16[64,1280]{1,0:T(8,128)(2,1)S(1)}, bf16[64,1280]{1,0:T(8,128)(2,1)S(1)}, u32[]{:S(2)}, u32[]{:S(2)}) collective-permute-start(bf16[64,1280]{1,0:T(8,128)(2,1)S(1)} %get-tuple-element.47), channel_id=1, source_target_pairs={{0,16},{1,17},{2,18},{3,19},{4,20},{5,21},{6,22},{7,23},{8,24},{9,... | collective-permute-start | bytes 491528 | tf_op jit(solution)/shard_map/ppermute | solution.py:198
  17.6 2.4 %collective-permute-start.11 = (bf16[64,1280]{1,0:T(8,128)(2,1)S(1)}, bf16[64,1280]{1,0:T(8,128)(2,1)S(1)}, u32[]{:S(2)}, u32[]{:S(2)}) collective-permute-start(bf16[64,1280]{1,0:T(8,128)(2,1)S(1)} %get-tuple-element.48), channel_id=1, source_target_pairs={{0,24},{1,25},{2,26},{3,27},{4,28},{5,29},{6,30},{7,31},{8,16},{9,... | collective-permute-start | bytes 491528 | tf_op jit(solution)/shard_map/ppermute | solution.py:198
  20.0 6.3 %collective-permute-done.1.refs_2_ = bf16[32,2432]{1,0:T(8,128)(2,1)S(1)} collective-permute-done((bf16[32,2432]{1,0:T(8,128)(2,1)S(1)}, bf16[32,2432]{1,0:T(8,128)(2,1)S(1)}, u32[]{:S(2)}, u32[]{:S(2)}) %collective-permute-start.1) | collective-permute-done | bytes 155680 | tf_op jit(solution)/shard_map/ppermute | solution.py:198
  26.3 1.4 %shard_map.65 = (bf16[64,2304]{1,0:T(8,128)(2,1)S(1)}, bf16[64,2304]{1,0:T(8,128)(2,1)S(1)}, bf16[64,2304]{1,0:T(8,128)(2,1)S(1)}, bf16[64,2304]{1,0:T(8,128)(2,...) custom-call(s32[1,4]{1,0:T(1,128)S(1)} %xor_add_fusion.e_ref, ...), custom_call_target="tpu_custom_call" | custom-call | flops 150994944 | bytes 1998864 | tf_op jit(solution)/shard_map/pallas_call | solution.py:22
  27.7 1.8 %collective-permute-start.3 = (bf16[64,2304]{1,0:T(8,128)(2,1)S(1)}, bf16[64,2304]{1,0:T(8,128)(2,1)S(1)}, u32[]{:S(2)}, u32[]{:S(2)}) collective-permute-start(bf16[64,2304]{1,0:T(8,128)(2,1)S(1)} %get-tuple-element.41), channel_id=1, source_target_pairs={{0,2},{1,3},{2,0},{3,1},{4,6},{5,7},{6,4},{7,5},{8,10},{9,11},{10,... | collective-permute-start | bytes 884744 | tf_op jit(solution)/shard_map/ppermute | solution.py:198
  29.5 1.5 %collective-permute-start.4 = (bf16[64,2304]{1,0:T(8,128)(2,1)S(1)}, bf16[64,2304]{1,0:T(8,128)(2,1)S(1)}, u32[]{:S(2)}, u32[]{:S(2)}) collective-permute-start(bf16[64,2304]{1,0:T(8,128)(2,1)S(1)} %get-tuple-element.42), channel_id=1, source_target_pairs={{0,4},{1,5},{2,6},{3,7},{4,0},{5,1},{6,2},{7,3},{8,12},{9,13},{10,... | collective-permute-start | bytes 884744 | tf_op jit(solution)/shard_map/ppermute | solution.py:198
  31.2 3.9 %collective-permute-done.10.refs_6_ = bf16[64,1280]{1,0:T(8,128)(2,1)S(1)} collective-permute-done((bf16[64,1280]{1,0:T(8,128)(2,1)S(1)}, bf16[64,1280]{1,0:T(8,128)(2,1)S(1)}, u32[]{:S(2)}, u32[]{:S(2)}) %collective-permute-start.10) | collective-permute-done | bytes 163872 | tf_op jit(solution)/shard_map/ppermute | solution.py:198
  35.2 0.5 collective-permute-start.17
  35.7 0.9 collective-permute-done.16.refs_4_
  36.8 0.3 collective-permute-start.12
  37.3 3.3 %collective-permute-done.4.refs_2_ = bf16[64,2304]{1,0:T(8,128)(2,1)S(1)} collective-permute-done((bf16[64,2304]{1,0:T(8,128)(2,1)S(1)}, bf16[64,2304]{1,0:T(8,128)(2,1)S(1)}, u32[]{:S(2)}, u32[]{:S(2)}) %collective-permute-start.4) | collective-permute-done | bytes 294944 | tf_op jit(solution)/shard_map/ppermute | solution.py:198
  40.6 0.5 collective-permute-start.15
  41.2 1.6 %collective-permute-done.19.refs_7_ = bf16[64,1280]{1,0:T(8,128)(2,1)S(1)} collective-permute-done((bf16[64,1280]{1,0:T(8,128)(2,1)S(1)}, bf16[64,1280]{1,0:T(8,128)(2,1)S(1)}, u32[]{:S(2)}, u32[]{:S(2)}) %collective-permute-start.19) | collective-permute-done | bytes 163872 | tf_op jit(solution)/shard_map/ppermute | solution.py:198
  42.9 2.0 %copy-done = bf16[1,3584,512]{2,1,0:T(8,128)(2,1)S(1)} copy-done((bf16[1,3584,512]{2,1,0:T(8,128)(2,1)S(1)}, bf16[1,3584,512]{2,1,0:T(8,128)(2,1)}, u32[]{:S(2)}) %copy-start) | copy-done | bytes 3670040
  44.9 2.0 %copy-done.2 = bf16[1,3584,512]{2,1,0:T(8,128)(2,1)S(1)} copy-done((bf16[1,3584,512]{2,1,0:T(8,128)(2,1)S(1)}, bf16[1,3584,512]{2,1,0:T(8,128)(2,1)}, u32[]{:S(2)}) %copy-start.2) | copy-done | bytes 3670040
  47.0 2.2 %shard_map.68.hidden_ref = bf16[256,512]{1,0:T(8,128)(2,1)S(1)} custom-call(bf16[64,2304]{1,0:T(8,128)(2,1)S(1)} %collective-permute-done.12.refs_0_, bf16[64,2304]{1,0:T(8,128)(2,1)S(1)} %collective-permute-done.13.refs_1_, bf16[64,2304]{1,0:T(8,128)(2,1)S(1)} %collective-permute-done.14.refs_2_, bf16[64,2304]{1,0:T(8,128)(2,1)S(1)} %collective-permute-done.15.refs_3_, ...), custom_call_target="tpu_custom_call" | custom-call | flops 1879048192 | bytes 9437184 | tf_op jit(solution)/shard_map/pallas_call | solution.py:22
  49.2 1.3 %shard_map.69 = (bf16[256,2304]{1,0:T(8,128)(2,1)S(1)}, bf16[256,1280]{1,0:T(8,128)(2,1)S(1)}) custom-call(bf16[256,512]{1,0:T(8,128)(2,1)S(1)} %shard_map.68.hidden_ref, bf16[1,512,3584]{2,1,0:T(8,128)(2,1)S(1)} %copy-done.4), custom_call_target="tpu_custom_call" | custom-call | flops 939524096 | bytes 5767168 | tf_op jit(solution)/shard_map/pallas_call | solution.py:22
  50.8 0.4 collective-permute-start.21
  51.1 0.4 copy-done.1
  51.5 2.2 %shard_map.67.hidden_ref = bf16[256,512]{1,0:T(8,128)(2,1)S(1)} custom-call(bf16[64,2304]{1,0:T(8,128)(2,1)S(1)} %get-tuple-element.40.refs_0_, bf16[64,2304]{1,0:T(8,128)(2,1)S(1)} %collective-permute-done.3.refs_1_, bf16[64,2304]{1,0:T(8,128)(2,1)S(1)} %collective-permute-done.4.refs_2_, bf16[64,2304]{1,0:T(8,128)(2,1)S(1)} %collective-permute-done.5.refs_3_, ...), custom_call_target="tpu_custom_call" | custom-call | flops 1879048192 | bytes 9437184 | tf_op jit(solution)/shard_map/pallas_call | solution.py:22
  53.7 0.7 collective-permute-done.21.second_ref
  54.4 1.3 %shard_map.70 = (bf16[64,2304]{1,0:T(8,128)(2,1)S(1)}, bf16[64,2304]{1,0:T(8,128)(2,1)S(1)}, bf16[64,2304]{1,0:T(8,128)(2,1)S(1)}, bf16[64,2304]{1,0:T(8,128)(2,...) custom-call(bf16[256,512]{1,0:T(8,128)(2,1)S(1)} %shard_map.67.hidde, ...), custom_call_target="tpu_custom_call" | custom-call | flops 939524096 | bytes 7602176 | tf_op jit(solution)/shard_map/pallas_call | solution.py:22
  55.8 1.3 %collective-permute-start.22 = (bf16[64,2304]{1,0:T(8,128)(2,1)S(1)}, bf16[64,2304]{1,0:T(8,128)(2,1)S(1)}, u32[]{:S(2)}, u32[]{:S(2)}) collective-permute-start(bf16[64,2304]{1,0:T(8,128)(2,1)S(1)} %get-tuple-element.52), channel_id=1, source_target_pairs={{0,2},{1,3},{2,0},{3,1},{4,6},{5,7},{6,4},{7,5},{8,10},{9,11},{10,... | collective-permute-start | bytes 884744 | tf_op jit(solution)/shard_map/ppermute | solution.py:198
  57.1 1.5 %collective-permute-start.23 = (bf16[64,2304]{1,0:T(8,128)(2,1)S(1)}, bf16[64,2304]{1,0:T(8,128)(2,1)S(1)}, u32[]{:S(2)}, u32[]{:S(2)}) collective-permute-start(bf16[64,2304]{1,0:T(8,128)(2,1)S(1)} %get-tuple-element.53), channel_id=1, source_target_pairs={{0,4},{1,5},{2,6},{3,7},{4,0},{5,1},{6,2},{7,3},{8,12},{9,13},{10,... | collective-permute-start | bytes 884744 | tf_op jit(solution)/shard_map/ppermute | solution.py:198
  58.6 0.7 collective-permute-start.24
  59.4 2.6 %collective-permute-start.29 = (bf16[64,1280]{1,0:T(8,128)(2,1)S(1)}, bf16[64,1280]{1,0:T(8,128)(2,1)S(1)}, u32[]{:S(2)}, u32[]{:S(2)}) collective-permute-start(bf16[64,1280]{1,0:T(8,128)(2,1)S(1)} %get-tuple-element.64), channel_id=1, source_target_pairs={{0,16},{1,17},{2,18},{3,19},{4,20},{5,21},{6,22},{7,23},{8,24},{9,... | collective-permute-start | bytes 491528 | tf_op jit(solution)/shard_map/ppermute | solution.py:198
  62.0 2.2 %collective-permute-start.30 = (bf16[64,1280]{1,0:T(8,128)(2,1)S(1)}, bf16[64,1280]{1,0:T(8,128)(2,1)S(1)}, u32[]{:S(2)}, u32[]{:S(2)}) collective-permute-start(bf16[64,1280]{1,0:T(8,128)(2,1)S(1)} %get-tuple-element.65), channel_id=1, source_target_pairs={{0,24},{1,25},{2,26},{3,27},{4,28},{5,29},{6,30},{7,31},{8,16},{9,... | collective-permute-start | bytes 491528 | tf_op jit(solution)/shard_map/ppermute | solution.py:198
  64.2 9.8 %collective-permute-done.29.refs_2_ = bf16[64,1280]{1,0:T(8,128)(2,1)S(1)} collective-permute-done((bf16[64,1280]{1,0:T(8,128)(2,1)S(1)}, bf16[64,1280]{1,0:T(8,128)(2,1)S(1)}, u32[]{:S(2)}, u32[]{:S(2)}) %collective-permute-start.29) | collective-permute-done | bytes 163872 | tf_op jit(solution)/shard_map/ppermute | solution.py:198
  73.9 0.4 shard_map.72
  74.4 0.8 collective-permute-start.31
  75.2 1.3 %collective-permute-start.32 = (bf16[32,1280]{1,0:T(8,128)(2,1)S(1)}, bf16[32,1280]{1,0:T(8,128)(2,1)S(1)}, u32[]{:S(2)}, u32[]{:S(2)}) collective-permute-start(bf16[32,1280]{1,0:T(8,128)(2,1)S(1)} %get-tuple-element.71), channel_id=1, source_target_pairs={{0,4},{1,5},{2,6},{3,7},{4,0},{5,1},{6,2},{7,3},{8,12},{9,13},{10,... | collective-permute-start | bytes 245768 | tf_op jit(solution)/shard_map/ppermute | solution.py:198
  76.5 1.5 %collective-permute-start.33 = (bf16[32,1280]{1,0:T(8,128)(2,1)S(1)}, bf16[32,1280]{1,0:T(8,128)(2,1)S(1)}, u32[]{:S(2)}, u32[]{:S(2)}) collective-permute-start(bf16[32,1280]{1,0:T(8,128)(2,1)S(1)} %get-tuple-element.72), channel_id=1, source_target_pairs={{0,6},{1,7},{2,4},{3,5},{4,2},{5,3},{6,0},{7,1},{8,14},{9,15},{10,... | collective-permute-start | bytes 245768 | tf_op jit(solution)/shard_map/ppermute | solution.py:198
  77.9 0.6 shard_map.71
  78.6 2.9 %collective-permute-start.25 = (bf16[32,2304]{1,0:T(8,128)(2,1)S(1)}, bf16[32,2304]{1,0:T(8,128)(2,1)S(1)}, u32[]{:S(2)}, u32[]{:S(2)}) collective-permute-start(bf16[32,2304]{1,0:T(8,128)(2,1)S(1)} %get-tuple-element.59), channel_id=1, source_target_pairs={{0,8},{1,9},{2,10},{3,11},{4,12},{5,13},{6,14},{7,15},{8,0},{9,1},... | collective-permute-start | bytes 442376 | tf_op jit(solution)/shard_map/ppermute | solution.py:198
  81.5 0.8 collective-permute-start.26
  82.2 1.7 %collective-permute-start.27 = (bf16[32,2304]{1,0:T(8,128)(2,1)S(1)}, bf16[32,2304]{1,0:T(8,128)(2,1)S(1)}, u32[]{:S(2)}, u32[]{:S(2)}) collective-permute-start(bf16[32,2304]{1,0:T(8,128)(2,1)S(1)} %get-tuple-element.61), channel_id=1, source_target_pairs={{0,24},{1,25},{2,26},{3,27},{4,28},{5,29},{6,30},{7,31},{8,16},{9,... | collective-permute-start | bytes 442376 | tf_op jit(solution)/shard_map/ppermute | solution.py:198
  83.9 1.9 %collective-permute-done.25 = bf16[32,2304]{1,0:T(8,128)(2,1)S(1)} collective-permute-done((bf16[32,2304]{1,0:T(8,128)(2,1)S(1)}, bf16[32,2304]{1,0:T(8,128)(2,1)S(1)}, u32[]{:S(2)}, u32[]{:S(2)}) %collective-permute-start.25) | collective-permute-done | bytes 147488 | tf_op jit(solution)/shard_map/ppermute | solution.py:198
  85.8 7.9 %collective-permute-done.26 = bf16[32,2304]{1,0:T(8,128)(2,1)S(1)} collective-permute-done((bf16[32,2304]{1,0:T(8,128)(2,1)S(1)}, bf16[32,2304]{1,0:T(8,128)(2,1)S(1)}, u32[]{:S(2)}, u32[]{:S(2)}) %collective-permute-start.26) | collective-permute-done | bytes 147488 | tf_op jit(solution)/shard_map/ppermute | solution.py:198
  93.8 0.7 pad_maximum_fusion
  (48 shorter events, 1.6 us)
Async XLA Ops:
  1.5 0.9 copy-start.5
  2.6 8.6 %collective-permute-start.8 = (bf16[32,1408]{1,0:T(8,128)(2,1)S(1)}, bf16[32,1408]{1,0:T(8,128)(2,1)S(1)}, u32[]{:S(2)}, u32[]{:S(2)}) collective-permute-start(bf16[32,1408]{1,0:T(8,128)(2,1)S(1)} %get-tuple-element.44.refs_0_), channel_id=1, source_target_pairs={{0,6},{1,7},{2,4},{3,5},{4,2},{5,3},{6,0},{7,1},{8,14},{9,15},{10,... | collective-permute-start | bytes 270344 | tf_op jit(solution)/shard_map/ppermute | solution.py:198
  6.6 5.3 %collective-permute-start.7 = (bf16[32,1408]{1,0:T(8,128)(2,1)S(1)}, bf16[32,1408]{1,0:T(8,128)(2,1)S(1)}, u32[]{:S(2)}, u32[]{:S(2)}) collective-permute-start(bf16[32,1408]{1,0:T(8,128)(2,1)S(1)} %get-tuple-element.44.refs_0_), channel_id=1, source_target_pairs={{0,4},{1,5},{2,6},{3,7},{4,0},{5,1},{6,2},{7,3},{8,12},{9,13},{10,... | collective-permute-start | bytes 270344 | tf_op jit(solution)/shard_map/ppermute | solution.py:198
  7.1 4.8 %collective-permute-start.6 = (bf16[32,1408]{1,0:T(8,128)(2,1)S(1)}, bf16[32,1408]{1,0:T(8,128)(2,1)S(1)}, u32[]{:S(2)}, u32[]{:S(2)}) collective-permute-start(bf16[32,1408]{1,0:T(8,128)(2,1)S(1)} %get-tuple-element.44.refs_0_), channel_id=1, source_target_pairs={{0,2},{1,3},{2,0},{3,1},{4,6},{5,7},{6,4},{7,5},{8,10},{9,11},{10,... | collective-permute-start | bytes 270344 | tf_op jit(solution)/shard_map/ppermute | solution.py:198
  7.2 10.3 %collective-permute-start.2 = (bf16[32,2432]{1,0:T(8,128)(2,1)S(1)}, bf16[32,2432]{1,0:T(8,128)(2,1)S(1)}, u32[]{:S(2)}, u32[]{:S(2)}) collective-permute-start(bf16[32,2432]{1,0:T(8,128)(2,1)S(1)} %get-tuple-element.39.refs_0_), channel_id=1, source_target_pairs={{0,24},{1,25},{2,26},{3,27},{4,28},{5,29},{6,30},{7,31},{8,16},{9,... | collective-permute-start | bytes 466952 | tf_op jit(solution)/shard_map/ppermute | solution.py:198
  11.2 15.1 %collective-permute-start.1 = (bf16[32,2432]{1,0:T(8,128)(2,1)S(1)}, bf16[32,2432]{1,0:T(8,128)(2,1)S(1)}, u32[]{:S(2)}, u32[]{:S(2)}) collective-permute-start(bf16[32,2432]{1,0:T(8,128)(2,1)S(1)} %get-tuple-element.39.refs_0_), channel_id=1, source_target_pairs={{0,16},{1,17},{2,18},{3,19},{4,20},{5,21},{6,22},{7,23},{8,24},{9,... | collective-permute-start | bytes 466952 | tf_op jit(solution)/shard_map/ppermute | solution.py:198
  11.2 15.1 %collective-permute-start = (bf16[32,2432]{1,0:T(8,128)(2,1)S(1)}, bf16[32,2432]{1,0:T(8,128)(2,1)S(1)}, u32[]{:S(2)}, u32[]{:S(2)}) collective-permute-start(bf16[32,2432]{1,0:T(8,128)(2,1)S(1)} %get-tuple-element.39.refs_0_), channel_id=1, source_target_pairs={{0,8},{1,9},{2,10},{3,11},{4,12},{5,13},{6,14},{7,15},{8,0},{9,1},... | collective-permute-start | bytes 466952 | tf_op jit(solution)/shard_map/ppermute | solution.py:198
  13.1 17.9 %collective-permute-start.9 = (bf16[64,1280]{1,0:T(8,128)(2,1)S(1)}, bf16[64,1280]{1,0:T(8,128)(2,1)S(1)}, u32[]{:S(2)}, u32[]{:S(2)}) collective-permute-start(bf16[64,1280]{1,0:T(8,128)(2,1)S(1)} %get-tuple-element.46), channel_id=1, source_target_pairs={{0,8},{1,9},{2,10},{3,11},{4,12},{5,13},{6,14},{7,15},{8,0},{9,1},... | collective-permute-start | bytes 491528 | tf_op jit(solution)/shard_map/ppermute | solution.py:198
  14.6 20.5 %collective-permute-start.10 = (bf16[64,1280]{1,0:T(8,128)(2,1)S(1)}, bf16[64,1280]{1,0:T(8,128)(2,1)S(1)}, u32[]{:S(2)}, u32[]{:S(2)}) collective-permute-start(bf16[64,1280]{1,0:T(8,128)(2,1)S(1)} %get-tuple-element.47), channel_id=1, source_target_pairs={{0,16},{1,17},{2,18},{3,19},{4,20},{5,21},{6,22},{7,23},{8,24},{9,... | collective-permute-start | bytes 491528 | tf_op jit(solution)/shard_map/ppermute | solution.py:198
  17.6 17.6 %collective-permute-start.11 = (bf16[64,1280]{1,0:T(8,128)(2,1)S(1)}, bf16[64,1280]{1,0:T(8,128)(2,1)S(1)}, u32[]{:S(2)}, u32[]{:S(2)}) collective-permute-start(bf16[64,1280]{1,0:T(8,128)(2,1)S(1)} %get-tuple-element.48), channel_id=1, source_target_pairs={{0,24},{1,25},{2,26},{3,27},{4,28},{5,29},{6,30},{7,31},{8,16},{9,... | collective-permute-start | bytes 491528 | tf_op jit(solution)/shard_map/ppermute | solution.py:198
  27.7 9.4 %collective-permute-start.3 = (bf16[64,2304]{1,0:T(8,128)(2,1)S(1)}, bf16[64,2304]{1,0:T(8,128)(2,1)S(1)}, u32[]{:S(2)}, u32[]{:S(2)}) collective-permute-start(bf16[64,2304]{1,0:T(8,128)(2,1)S(1)} %get-tuple-element.41), channel_id=1, source_target_pairs={{0,2},{1,3},{2,0},{3,1},{4,6},{5,7},{6,4},{7,5},{8,10},{9,11},{10,... | collective-permute-start | bytes 884744 | tf_op jit(solution)/shard_map/ppermute | solution.py:198
  29.5 11.2 %collective-permute-start.4 = (bf16[64,2304]{1,0:T(8,128)(2,1)S(1)}, bf16[64,2304]{1,0:T(8,128)(2,1)S(1)}, u32[]{:S(2)}, u32[]{:S(2)}) collective-permute-start(bf16[64,2304]{1,0:T(8,128)(2,1)S(1)} %get-tuple-element.42), channel_id=1, source_target_pairs={{0,4},{1,5},{2,6},{3,7},{4,0},{5,1},{6,2},{7,3},{8,12},{9,13},{10,... | collective-permute-start | bytes 884744 | tf_op jit(solution)/shard_map/ppermute | solution.py:198
  31.0 9.6 %collective-permute-start.5 = (bf16[64,2304]{1,0:T(8,128)(2,1)S(1)}, bf16[64,2304]{1,0:T(8,128)(2,1)S(1)}, u32[]{:S(2)}, u32[]{:S(2)}) collective-permute-start(bf16[64,2304]{1,0:T(8,128)(2,1)S(1)} %get-tuple-element.43), channel_id=1, source_target_pairs={{0,6},{1,7},{2,4},{3,5},{4,2},{5,3},{6,0},{7,1},{8,14},{9,15},{10,... | collective-permute-start | bytes 884744 | tf_op jit(solution)/shard_map/ppermute | solution.py:198
  35.2 1.4 %collective-permute-start.16 = (bf16[64,1280]{1,0:T(8,128)(2,1)S(1)}, bf16[64,1280]{1,0:T(8,128)(2,1)S(1)}, u32[]{:S(2)}, u32[]{:S(2)}) collective-permute-start(bf16[64,1280]{1,0:T(8,128)(2,1)S(1)} %get-tuple-element.45.refs_4_), channel_id=1, source_target_pairs={{0,1},{1,0},{2,3},{3,2},{4,5},{5,4},{6,7},{7,6},{8,9},{9,8},{10,11... | collective-permute-start | bytes 491528 | tf_op jit(solution)/shard_map/ppermute | solution.py:198
  35.2 1.6 %collective-permute-start.17 = (bf16[64,1280]{1,0:T(8,128)(2,1)S(1)}, bf16[64,1280]{1,0:T(8,128)(2,1)S(1)}, u32[]{:S(2)}, u32[]{:S(2)}) collective-permute-start(bf16[64,1280]{1,0:T(8,128)(2,1)S(1)} %collective-permute-done.9.refs_5_), channel_id=1, source_target_pairs={{0,1},{1,0},{2,3},{3,2},{4,5},{5,4},{6,7},{7,6},{8,9},{9,8},{10,11... | collective-permute-start | bytes 491528 | tf_op jit(solution)/shard_map/ppermute | solution.py:198
  36.5 4.6 %collective-permute-start.18 = (bf16[64,1280]{1,0:T(8,128)(2,1)S(1)}, bf16[64,1280]{1,0:T(8,128)(2,1)S(1)}, u32[]{:S(2)}, u32[]{:S(2)}) collective-permute-start(bf16[64,1280]{1,0:T(8,128)(2,1)S(1)} %collective-permute-done.10.refs_6_), channel_id=1, source_target_pairs={{0,1},{1,0},{2,3},{3,2},{4,5},{5,4},{6,7},{7,6},{8,9},{9,8},{10,11... | collective-permute-start | bytes 491528 | tf_op jit(solution)/shard_map/ppermute | solution.py:198
  36.8 6.1 %collective-permute-start.12 = (bf16[64,2304]{1,0:T(8,128)(2,1)S(1)}, bf16[64,2304]{1,0:T(8,128)(2,1)S(1)}, u32[]{:S(2)}, u32[]{:S(2)}) collective-permute-start(bf16[64,2304]{1,0:T(8,128)(2,1)S(1)} %get-tuple-element.40.refs_0_), channel_id=1, source_target_pairs={{0,1},{1,0},{2,3},{3,2},{4,5},{5,4},{6,7},{7,6},{8,9},{9,8},{10,11... | collective-permute-start | bytes 884744 | tf_op jit(solution)/shard_map/ppermute | solution.py:198
  37.1 5.8 %collective-permute-start.13 = (bf16[64,2304]{1,0:T(8,128)(2,1)S(1)}, bf16[64,2304]{1,0:T(8,128)(2,1)S(1)}, u32[]{:S(2)}, u32[]{:S(2)}) collective-permute-start(bf16[64,2304]{1,0:T(8,128)(2,1)S(1)} %collective-permute-done.3.refs_1_), channel_id=1, source_target_pairs={{0,1},{1,0},{2,3},{3,2},{4,5},{5,4},{6,7},{7,6},{8,9},{9,8},{10,11... | collective-permute-start | bytes 884744 | tf_op jit(solution)/shard_map/ppermute | solution.py:198
  40.6 2.2 %collective-permute-start.14 = (bf16[64,2304]{1,0:T(8,128)(2,1)S(1)}, bf16[64,2304]{1,0:T(8,128)(2,1)S(1)}, u32[]{:S(2)}, u32[]{:S(2)}) collective-permute-start(bf16[64,2304]{1,0:T(8,128)(2,1)S(1)} %collective-permute-done.4.refs_2_), channel_id=1, source_target_pairs={{0,1},{1,0},{2,3},{3,2},{4,5},{5,4},{6,7},{7,6},{8,9},{9,8},{10,11... | collective-permute-start | bytes 884744 | tf_op jit(solution)/shard_map/ppermute | solution.py:198
  40.6 2.2 %collective-permute-start.15 = (bf16[64,2304]{1,0:T(8,128)(2,1)S(1)}, bf16[64,2304]{1,0:T(8,128)(2,1)S(1)}, u32[]{:S(2)}, u32[]{:S(2)}) collective-permute-start(bf16[64,2304]{1,0:T(8,128)(2,1)S(1)} %collective-permute-done.5.refs_3_), channel_id=1, source_target_pairs={{0,1},{1,0},{2,3},{3,2},{4,5},{5,4},{6,7},{7,6},{8,9},{9,8},{10,11... | collective-permute-start | bytes 884744 | tf_op jit(solution)/shard_map/ppermute | solution.py:198
  41.1 1.7 %collective-permute-start.19 = (bf16[64,1280]{1,0:T(8,128)(2,1)S(1)}, bf16[64,1280]{1,0:T(8,128)(2,1)S(1)}, u32[]{:S(2)}, u32[]{:S(2)}) collective-permute-start(bf16[64,1280]{1,0:T(8,128)(2,1)S(1)} %collective-permute-done.11.refs_7_), channel_id=1, source_target_pairs={{0,1},{1,0},{2,3},{3,2},{4,5},{5,4},{6,7},{7,6},{8,9},{9,8},{10,11... | collective-permute-start | bytes 491528 | tf_op jit(solution)/shard_map/ppermute | solution.py:198
  42.9 2.0 %copy-start = (bf16[1,3584,512]{2,1,0:T(8,128)(2,1)S(1)}, bf16[1,3584,512]{2,1,0:T(8,128)(2,1)}, u32[]{:S(2)}) copy-start(bf16[1,3584,512]{2,1,0:T(8,128)(2,1)} %refs_8_.3) | copy-start | bytes 11010052
  44.9 2.0 %copy-start.2 = (bf16[1,3584,512]{2,1,0:T(8,128)(2,1)S(1)}, bf16[1,3584,512]{2,1,0:T(8,128)(2,1)}, u32[]{:S(2)}) copy-start(bf16[1,3584,512]{2,1,0:T(8,128)(2,1)} %refs_9_.3) | copy-start | bytes 11010052
  47.0 2.3 %copy-start.4 = (bf16[1,512,3584]{2,1,0:T(8,128)(2,1)S(1)}, bf16[1,512,3584]{2,1,0:T(8,128)(2,1)}, u32[]{:S(2)}) copy-start(bf16[1,512,3584]{2,1,0:T(8,128)(2,1)} %down_ref.3) | copy-start | bytes 11010052
  47.0 4.2 %copy-start.3 = (bf16[1,3584,512]{2,1,0:T(8,128)(2,1)S(1)}, bf16[1,3584,512]{2,1,0:T(8,128)(2,1)}, u32[]{:S(2)}) copy-start(bf16[1,3584,512]{2,1,0:T(8,128)(2,1)} %refs_9_.3) | copy-start | bytes 11010052
  49.2 2.3 %copy-start.1 = (bf16[1,3584,512]{2,1,0:T(8,128)(2,1)S(1)}, bf16[1,3584,512]{2,1,0:T(8,128)(2,1)}, u32[]{:S(2)}) copy-start(bf16[1,3584,512]{2,1,0:T(8,128)(2,1)} %refs_8_.3) | copy-start | bytes 11010052
  50.5 3.9 %collective-permute-start.20 = (bf16[256,2304]{1,0:T(8,128)(2,1)S(1)}, bf16[256,2304]{1,0:T(8,128)(2,1)S(1)}, u32[]{:S(2)}, u32[]{:S(2)}) collective-permute-start(bf16[256,2304]{1,0:T(8,128)(2,1)S(1)} %get-tuple-element.49), channel_id=1, source_target_pairs={{0,1},{1,0},{2,3},{3,2},{4,5},{5,4},{6,7},{7,6},{8,9},{9,8},{10,11... | collective-permute-start | bytes 3538952 | tf_op jit(solution)/shard_map/ppermute | solution.py:198
  50.8 3.6 %collective-permute-start.21 = (bf16[256,1280]{1,0:T(8,128)(2,1)S(1)}, bf16[256,1280]{1,0:T(8,128)(2,1)S(1)}, u32[]{:S(2)}, u32[]{:S(2)}) collective-permute-start(bf16[256,1280]{1,0:T(8,128)(2,1)S(1)} %get-tuple-element.50), channel_id=1, source_target_pairs={{0,1},{1,0},{2,3},{3,2},{4,5},{5,4},{6,7},{7,6},{8,9},{9,8},{10,11... | collective-permute-start | bytes 1966088 | tf_op jit(solution)/shard_map/ppermute | solution.py:198
  55.7 6.3 %collective-permute-start.28 = (bf16[64,1280]{1,0:T(8,128)(2,1)S(1)}, bf16[64,1280]{1,0:T(8,128)(2,1)S(1)}, u32[]{:S(2)}, u32[]{:S(2)}) collective-permute-start(bf16[64,1280]{1,0:T(8,128)(2,1)S(1)} %get-tuple-element.63), channel_id=1, source_target_pairs={{0,8},{1,9},{2,10},{3,11},{4,12},{5,13},{6,14},{7,15},{8,0},{9,1},... | collective-permute-start | bytes 491528 | tf_op jit(solution)/shard_map/ppermute | solution.py:198
  55.8 20.7 %collective-permute-start.22 = (bf16[64,2304]{1,0:T(8,128)(2,1)S(1)}, bf16[64,2304]{1,0:T(8,128)(2,1)S(1)}, u32[]{:S(2)}, u32[]{:S(2)}) collective-permute-start(bf16[64,2304]{1,0:T(8,128)(2,1)S(1)} %get-tuple-element.52), channel_id=1, source_target_pairs={{0,2},{1,3},{2,0},{3,1},{4,6},{5,7},{6,4},{7,5},{8,10},{9,11},{10,... | collective-permute-start | bytes 884744 | tf_op jit(solution)/shard_map/ppermute | solution.py:198
  57.1 20.8 %collective-permute-start.23 = (bf16[64,2304]{1,0:T(8,128)(2,1)S(1)}, bf16[64,2304]{1,0:T(8,128)(2,1)S(1)}, u32[]{:S(2)}, u32[]{:S(2)}) collective-permute-start(bf16[64,2304]{1,0:T(8,128)(2,1)S(1)} %get-tuple-element.53), channel_id=1, source_target_pairs={{0,4},{1,5},{2,6},{3,7},{4,0},{5,1},{6,2},{7,3},{8,12},{9,13},{10,... | collective-permute-start | bytes 884744 | tf_op jit(solution)/shard_map/ppermute | solution.py:198
  58.6 19.3 %collective-permute-start.24 = (bf16[64,2304]{1,0:T(8,128)(2,1)S(1)}, bf16[64,2304]{1,0:T(8,128)(2,1)S(1)}, u32[]{:S(2)}, u32[]{:S(2)}) collective-permute-start(bf16[64,2304]{1,0:T(8,128)(2,1)S(1)} %get-tuple-element.54), channel_id=1, source_target_pairs={{0,6},{1,7},{2,4},{3,5},{4,2},{5,3},{6,0},{7,1},{8,14},{9,15},{10,... | collective-permute-start | bytes 884744 | tf_op jit(solution)/shard_map/ppermute | solution.py:198
  59.4 14.6 %collective-permute-start.29 = (bf16[64,1280]{1,0:T(8,128)(2,1)S(1)}, bf16[64,1280]{1,0:T(8,128)(2,1)S(1)}, u32[]{:S(2)}, u32[]{:S(2)}) collective-permute-start(bf16[64,1280]{1,0:T(8,128)(2,1)S(1)} %get-tuple-element.64), channel_id=1, source_target_pairs={{0,16},{1,17},{2,18},{3,19},{4,20},{5,21},{6,22},{7,23},{8,24},{9,... | collective-permute-start | bytes 491528 | tf_op jit(solution)/shard_map/ppermute | solution.py:198
  62.0 11.9 %collective-permute-start.30 = (bf16[64,1280]{1,0:T(8,128)(2,1)S(1)}, bf16[64,1280]{1,0:T(8,128)(2,1)S(1)}, u32[]{:S(2)}, u32[]{:S(2)}) collective-permute-start(bf16[64,1280]{1,0:T(8,128)(2,1)S(1)} %get-tuple-element.65), channel_id=1, source_target_pairs={{0,24},{1,25},{2,26},{3,27},{4,28},{5,29},{6,30},{7,31},{8,16},{9,... | collective-permute-start | bytes 491528 | tf_op jit(solution)/shard_map/ppermute | solution.py:198
  74.4 7.8 %collective-permute-start.31 = (bf16[32,1280]{1,0:T(8,128)(2,1)S(1)}, bf16[32,1280]{1,0:T(8,128)(2,1)S(1)}, u32[]{:S(2)}, u32[]{:S(2)}) collective-permute-start(bf16[32,1280]{1,0:T(8,128)(2,1)S(1)} %get-tuple-element.70), channel_id=1, source_target_pairs={{0,2},{1,3},{2,0},{3,1},{4,6},{5,7},{6,4},{7,5},{8,10},{9,11},{10,... | collective-permute-start | bytes 245768 | tf_op jit(solution)/shard_map/ppermute | solution.py:198
  75.2 8.7 %collective-permute-start.32 = (bf16[32,1280]{1,0:T(8,128)(2,1)S(1)}, bf16[32,1280]{1,0:T(8,128)(2,1)S(1)}, u32[]{:S(2)}, u32[]{:S(2)}) collective-permute-start(bf16[32,1280]{1,0:T(8,128)(2,1)S(1)} %get-tuple-element.71), channel_id=1, source_target_pairs={{0,4},{1,5},{2,6},{3,7},{4,0},{5,1},{6,2},{7,3},{8,12},{9,13},{10,... | collective-permute-start | bytes 245768 | tf_op jit(solution)/shard_map/ppermute | solution.py:198
  76.5 7.4 %collective-permute-start.33 = (bf16[32,1280]{1,0:T(8,128)(2,1)S(1)}, bf16[32,1280]{1,0:T(8,128)(2,1)S(1)}, u32[]{:S(2)}, u32[]{:S(2)}) collective-permute-start(bf16[32,1280]{1,0:T(8,128)(2,1)S(1)} %get-tuple-element.72), channel_id=1, source_target_pairs={{0,6},{1,7},{2,4},{3,5},{4,2},{5,3},{6,0},{7,1},{8,14},{9,15},{10,... | collective-permute-start | bytes 245768 | tf_op jit(solution)/shard_map/ppermute | solution.py:198
  78.6 7.2 %collective-permute-start.25 = (bf16[32,2304]{1,0:T(8,128)(2,1)S(1)}, bf16[32,2304]{1,0:T(8,128)(2,1)S(1)}, u32[]{:S(2)}, u32[]{:S(2)}) collective-permute-start(bf16[32,2304]{1,0:T(8,128)(2,1)S(1)} %get-tuple-element.59), channel_id=1, source_target_pairs={{0,8},{1,9},{2,10},{3,11},{4,12},{5,13},{6,14},{7,15},{8,0},{9,1},... | collective-permute-start | bytes 442376 | tf_op jit(solution)/shard_map/ppermute | solution.py:198
  81.5 12.3 %collective-permute-start.26 = (bf16[32,2304]{1,0:T(8,128)(2,1)S(1)}, bf16[32,2304]{1,0:T(8,128)(2,1)S(1)}, u32[]{:S(2)}, u32[]{:S(2)}) collective-permute-start(bf16[32,2304]{1,0:T(8,128)(2,1)S(1)} %get-tuple-element.60), channel_id=1, source_target_pairs={{0,16},{1,17},{2,18},{3,19},{4,20},{5,21},{6,22},{7,23},{8,24},{9,... | collective-permute-start | bytes 442376 | tf_op jit(solution)/shard_map/ppermute | solution.py:198
  82.2 11.5 %collective-permute-start.27 = (bf16[32,2304]{1,0:T(8,128)(2,1)S(1)}, bf16[32,2304]{1,0:T(8,128)(2,1)S(1)}, u32[]{:S(2)}, u32[]{:S(2)}) collective-permute-start(bf16[32,2304]{1,0:T(8,128)(2,1)S(1)} %get-tuple-element.61), channel_id=1, source_target_pairs={{0,24},{1,25},{2,26},{3,27},{4,28},{5,29},{6,30},{7,31},{8,16},{9,... | collective-permute-start | bytes 442376 | tf_op jit(solution)/shard_map/ppermute | solution.py:198

commit v3 on v2

--- a/solution.py
+++ b/solution.py
@@ -11,7 +11,11 @@
 LANES = 128
 SHARE = (2, 3)
 TILE = 512
+CHUNK = 768
 VMEM_LIMIT = 24 << 20
+LOAD_LIMIT = 41 << 20
+HEAD_LIMIT = 60 << 20
+GROUPS = 1
 
 
 def call(kernel, out_shapes, *operands, flops=0, scalars=0):
@@ -45,27 +49,68 @@
     return high, middle, low
 
 
-def tag_kernel(experts, x_ref, ids_ref, weights_ref, first_ref, second_ref):
-    rows, width = x_ref.shape
-    split = first_ref.shape[1] - (first_ref.shape[1] + second_ref.shape[1] - width) // 2
-    tag_lanes = first_ref.shape[1] - split
-    lane = lax.broadcasted_iota(jnp.int32, (rows, tag_lanes), 1)
-    expert = lane % experts
-    group = lane // experts
-    flags = jnp.zeros((rows, tag_lanes), F32)
-    weights = jnp.zeros((rows, tag_lanes), F32)
-    for k in range(ids_ref.shape[1]):
-        match = ids_ref[:, k : k + 1] == expert
+def tag_kernel(experts, x_hbm, ids_hbm, weights_hbm, first_ref, second_ref, ids_in, weights_in, ids_ref, weights_ref, sems):
+    rows, width = x_hbm.shape
+    top = ids_hbm.shape[0]
+    tag_lanes = (first_ref.shape[1] + second_ref.shape[1] - width) // 2
+    split = first_ref.shape[1] - tag_lanes
+    ids_ref[...] = jnp.full(ids_ref.shape, -1, jnp.int32)
+    weights_ref[...] = jnp.zeros(weights_ref.shape, F32)
+    small = [
+        pltpu.make_async_copy(ids_hbm, ids_in, sems.at[0]),
+        pltpu.make_async_copy(weights_hbm, weights_in, sems.at[1]),
+    ]
+    large = [
+        pltpu.make_async_copy(x_hbm.at[:, :split], first_ref.at[:, :split], sems.at[2]),
+        pltpu.make_async_copy(x_hbm.at[:, split:], second_ref.at[:, : width - split], sems.at[3]),
+    ]
+    for copy in small + large:
+        copy.start()
+    for copy in small:
+        copy.wait()
+    ids_ref[:, :rows] = ids_in[...]
+    weights_ref[:, :rows] = weights_in[...]
+    lanes = ids_ref.shape[1]
+    row = lax.broadcasted_iota(jnp.int32, (tag_lanes, lanes), 0)
+    expert = row % experts
+    group = row // experts
+    flags = jnp.zeros((tag_lanes, lanes), F32)
+    weights = jnp.zeros((tag_lanes, lanes), F32)
+    for k in range(top):
+        match = ids_ref[k : k + 1, :] == expert
         flags = jnp.where(match, 1.0, flags)
-        weights = jnp.where(match, weights_ref[:, k : k + 1], weights)
+        weights = jnp.where(match, weights_ref[k : k + 1, :], weights)
     parts = [flags] + [part.astype(F32) for part in split3(weights)]
-    tag = jnp.zeros((rows, tag_lanes), F32)
+    tag = jnp.zeros((tag_lanes, lanes), F32)
     for number, part in enumerate(parts):
         tag = jnp.where(group == number, part, tag)
-    first_ref[:, :split] = x_ref[:, :split]
-    first_ref[:, split:] = tag.astype(BF16)
-    second_ref[:, : width - split] = x_ref[:, split:]
-    second_ref[:, width - split :] = tag.astype(BF16)
+    tag = tag.T[:rows].astype(BF16)
+    first_ref[:, split:] = tag
+    second_ref[:, width - split :] = tag
+    for copy in large:
+        copy.wait()
+
+
+def tagged_parts(experts, split, moe_input, route_ids, route_weights):
+    rows, width = moe_input.shape
+    top = route_ids.shape[1]
+    tag_lanes = pl.cdiv(4 * experts, LANES) * LANES
+    lanes = pl.cdiv(rows, LANES) * LANES
+    return pl.pallas_call(
+        functools.partial(tag_kernel, experts),
+        out_shape=shaped(1, (rows, split + tag_lanes)) + shaped(1, (rows, width - split + tag_lanes)),
+        in_specs=[pl.BlockSpec(memory_space=pl.ANY)] * 3,
+        out_specs=[pl.BlockSpec(memory_space=pltpu.VMEM)] * 2,
+        scratch_shapes=[
+            pltpu.VMEM((top, rows), jnp.int32),
+            pltpu.VMEM((top, rows), F32),
+            pltpu.VMEM((top, lanes), jnp.int32),
+            pltpu.VMEM((top, lanes), F32),
+            pltpu.SemaphoreType.DMA((4,)),
+        ],
+        compiler_params=pltpu.CompilerParams(vmem_limit_bytes=HEAD_LIMIT),
+        cost_estimate=pl.CostEstimate(flops=0, bytes_accessed=4 * rows * width, transcendentals=0),
+    )(moe_input, route_ids.T, route_weights.T)
 
 
 def pick_kernel(experts, cap, sources, targets, e_ref, *refs):
@@ -122,6 +167,19 @@
             outs[s][:, columns] = total[s * rows : (s + 1) * rows].astype(outs[s].dtype)
 
 
+def final_kernel(*refs):
+    terms, out_ref = refs[:-1], refs[-1]
+    start = 0
+    while terms:
+        size = terms[0].shape[1]
+        count = sum(r.shape[1] == size for r in terms)
+        total = terms[0][...]
+        for r in terms[1:count]:
+            total = total + r[...].astype(F32)
+        out_ref[:, pl.ds(start, size)] = total.astype(BF16)
+        terms, start = terms[count:], start + size
+
+
 def reorder(blocks, planes, cap, inverse=False):
     count = blocks * planes * cap
     row = lax.broadcasted_iota(jnp.int32, (count, count), 1 if inverse else 0)
@@ -131,8 +189,8 @@
 
 
 def hidden_kernel(blocks, planes, cap, *refs):
-    firsts, seconds = refs[:planes], refs[planes : planes + blocks]
-    gate_ref, up_ref, hidden_ref = refs[planes + blocks :]
+    firsts, seconds = refs[: planes * GROUPS], refs[planes * GROUPS : planes * GROUPS + blocks]
+    gate_ref, up_ref, hidden_ref = refs[planes * GROUPS + blocks :]
     split = firsts[0].shape[1]
     first = jnp.concatenate([r[...] for r in firsts], axis=0)
     second = jnp.concatenate([r[...] for r in seconds], axis=0)
@@ -147,6 +205,70 @@
         gate_value = product(gate_ref, columns)
         up_value = product(up_ref, columns)
         hidden_ref[:, columns] = (gate_value * jax.nn.sigmoid(gate_value) * up_value).astype(BF16)
+
+
+def chunks(split, width):
+    cuts = list(range(0, split, CHUNK)) + list(range(split, width, CHUNK)) + [width]
+    return [(start, stop - start) for start, stop in zip(cuts[:-1], cuts[1:])]
+
+
+def load_hidden_kernel(blocks, planes, cap, *refs):
+    firsts, seconds = refs[: planes * GROUPS], refs[planes * GROUPS : planes * GROUPS + blocks]
+    gate_hbm, up_hbm, down_hbm, hidden_ref, gate_ref, up_ref, down_ref, gate_sum, up_sum, sems = refs[planes * GROUPS + blocks :]
+    split = firsts[0].shape[1]
+    pieces = chunks(split, gate_ref.shape[1])
+    copies = []
+    for number, (start, size) in enumerate(pieces):
+        depth = pl.ds(start, size)
+        copies.append((
+            pltpu.make_async_copy(gate_hbm.at[:, depth], gate_ref.at[:, depth], sems.at[0, number]),
+            pltpu.make_async_copy(up_hbm.at[:, depth], up_ref.at[:, depth], sems.at[1, number]),
+        ))
+    last = pltpu.make_async_copy(down_hbm, down_ref, sems.at[0, len(pieces)])
+    for pair in copies:
+        pair[0].start()
+        pair[1].start()
+    last.start()
+    first = jnp.concatenate([r[...] for r in firsts], axis=0)
+    second = jnp.concatenate([r[...] for r in seconds], axis=0)
+    second = jnp.dot(reorder(blocks, planes, cap), second, preferred_element_type=F32).astype(BF16)
+    for number, (start, size) in enumerate(pieces):
+        x = first[:, start : start + size] if start < split else second[:, start - split : start - split + size]
+        depth = pl.ds(start, size)
+        for copy, ref, total in zip(copies[number], (gate_ref, up_ref), (gate_sum, up_sum)):
+            copy.wait()
+            part = jnp.dot(x, ref[0, depth, :], preferred_element_type=F32)
+            if number == 0:
+                total[...] = part
+            else:
+                total[...] += part
+    gate_value = gate_sum[...]
+    hidden_ref[...] = (gate_value * jax.nn.sigmoid(gate_value) * up_sum[...]).astype(BF16)
+    last.wait()
+
+
+def load_hidden(sizes, first, second, *weights):
+    slots = sizes[0] * sizes[1] * sizes[2]
+    split = first[0].shape[1]
+    width, hidden_width = weights[0].shape[1:]
+    vmem = pl.BlockSpec(memory_space=pltpu.VMEM)
+    return pl.pallas_call(
+        functools.partial(load_hidden_kernel, *sizes),
+        out_shape=shaped(1, (slots, hidden_width)) + [jax.ShapeDtypeStruct(w.shape, w.dtype) for w in weights],
+        in_specs=[vmem] * (len(first) + len(second)) + [pl.BlockSpec(memory_space=pl.ANY)] * 3,
+        out_specs=[vmem] * 4,
+        scratch_shapes=[
+            pltpu.VMEM((slots, hidden_width), F32),
+            pltpu.VMEM((slots, hidden_width), F32),
+            pltpu.SemaphoreType.DMA((2, len(chunks(split, width)) + 1)),
+        ],
+        compiler_params=pltpu.CompilerParams(vmem_limit_bytes=LOAD_LIMIT),
+        cost_estimate=pl.CostEstimate(
+            flops=4 * slots * width * hidden_width,
+            bytes_accessed=sum(w.size * w.dtype.itemsize for w in weights),
+            transcendentals=0,
+        ),
+    )(*first, *second, *weights)
 
 
 def down_kernel(blocks, planes, cap, hidden_ref, down_ref, first_ref, second_ref):
@@ -174,9 +296,9 @@
             for number, out in enumerate(outs):
                 out[:, columns] = both[number * rows : (number + 1) * rows]
 
-    halves(hidden, 0, first_ref, outs[:planes])
+    halves(hidden, 0, first_ref, outs[: planes * GROUPS])
     hidden = jnp.dot(reorder(blocks, planes, cap, True), hidden, preferred_element_type=F32).astype(BF16)
-    halves(hidden, split, second_ref, outs[planes:])
+    halves(hidden, split, second_ref, outs[planes * GROUPS :])
 
 
 def body(moe_input, route_ids, route_weights, gate_weight, up_weight, down_weight):
@@ -203,31 +325,31 @@
     def over_planes(arrays):
         return [arrays[0]] + [swap(arrays[j], 2 * j) for j in range(1, planes)]
 
-    tag_lanes = pl.cdiv(4 * experts, LANES) * LANES
-    tagged_first, tagged_second = call(
-        functools.partial(tag_kernel, experts),
-        shaped(1, (rows, split + tag_lanes)) + shaped(1, (rows, rest + tag_lanes)),
-        moe_input, route_ids, route_weights,
-    )
+    tagged_first, tagged_second = tagged_parts(experts, split, moe_input, route_ids, route_weights)
     plane_ids = my_block * planes + (my_plane ^ jnp.arange(planes, dtype=jnp.int32))
     block_ids = (my_block ^ jnp.arange(blocks, dtype=jnp.int32)) * planes + my_plane
     column = over_blocks([tagged_first] * blocks)
     plane = over_planes([tagged_second] * planes)
+    group = blocks // GROUPS
 
     def pick(arrays, targets, ids, columns):
         sources = len(arrays)
         out = call(
             functools.partial(pick_kernel, experts, cap, sources, targets),
-            shaped(targets, (sources * cap, columns)) + shaped(3, (sources * rows, slots)),
+            shaped(targets, (sources * cap, columns)) + shaped(3, (sources * rows, targets * sources * cap)),
             ids.reshape(1, targets), *arrays,
-            flops=2 * slots * sources * rows * columns, scalars=1,
+            flops=2 * targets * sources * cap * sources * rows * columns, scalars=1,
         )
         return out[:targets], out[targets:]
 
-    first, first_factors = pick(column, planes, plane_ids, split)
+    first, first_factors = [], []
+    for g in range(GROUPS):
+        pieces, factors = pick(column[g * group : (g + 1) * group], planes, plane_ids, split)
+        first.append(over_planes(pieces))
+        first_factors.append(factors)
     second, second_factors = pick(plane, blocks, block_ids, rest)
-    first = over_planes(first)
     second = over_blocks(second)
+    first = [first[g][j] for j in range(planes) for g in range(GROUPS)]
     first_other = [swap(piece, 1) for piece in first]
     second_other = [swap(piece, 1) for piece in second]
 
@@ -242,8 +364,10 @@
             flops=4 * slots * width * hidden_width,
         )[0]
 
+    hidden_other, gate_weight, up_weight, down_weight = load_hidden(
+        sizes, first_other, second_other, gate_weight, up_weight, down_weight
+    )
     hidden_mine = hidden_of(first, second)
-    hidden_other = hidden_of(first_other, second_other)
     parts = call(
         functools.partial(down_kernel, *sizes),
         shaped(1, (slots, split)) + shaped(1, (slots, rest)),
@@ -252,31 +376,26 @@
     )
     results = call(
         functools.partial(add_down_kernel, *sizes),
-        shaped(planes, (blocks * cap, split)) + shaped(blocks, (planes * cap, rest)),
+        shaped(planes * GROUPS, (group * cap, split)) + shaped(blocks, (planes * cap, rest)),
         hidden_mine, down_weight, swap(parts[0], 1), swap(parts[1], 1),
         flops=2 * slots * width * hidden_width,
     )
-    first = over_planes(results[:planes])
-    second = over_blocks(results[planes:])
-
-    def combine(arrays, factors, sources, columns):
+    def combine(arrays, factors, sources, columns, own):
         return call(
             functools.partial(combine_kernel, sources, len(arrays)),
-            shaped(1, (rows, columns), F32) + shaped(sources - 1, (rows, columns)),
+            shaped(own, (rows, columns), F32) + shaped(sources - own, (rows, columns)),
             *arrays, *factors,
-            flops=6 * slots * sources * rows * columns,
+            flops=6 * arrays[0].shape[0] * len(arrays) * sources * rows * columns,
         )
 
-    first = over_blocks(combine(first, first_factors, blocks, split))
-    second = over_planes(combine(second, second_factors, planes, rest))
-
-    def total(arrays):
-        result = arrays[0]
-        for array in arrays[1:]:
-            result = result + array.astype(F32)
-        return result.astype(BF16)
-
-    return jnp.concatenate([total(first), total(second)], axis=1)
+    first = []
+    for g in reversed(range(GROUPS)):
+        returned = over_planes(results[g : planes * GROUPS : GROUPS])
+        first = list(combine(returned, first_factors[g], group, split, int(g == 0))) + first
+    first = over_blocks(first)
+    second = over_blocks(results[planes * GROUPS :])
+    second = over_planes(combine(second, second_factors, planes, rest, 1))
+    return call(final_kernel, shaped(1, (rows, width)), *first, *second)[0]
 
 
 def solution(mesh):

time: 94.8 us -> 90.6 us (0.956)
  local copies, waits for them, and re-layouts: 6.9 us -> 1.8 us
  Pallas kernels: 10.9 us -> 15.4 us
  waiting for transfers between devices: 36.5 us -> 34.6 us
    pallas_call x0 -> x2, Pallas kernels: none -> 6.08 us  [the longest x1 4.38 us: load_hidden(): pl.pallas_call(functools.partial(load_hidden_kernel, *sizes), out_shape=s...]
    unnamed x14 -> x4, local copies, waits for them, and re-layouts: 6.9 us -> 1.8 us
    ppermute x34, waiting for transfers between devices: 36.5 us -> 34.6 us  [swap(): return lax.ppermute(array, 'ep', [(i, i ^ mask) for i in range(devices)])]
    pallas_call x9 -> x8, Pallas kernels: 10.9 us -> 9.31 us  [call(): pl.pallas_call(kernel, out_shape=out_shapes, in_specs=[smem] * scalars +...]
  transfers between devices with their start and end apart: 34 -> 34, of which waited for: 10 -> 12; matrix products, arithmetic and copies ran while one was open for 0% -> 0% of each run, Pallas kernels for 6% -> 7%
where the time goes in v3:
time: 90.6 us; the launch traced here: 90.4 us
  starting transfers between devices  38.5 us (42%)
  waiting for transfers between devices  34.6 us (38%)
  Pallas kernels  15.4 us (17%)
  local copies, waits for them, and re-layouts  1.8 us (2%)
    ppermute x34, starting transfers between devices, swap(): return lax.ppermute(array, 'ep', [(i, i ^ mask) for i in range(devices)])  38.5 us
    ppermute x34, waiting for transfers between devices, swap(): return lax.ppermute(array, 'ep', [(i, i ^ mask) for i in range(devices)])  34.6 us
    pallas_call x8, Pallas kernels, call(): pl.pallas_call(kernel, out_shape=out_shapes, in_specs=[smem] * scalars +...  9.31 us
    pallas_call x1, Pallas kernels, load_hidden(): pl.pallas_call(functools.partial(load_hidden_kernel, *sizes), out_shape=s...  4.38 us
  transfers between devices with their start and end apart: 34, of which 12 were waited for; matrix products, arithmetic and copies ran while one was open for 0% of the time, Pallas kernels for 7%

profile of v3, /device:TPU:0, one launch (start us, length us, event | category | flops | bytes accessed | tf_op | source)
XLA Modules:
  0.0 90.4 jit_solution(5386384602238739412)
XLA Ops:
  0.0 1.7 %shard_map.64 = (bf16[32,2432]{1,0:T(8,128)(2,1)}, bf16[32,1408]{1,0:T(8,128)(2,1)}) custom-call(bf16[32,3584]{1,0:T(8,128)(2,1)} %x_hbm.1, s32[8,32]{1,0:T(8,128)} %bitcast.2, f32[8,32]{1,0:T(8,128)} %bitcast.3), custom_call_target="tpu_custom_call" | custom-call | bytes 458752 | tf_op jit(solution)/shard_map/pallas_call | solution.py:99
  1.7 4.0 %collective-permute-start.8 = (bf16[32,1408]{1,0:T(8,128)(2,1)}, bf16[32,1408]{1,0:T(8,128)(2,1)S(1)}, u32[]{:S(2)}, u32[]{:S(2)}) collective-permute-start(bf16[32,1408]{1,0:T(8,128)(2,1)} %get-tuple-element.48.refs_0_), channel_id=1, source_target_pairs={{0,6},{1,7},{2,4},{3,5},{4,2},{5,3},{6,0},{7,1},{8,14},{9,15},{10,... | collective-permute-start | bytes 270344 | tf_op jit(solution)/shard_map/ppermute | solution.py:320
  5.7 0.5 collective-permute-start.7
  6.3 4.0 %collective-permute-start.2 = (bf16[32,2432]{1,0:T(8,128)(2,1)}, bf16[32,2432]{1,0:T(8,128)(2,1)S(1)}, u32[]{:S(2)}, u32[]{:S(2)}) collective-permute-start(bf16[32,2432]{1,0:T(8,128)(2,1)} %get-tuple-element.43.refs_0_), channel_id=1, source_target_pairs={{0,24},{1,25},{2,26},{3,27},{4,28},{5,29},{6,30},{7,31},{8,16},{9,... | collective-permute-start | bytes 466952 | tf_op jit(solution)/shard_map/ppermute | solution.py:320
  10.3 0.6 collective-permute-start
  11.0 0.9 copy-done.1
  11.8 1.2 %shard_map.66 = (bf16[64,1280]{1,0:T(8,128)(2,1)S(1)}, bf16[64,1280]{1,0:T(8,128)(2,1)S(1)}, bf16[64,1280]{1,0:T(8,128)(2,1)S(1)}, bf16[64,1280]{1,0:T(8,128)(2,...) custom-call(s32[1,4]{1,0:T(1,128)S(1)} %multiply_add_fusion.e_ref, ...), custom_call_target="tpu_custom_call" | custom-call | flops 83886080 | bytes 1212432 | tf_op jit(solution)/shard_map/pallas_call | solution.py:26
  13.1 1.6 %collective-permute-start.9 = (bf16[64,1280]{1,0:T(8,128)(2,1)S(1)}, bf16[64,1280]{1,0:T(8,128)(2,1)S(1)}, u32[]{:S(2)}, u32[]{:S(2)}) collective-permute-start(bf16[64,1280]{1,0:T(8,128)(2,1)S(1)} %get-tuple-element.50), channel_id=1, source_target_pairs={{0,8},{1,9},{2,10},{3,11},{4,12},{5,13},{6,14},{7,15},{8,0},{9,1},... | collective-permute-start | bytes 491528 | tf_op jit(solution)/shard_map/ppermute | solution.py:320
  14.7 2.8 %collective-permute-start.10 = (bf16[64,1280]{1,0:T(8,128)(2,1)S(1)}, bf16[64,1280]{1,0:T(8,128)(2,1)S(1)}, u32[]{:S(2)}, u32[]{:S(2)}) collective-permute-start(bf16[64,1280]{1,0:T(8,128)(2,1)S(1)} %get-tuple-element.51), channel_id=1, source_target_pairs={{0,16},{1,17},{2,18},{3,19},{4,20},{5,21},{6,22},{7,23},{8,24},{9,... | collective-permute-start | bytes 491528 | tf_op jit(solution)/shard_map/ppermute | solution.py:320
  17.5 1.7 %collective-permute-start.11 = (bf16[64,1280]{1,0:T(8,128)(2,1)S(1)}, bf16[64,1280]{1,0:T(8,128)(2,1)S(1)}, u32[]{:S(2)}, u32[]{:S(2)}) collective-permute-start(bf16[64,1280]{1,0:T(8,128)(2,1)S(1)} %get-tuple-element.52), channel_id=1, source_target_pairs={{0,24},{1,25},{2,26},{3,27},{4,28},{5,29},{6,30},{7,31},{8,16},{9,... | collective-permute-start | bytes 491528 | tf_op jit(solution)/shard_map/ppermute | solution.py:320
  19.3 6.3 %collective-permute-done.1.refs_2_ = bf16[32,2432]{1,0:T(8,128)(2,1)S(1)} collective-permute-done((bf16[32,2432]{1,0:T(8,128)(2,1)}, bf16[32,2432]{1,0:T(8,128)(2,1)S(1)}, u32[]{:S(2)}, u32[]{:S(2)}) %collective-permute-start.1) | collective-permute-done | bytes 155680 | tf_op jit(solution)/shard_map/ppermute | solution.py:320
  25.6 0.9 %copy-done = bf16[32,2432]{1,0:T(8,128)(2,1)S(1)} copy-done((bf16[32,2432]{1,0:T(8,128)(2,1)S(1)}, bf16[32,2432]{1,0:T(8,128)(2,1)}, u32[]{:S(2)}) %copy-start) | copy-done | bytes 155672
  26.5 1.4 %shard_map.65 = (bf16[64,2304]{1,0:T(8,128)(2,1)S(1)}, bf16[64,2304]{1,0:T(8,128)(2,1)S(1)}, bf16[64,2304]{1,0:T(8,128)(2,1)S(1)}, bf16[64,2304]{1,0:T(8,128)(2,...) custom-call(s32[1,4]{1,0:T(1,128)S(1)} %xor_add_fusion.e_ref, ...), custom_call_target="tpu_custom_call" | custom-call | flops 150994944 | bytes 1998864 | tf_op jit(solution)/shard_map/pallas_call | solution.py:26
  27.9 1.8 %collective-permute-start.3 = (bf16[64,2304]{1,0:T(8,128)(2,1)S(1)}, bf16[64,2304]{1,0:T(8,128)(2,1)S(1)}, u32[]{:S(2)}, u32[]{:S(2)}) collective-permute-start(bf16[64,2304]{1,0:T(8,128)(2,1)S(1)} %get-tuple-element.45), channel_id=1, source_target_pairs={{0,2},{1,3},{2,0},{3,1},{4,6},{5,7},{6,4},{7,5},{8,10},{9,11},{10,... | collective-permute-start | bytes 884744 | tf_op jit(solution)/shard_map/ppermute | solution.py:320
  29.7 1.5 %collective-permute-start.4 = (bf16[64,2304]{1,0:T(8,128)(2,1)S(1)}, bf16[64,2304]{1,0:T(8,128)(2,1)S(1)}, u32[]{:S(2)}, u32[]{:S(2)}) collective-permute-start(bf16[64,2304]{1,0:T(8,128)(2,1)S(1)} %get-tuple-element.46), channel_id=1, source_target_pairs={{0,4},{1,5},{2,6},{3,7},{4,0},{5,1},{6,2},{7,3},{8,12},{9,13},{10,... | collective-permute-start | bytes 884744 | tf_op jit(solution)/shard_map/ppermute | solution.py:320
  31.2 0.3 collective-permute-start.5
  31.5 3.0 %collective-permute-done.10.refs_6_ = bf16[64,1280]{1,0:T(8,128)(2,1)S(1)} collective-permute-done((bf16[64,1280]{1,0:T(8,128)(2,1)S(1)}, bf16[64,1280]{1,0:T(8,128)(2,1)S(1)}, u32[]{:S(2)}, u32[]{:S(2)}) %collective-permute-start.10) | collective-permute-done | bytes 163872 | tf_op jit(solution)/shard_map/ppermute | solution.py:320
  34.5 0.5 collective-permute-start.17
  35.0 0.9 collective-permute-done.16.refs_4_
  36.1 0.3 collective-permute-start.12
  36.6 4.2 %collective-permute-done.4.refs_2_ = bf16[64,2304]{1,0:T(8,128)(2,1)S(1)} collective-permute-done((bf16[64,2304]{1,0:T(8,128)(2,1)S(1)}, bf16[64,2304]{1,0:T(8,128)(2,1)S(1)}, u32[]{:S(2)}, u32[]{:S(2)}) %collective-permute-start.4) | collective-permute-done | bytes 294944 | tf_op jit(solution)/shard_map/ppermute | solution.py:320
  40.8 0.5 collective-permute-start.15
  41.4 1.6 %collective-permute-done.19.refs_7_ = bf16[64,1280]{1,0:T(8,128)(2,1)S(1)} collective-permute-done((bf16[64,1280]{1,0:T(8,128)(2,1)S(1)}, bf16[64,1280]{1,0:T(8,128)(2,1)S(1)}, u32[]{:S(2)}, u32[]{:S(2)}) %collective-permute-start.19) | collective-permute-done | bytes 163872 | tf_op jit(solution)/shard_map/ppermute | solution.py:320
  43.1 4.4 %shard_map.67 = (bf16[256,512]{1,0:T(8,128)(2,1)S(1)}, bf16[1,3584,512]{2,1,0:T(8,128)(2,1)S(1)}, bf16[1,3584,512]{2,1,0:T(8,128)(2,1)S(1)}, bf16[1,512,3584]{2,1,0:T(8,128)(2,1)S(1)}) custom-call(bf16[64,2304]{1,0:T(8,128)(2,1)S(1)} %collective-permute-done.12.refs_0_, bf16[64,2304]{1,0:T(8,128)(2,1)S(1)} %collective-permute-done.13.refs_1_, ...), custom_call_target="tpu_custom_call" | custom-call | flops 1879048192 | bytes 11010048 | tf_op jit(solution)/shard_map/pallas_call | solution.py:255
  47.5 1.3 %shard_map.69 = (bf16[256,2304]{1,0:T(8,128)(2,1)S(1)}, bf16[256,1280]{1,0:T(8,128)(2,1)S(1)}) custom-call(bf16[256,512]{1,0:T(8,128)(2,1)S(1)} %get-tuple-element.56.hidden_ref, bf16[1,512,3584]{2,1,0:T(8,128)(2,1)S(1)} %get-tuple-element.55.down_ref), custom_call_target="tpu_custom_call" | custom-call | flops 939524096 | bytes 5767168 | tf_op jit(solution)/shard_map/pallas_call | solution.py:26
  48.8 0.2 collective-permute-start.20
  49.0 0.4 collective-permute-start.21
  49.4 2.2 %shard_map.68.hidden_ref = bf16[256,512]{1,0:T(8,128)(2,1)S(1)} custom-call(bf16[64,2304]{1,0:T(8,128)(2,1)S(1)} %get-tuple-element.44.refs_0_, bf16[64,2304]{1,0:T(8,128)(2,1)S(1)} %collective-permute-done.3.refs_1_, bf16[64,2304]{1,0:T(8,128)(2,1)S(1)} %collective-permute-done.4.refs_2_, bf16[64,2304]{1,0:T(8,128)(2,1)S(1)} %collective-permute-done.5.refs_3_, ...), custom_call_target="tpu_custom_call" | custom-call | flops 1879048192 | bytes 9437184 | tf_op jit(solution)/shard_map/pallas_call | solution.py:26
  51.6 1.0 %collective-permute-done.21.second_ref = bf16[256,1280]{1,0:T(8,128)(2,1)S(1)} collective-permute-done((bf16[256,1280]{1,0:T(8,128)(2,1)S(1)}, bf16[256,1280]{1,0:T(8,128)(2,1)S(1)}, u32[]{:S(2)}, u32[]{:S(2)}) %collective-permute-start.21) | collective-permute-done | bytes 655392 | tf_op jit(solution)/shard_map/ppermute | solution.py:320
  52.7 1.3 %shard_map.70 = (bf16[64,2304]{1,0:T(8,128)(2,1)S(1)}, bf16[64,2304]{1,0:T(8,128)(2,1)S(1)}, bf16[64,2304]{1,0:T(8,128)(2,1)S(1)}, bf16[64,2304]{1,0:T(8,128)(2,...) custom-call(bf16[256,512]{1,0:T(8,128)(2,1)S(1)} %shard_map.68.hidde, ...), custom_call_target="tpu_custom_call" | custom-call | flops 939524096 | bytes 7602176 | tf_op jit(solution)/shard_map/pallas_call | solution.py:26
  54.0 0.9 collective-permute-start.22
  54.9 1.2 %collective-permute-start.23 = (bf16[64,2304]{1,0:T(8,128)(2,1)S(1)}, bf16[64,2304]{1,0:T(8,128)(2,1)S(1)}, u32[]{:S(2)}, u32[]{:S(2)}) collective-permute-start(bf16[64,2304]{1,0:T(8,128)(2,1)S(1)} %get-tuple-element.61), channel_id=1, source_target_pairs={{0,4},{1,5},{2,6},{3,7},{4,0},{5,1},{6,2},{7,3},{8,12},{9,13},{10,... | collective-permute-start | bytes 884744 | tf_op jit(solution)/shard_map/ppermute | solution.py:320
  56.1 1.5 %collective-permute-start.24 = (bf16[64,2304]{1,0:T(8,128)(2,1)S(1)}, bf16[64,2304]{1,0:T(8,128)(2,1)S(1)}, u32[]{:S(2)}, u32[]{:S(2)}) collective-permute-start(bf16[64,2304]{1,0:T(8,128)(2,1)S(1)} %get-tuple-element.62), channel_id=1, source_target_pairs={{0,6},{1,7},{2,4},{3,5},{4,2},{5,3},{6,0},{7,1},{8,14},{9,15},{10,... | collective-permute-start | bytes 884744 | tf_op jit(solution)/shard_map/ppermute | solution.py:320
  57.6 2.6 %collective-permute-start.29 = (bf16[64,1280]{1,0:T(8,128)(2,1)S(1)}, bf16[64,1280]{1,0:T(8,128)(2,1)S(1)}, u32[]{:S(2)}, u32[]{:S(2)}) collective-permute-start(bf16[64,1280]{1,0:T(8,128)(2,1)S(1)} %get-tuple-element.72), channel_id=1, source_target_pairs={{0,16},{1,17},{2,18},{3,19},{4,20},{5,21},{6,22},{7,23},{8,24},{9,... | collective-permute-start | bytes 491528 | tf_op jit(solution)/shard_map/ppermute | solution.py:320
  60.3 2.2 %collective-permute-start.30 = (bf16[64,1280]{1,0:T(8,128)(2,1)S(1)}, bf16[64,1280]{1,0:T(8,128)(2,1)S(1)}, u32[]{:S(2)}, u32[]{:S(2)}) collective-permute-start(bf16[64,1280]{1,0:T(8,128)(2,1)S(1)} %get-tuple-element.73), channel_id=1, source_target_pairs={{0,24},{1,25},{2,26},{3,27},{4,28},{5,29},{6,30},{7,31},{8,16},{9,... | collective-permute-start | bytes 491528 | tf_op jit(solution)/shard_map/ppermute | solution.py:320
  62.4 9.8 %collective-permute-done.29.refs_2_ = bf16[64,1280]{1,0:T(8,128)(2,1)S(1)} collective-permute-done((bf16[64,1280]{1,0:T(8,128)(2,1)S(1)}, bf16[64,1280]{1,0:T(8,128)(2,1)S(1)}, u32[]{:S(2)}, u32[]{:S(2)}) %collective-permute-start.29) | collective-permute-done | bytes 163872 | tf_op jit(solution)/shard_map/ppermute | solution.py:320
  72.2 0.4 shard_map.72
  72.6 0.9 collective-permute-start.31
  73.5 0.6 shard_map.71
  74.1 2.9 %collective-permute-start.25 = (bf16[32,2304]{1,0:T(8,128)(2,1)S(1)}, bf16[32,2304]{1,0:T(8,128)(2,1)S(1)}, u32[]{:S(2)}, u32[]{:S(2)}) collective-permute-start(bf16[32,2304]{1,0:T(8,128)(2,1)S(1)} %get-tuple-element.67), channel_id=1, source_target_pairs={{0,8},{1,9},{2,10},{3,11},{4,12},{5,13},{6,14},{7,15},{8,0},{9,1},... | collective-permute-start | bytes 442376 | tf_op jit(solution)/shard_map/ppermute | solution.py:320
  77.0 0.5 collective-permute-start.26
  77.5 1.9 %collective-permute-start.27 = (bf16[32,2304]{1,0:T(8,128)(2,1)S(1)}, bf16[32,2304]{1,0:T(8,128)(2,1)S(1)}, u32[]{:S(2)}, u32[]{:S(2)}) collective-permute-start(bf16[32,2304]{1,0:T(8,128)(2,1)S(1)} %get-tuple-element.69), channel_id=1, source_target_pairs={{0,24},{1,25},{2,26},{3,27},{4,28},{5,29},{6,30},{7,31},{8,16},{9,... | collective-permute-start | bytes 442376 | tf_op jit(solution)/shard_map/ppermute | solution.py:320
  79.4 1.2 %collective-permute-start.32 = (bf16[32,1280]{1,0:T(8,128)(2,1)S(1)}, bf16[32,1280]{1,0:T(8,128)(2,1)S(1)}, u32[]{:S(2)}, u32[]{:S(2)}) collective-permute-start(bf16[32,1280]{1,0:T(8,128)(2,1)S(1)} %get-tuple-element.79), channel_id=1, source_target_pairs={{0,4},{1,5},{2,6},{3,7},{4,0},{5,1},{6,2},{7,3},{8,12},{9,13},{10,... | collective-permute-start | bytes 245768 | tf_op jit(solution)/shard_map/ppermute | solution.py:320
  80.7 1.5 %collective-permute-start.33 = (bf16[32,1280]{1,0:T(8,128)(2,1)S(1)}, bf16[32,1280]{1,0:T(8,128)(2,1)S(1)}, u32[]{:S(2)}, u32[]{:S(2)}) collective-permute-start(bf16[32,1280]{1,0:T(8,128)(2,1)S(1)} %get-tuple-element.80), channel_id=1, source_target_pairs={{0,6},{1,7},{2,4},{3,5},{4,2},{5,3},{6,0},{7,1},{8,14},{9,15},{10,... | collective-permute-start | bytes 245768 | tf_op jit(solution)/shard_map/ppermute | solution.py:320
  82.1 1.7 %collective-permute-done.32.refs_6_ = bf16[32,1280]{1,0:T(8,128)(2,1)S(1)} collective-permute-done((bf16[32,1280]{1,0:T(8,128)(2,1)S(1)}, bf16[32,1280]{1,0:T(8,128)(2,1)S(1)}, u32[]{:S(2)}, u32[]{:S(2)}) %collective-permute-start.32) | collective-permute-done | bytes 81952 | tf_op jit(solution)/shard_map/ppermute | solution.py:320
  83.9 2.1 %collective-permute-done.33.refs_7_ = bf16[32,1280]{1,0:T(8,128)(2,1)S(1)} collective-permute-done((bf16[32,1280]{1,0:T(8,128)(2,1)S(1)}, bf16[32,1280]{1,0:T(8,128)(2,1)S(1)}, u32[]{:S(2)}, u32[]{:S(2)}) %collective-permute-start.33) | collective-permute-done | bytes 81952 | tf_op jit(solution)/shard_map/ppermute | solution.py:320
  86.0 3.6 %collective-permute-done.26.refs_2_ = bf16[32,2304]{1,0:T(8,128)(2,1)S(1)} collective-permute-done((bf16[32,2304]{1,0:T(8,128)(2,1)S(1)}, bf16[32,2304]{1,0:T(8,128)(2,1)S(1)}, u32[]{:S(2)}, u32[]{:S(2)}) %collective-permute-start.26) | collective-permute-done | bytes 147488 | tf_op jit(solution)/shard_map/ppermute | solution.py:320
  89.6 0.8 shard_map.73
  (36 shorter events, 0.8 us)
Async XLA Ops:
  1.7 8.6 %collective-permute-start.8 = (bf16[32,1408]{1,0:T(8,128)(2,1)}, bf16[32,1408]{1,0:T(8,128)(2,1)S(1)}, u32[]{:S(2)}, u32[]{:S(2)}) collective-permute-start(bf16[32,1408]{1,0:T(8,128)(2,1)} %get-tuple-element.48.refs_0_), channel_id=1, source_target_pairs={{0,6},{1,7},{2,4},{3,5},{4,2},{5,3},{6,0},{7,1},{8,14},{9,15},{10,... | collective-permute-start | bytes 270344 | tf_op jit(solution)/shard_map/ppermute | solution.py:320
  5.7 5.3 %collective-permute-start.7 = (bf16[32,1408]{1,0:T(8,128)(2,1)}, bf16[32,1408]{1,0:T(8,128)(2,1)S(1)}, u32[]{:S(2)}, u32[]{:S(2)}) collective-permute-start(bf16[32,1408]{1,0:T(8,128)(2,1)} %get-tuple-element.48.refs_0_), channel_id=1, source_target_pairs={{0,4},{1,5},{2,6},{3,7},{4,0},{5,1},{6,2},{7,3},{8,12},{9,13},{10,... | collective-permute-start | bytes 270344 | tf_op jit(solution)/shard_map/ppermute | solution.py:320
  6.2 4.8 %collective-permute-start.6 = (bf16[32,1408]{1,0:T(8,128)(2,1)}, bf16[32,1408]{1,0:T(8,128)(2,1)S(1)}, u32[]{:S(2)}, u32[]{:S(2)}) collective-permute-start(bf16[32,1408]{1,0:T(8,128)(2,1)} %get-tuple-element.48.refs_0_), channel_id=1, source_target_pairs={{0,2},{1,3},{2,0},{3,1},{4,6},{5,7},{6,4},{7,5},{8,10},{9,11},{10,... | collective-permute-start | bytes 270344 | tf_op jit(solution)/shard_map/ppermute | solution.py:320
  6.3 11.2 %collective-permute-start.2 = (bf16[32,2432]{1,0:T(8,128)(2,1)}, bf16[32,2432]{1,0:T(8,128)(2,1)S(1)}, u32[]{:S(2)}, u32[]{:S(2)}) collective-permute-start(bf16[32,2432]{1,0:T(8,128)(2,1)} %get-tuple-element.43.refs_0_), channel_id=1, source_target_pairs={{0,24},{1,25},{2,26},{3,27},{4,28},{5,29},{6,30},{7,31},{8,16},{9,... | collective-permute-start | bytes 466952 | tf_op jit(solution)/shard_map/ppermute | solution.py:320
  10.3 15.3 %collective-permute-start.1 = (bf16[32,2432]{1,0:T(8,128)(2,1)}, bf16[32,2432]{1,0:T(8,128)(2,1)S(1)}, u32[]{:S(2)}, u32[]{:S(2)}) collective-permute-start(bf16[32,2432]{1,0:T(8,128)(2,1)} %get-tuple-element.43.refs_0_), channel_id=1, source_target_pairs={{0,16},{1,17},{2,18},{3,19},{4,20},{5,21},{6,22},{7,23},{8,24},{9,... | collective-permute-start | bytes 466952 | tf_op jit(solution)/shard_map/ppermute | solution.py:320
  10.3 15.3 %collective-permute-start = (bf16[32,2432]{1,0:T(8,128)(2,1)}, bf16[32,2432]{1,0:T(8,128)(2,1)S(1)}, u32[]{:S(2)}, u32[]{:S(2)}) collective-permute-start(bf16[32,2432]{1,0:T(8,128)(2,1)} %get-tuple-element.43.refs_0_), channel_id=1, source_target_pairs={{0,8},{1,9},{2,10},{3,11},{4,12},{5,13},{6,14},{7,15},{8,0},{9,1},... | collective-permute-start | bytes 466952 | tf_op jit(solution)/shard_map/ppermute | solution.py:320
  11.0 0.9 copy-start.1
  13.1 18.1 %collective-permute-start.9 = (bf16[64,1280]{1,0:T(8,128)(2,1)S(1)}, bf16[64,1280]{1,0:T(8,128)(2,1)S(1)}, u32[]{:S(2)}, u32[]{:S(2)}) collective-permute-start(bf16[64,1280]{1,0:T(8,128)(2,1)S(1)} %get-tuple-element.50), channel_id=1, source_target_pairs={{0,8},{1,9},{2,10},{3,11},{4,12},{5,13},{6,14},{7,15},{8,0},{9,1},... | collective-permute-start | bytes 491528 | tf_op jit(solution)/shard_map/ppermute | solution.py:320
  14.7 19.8 %collective-permute-start.10 = (bf16[64,1280]{1,0:T(8,128)(2,1)S(1)}, bf16[64,1280]{1,0:T(8,128)(2,1)S(1)}, u32[]{:S(2)}, u32[]{:S(2)}) collective-permute-start(bf16[64,1280]{1,0:T(8,128)(2,1)S(1)} %get-tuple-element.51), channel_id=1, source_target_pairs={{0,16},{1,17},{2,18},{3,19},{4,20},{5,21},{6,22},{7,23},{8,24},{9,... | collective-permute-start | bytes 491528 | tf_op jit(solution)/shard_map/ppermute | solution.py:320
  17.5 16.9 %collective-permute-start.11 = (bf16[64,1280]{1,0:T(8,128)(2,1)S(1)}, bf16[64,1280]{1,0:T(8,128)(2,1)S(1)}, u32[]{:S(2)}, u32[]{:S(2)}) collective-permute-start(bf16[64,1280]{1,0:T(8,128)(2,1)S(1)} %get-tuple-element.52), channel_id=1, source_target_pairs={{0,24},{1,25},{2,26},{3,27},{4,28},{5,29},{6,30},{7,31},{8,16},{9,... | collective-permute-start | bytes 491528 | tf_op jit(solution)/shard_map/ppermute | solution.py:320
  25.6 0.9 %copy-start = (bf16[32,2432]{1,0:T(8,128)(2,1)S(1)}, bf16[32,2432]{1,0:T(8,128)(2,1)}, u32[]{:S(2)}) copy-start(bf16[32,2432]{1,0:T(8,128)(2,1)} %get-tuple-element.43.refs_0_) | copy-start | bytes 466948
  27.9 8.6 %collective-permute-start.3 = (bf16[64,2304]{1,0:T(8,128)(2,1)S(1)}, bf16[64,2304]{1,0:T(8,128)(2,1)S(1)}, u32[]{:S(2)}, u32[]{:S(2)}) collective-permute-start(bf16[64,2304]{1,0:T(8,128)(2,1)S(1)} %get-tuple-element.45), channel_id=1, source_target_pairs={{0,2},{1,3},{2,0},{3,1},{4,6},{5,7},{6,4},{7,5},{8,10},{9,11},{10,... | collective-permute-start | bytes 884744 | tf_op jit(solution)/shard_map/ppermute | solution.py:320
  29.7 11.2 %collective-permute-start.4 = (bf16[64,2304]{1,0:T(8,128)(2,1)S(1)}, bf16[64,2304]{1,0:T(8,128)(2,1)S(1)}, u32[]{:S(2)}, u32[]{:S(2)}) collective-permute-start(bf16[64,2304]{1,0:T(8,128)(2,1)S(1)} %get-tuple-element.46), channel_id=1, source_target_pairs={{0,4},{1,5},{2,6},{3,7},{4,0},{5,1},{6,2},{7,3},{8,12},{9,13},{10,... | collective-permute-start | bytes 884744 | tf_op jit(solution)/shard_map/ppermute | solution.py:320
  31.2 9.6 %collective-permute-start.5 = (bf16[64,2304]{1,0:T(8,128)(2,1)S(1)}, bf16[64,2304]{1,0:T(8,128)(2,1)S(1)}, u32[]{:S(2)}, u32[]{:S(2)}) collective-permute-start(bf16[64,2304]{1,0:T(8,128)(2,1)S(1)} %get-tuple-element.47), channel_id=1, source_target_pairs={{0,6},{1,7},{2,4},{3,5},{4,2},{5,3},{6,0},{7,1},{8,14},{9,15},{10,... | collective-permute-start | bytes 884744 | tf_op jit(solution)/shard_map/ppermute | solution.py:320
  34.5 1.4 %collective-permute-start.16 = (bf16[64,1280]{1,0:T(8,128)(2,1)S(1)}, bf16[64,1280]{1,0:T(8,128)(2,1)S(1)}, u32[]{:S(2)}, u32[]{:S(2)}) collective-permute-start(bf16[64,1280]{1,0:T(8,128)(2,1)S(1)} %get-tuple-element.49.refs_4_), channel_id=1, source_target_pairs={{0,1},{1,0},{2,3},{3,2},{4,5},{5,4},{6,7},{7,6},{8,9},{9,8},{10,11... | collective-permute-start | bytes 491528 | tf_op jit(solution)/shard_map/ppermute | solution.py:320
  34.5 1.6 %collective-permute-start.17 = (bf16[64,1280]{1,0:T(8,128)(2,1)S(1)}, bf16[64,1280]{1,0:T(8,128)(2,1)S(1)}, u32[]{:S(2)}, u32[]{:S(2)}) collective-permute-start(bf16[64,1280]{1,0:T(8,128)(2,1)S(1)} %collective-permute-done.9.refs_5_), channel_id=1, source_target_pairs={{0,1},{1,0},{2,3},{3,2},{4,5},{5,4},{6,7},{7,6},{8,9},{9,8},{10,11... | collective-permute-start | bytes 491528 | tf_op jit(solution)/shard_map/ppermute | solution.py:320
  35.8 5.5 %collective-permute-start.18 = (bf16[64,1280]{1,0:T(8,128)(2,1)S(1)}, bf16[64,1280]{1,0:T(8,128)(2,1)S(1)}, u32[]{:S(2)}, u32[]{:S(2)}) collective-permute-start(bf16[64,1280]{1,0:T(8,128)(2,1)S(1)} %collective-permute-done.10.refs_6_), channel_id=1, source_target_pairs={{0,1},{1,0},{2,3},{3,2},{4,5},{5,4},{6,7},{7,6},{8,9},{9,8},{10,11... | collective-permute-start | bytes 491528 | tf_op jit(solution)/shard_map/ppermute | solution.py:320
  36.1 7.0 %collective-permute-start.12 = (bf16[64,2304]{1,0:T(8,128)(2,1)S(1)}, bf16[64,2304]{1,0:T(8,128)(2,1)S(1)}, u32[]{:S(2)}, u32[]{:S(2)}) collective-permute-start(bf16[64,2304]{1,0:T(8,128)(2,1)S(1)} %get-tuple-element.44.refs_0_), channel_id=1, source_target_pairs={{0,1},{1,0},{2,3},{3,2},{4,5},{5,4},{6,7},{7,6},{8,9},{9,8},{10,11... | collective-permute-start | bytes 884744 | tf_op jit(solution)/shard_map/ppermute | solution.py:320
  36.5 6.6 %collective-permute-start.13 = (bf16[64,2304]{1,0:T(8,128)(2,1)S(1)}, bf16[64,2304]{1,0:T(8,128)(2,1)S(1)}, u32[]{:S(2)}, u32[]{:S(2)}) collective-permute-start(bf16[64,2304]{1,0:T(8,128)(2,1)S(1)} %collective-permute-done.3.refs_1_), channel_id=1, source_target_pairs={{0,1},{1,0},{2,3},{3,2},{4,5},{5,4},{6,7},{7,6},{8,9},{9,8},{10,11... | collective-permute-start | bytes 884744 | tf_op jit(solution)/shard_map/ppermute | solution.py:320
  40.8 2.2 %collective-permute-start.14 = (bf16[64,2304]{1,0:T(8,128)(2,1)S(1)}, bf16[64,2304]{1,0:T(8,128)(2,1)S(1)}, u32[]{:S(2)}, u32[]{:S(2)}) collective-permute-start(bf16[64,2304]{1,0:T(8,128)(2,1)S(1)} %collective-permute-done.4.refs_2_), channel_id=1, source_target_pairs={{0,1},{1,0},{2,3},{3,2},{4,5},{5,4},{6,7},{7,6},{8,9},{9,8},{10,11... | collective-permute-start | bytes 884744 | tf_op jit(solution)/shard_map/ppermute | solution.py:320
  40.8 2.2 %collective-permute-start.15 = (bf16[64,2304]{1,0:T(8,128)(2,1)S(1)}, bf16[64,2304]{1,0:T(8,128)(2,1)S(1)}, u32[]{:S(2)}, u32[]{:S(2)}) collective-permute-start(bf16[64,2304]{1,0:T(8,128)(2,1)S(1)} %collective-permute-done.5.refs_3_), channel_id=1, source_target_pairs={{0,1},{1,0},{2,3},{3,2},{4,5},{5,4},{6,7},{7,6},{8,9},{9,8},{10,11... | collective-permute-start | bytes 884744 | tf_op jit(solution)/shard_map/ppermute | solution.py:320
  41.4 1.7 %collective-permute-start.19 = (bf16[64,1280]{1,0:T(8,128)(2,1)S(1)}, bf16[64,1280]{1,0:T(8,128)(2,1)S(1)}, u32[]{:S(2)}, u32[]{:S(2)}) collective-permute-start(bf16[64,1280]{1,0:T(8,128)(2,1)S(1)} %collective-permute-done.11.refs_7_), channel_id=1, source_target_pairs={{0,1},{1,0},{2,3},{3,2},{4,5},{5,4},{6,7},{7,6},{8,9},{9,8},{10,11... | collective-permute-start | bytes 491528 | tf_op jit(solution)/shard_map/ppermute | solution.py:320
  48.8 3.9 %collective-permute-start.20 = (bf16[256,2304]{1,0:T(8,128)(2,1)S(1)}, bf16[256,2304]{1,0:T(8,128)(2,1)S(1)}, u32[]{:S(2)}, u32[]{:S(2)}) collective-permute-start(bf16[256,2304]{1,0:T(8,128)(2,1)S(1)} %get-tuple-element.57), channel_id=1, source_target_pairs={{0,1},{1,0},{2,3},{3,2},{4,5},{5,4},{6,7},{7,6},{8,9},{9,8},{10,11... | collective-permute-start | bytes 3538952 | tf_op jit(solution)/shard_map/ppermute | solution.py:320
  49.0 3.6 %collective-permute-start.21 = (bf16[256,1280]{1,0:T(8,128)(2,1)S(1)}, bf16[256,1280]{1,0:T(8,128)(2,1)S(1)}, u32[]{:S(2)}, u32[]{:S(2)}) collective-permute-start(bf16[256,1280]{1,0:T(8,128)(2,1)S(1)} %get-tuple-element.58), channel_id=1, source_target_pairs={{0,1},{1,0},{2,3},{3,2},{4,5},{5,4},{6,7},{7,6},{8,9},{9,8},{10,11... | collective-permute-start | bytes 1966088 | tf_op jit(solution)/shard_map/ppermute | solution.py:320
  54.0 6.3 %collective-permute-start.28 = (bf16[64,1280]{1,0:T(8,128)(2,1)S(1)}, bf16[64,1280]{1,0:T(8,128)(2,1)S(1)}, u32[]{:S(2)}, u32[]{:S(2)}) collective-permute-start(bf16[64,1280]{1,0:T(8,128)(2,1)S(1)} %get-tuple-element.71), channel_id=1, source_target_pairs={{0,8},{1,9},{2,10},{3,11},{4,12},{5,13},{6,14},{7,15},{8,0},{9,1},... | collective-permute-start | bytes 491528 | tf_op jit(solution)/shard_map/ppermute | solution.py:320
  54.0 19.4 %collective-permute-start.22 = (bf16[64,2304]{1,0:T(8,128)(2,1)S(1)}, bf16[64,2304]{1,0:T(8,128)(2,1)S(1)}, u32[]{:S(2)}, u32[]{:S(2)}) collective-permute-start(bf16[64,2304]{1,0:T(8,128)(2,1)S(1)} %get-tuple-element.60), channel_id=1, source_target_pairs={{0,2},{1,3},{2,0},{3,1},{4,6},{5,7},{6,4},{7,5},{8,10},{9,11},{10,... | collective-permute-start | bytes 884744 | tf_op jit(solution)/shard_map/ppermute | solution.py:320
  54.9 18.6 %collective-permute-start.23 = (bf16[64,2304]{1,0:T(8,128)(2,1)S(1)}, bf16[64,2304]{1,0:T(8,128)(2,1)S(1)}, u32[]{:S(2)}, u32[]{:S(2)}) collective-permute-start(bf16[64,2304]{1,0:T(8,128)(2,1)S(1)} %get-tuple-element.61), channel_id=1, source_target_pairs={{0,4},{1,5},{2,6},{3,7},{4,0},{5,1},{6,2},{7,3},{8,12},{9,13},{10,... | collective-permute-start | bytes 884744 | tf_op jit(solution)/shard_map/ppermute | solution.py:320
  56.1 17.4 %collective-permute-start.24 = (bf16[64,2304]{1,0:T(8,128)(2,1)S(1)}, bf16[64,2304]{1,0:T(8,128)(2,1)S(1)}, u32[]{:S(2)}, u32[]{:S(2)}) collective-permute-start(bf16[64,2304]{1,0:T(8,128)(2,1)S(1)} %get-tuple-element.62), channel_id=1, source_target_pairs={{0,6},{1,7},{2,4},{3,5},{4,2},{5,3},{6,0},{7,1},{8,14},{9,15},{10,... | collective-permute-start | bytes 884744 | tf_op jit(solution)/shard_map/ppermute | solution.py:320
  57.6 14.6 %collective-permute-start.29 = (bf16[64,1280]{1,0:T(8,128)(2,1)S(1)}, bf16[64,1280]{1,0:T(8,128)(2,1)S(1)}, u32[]{:S(2)}, u32[]{:S(2)}) collective-permute-start(bf16[64,1280]{1,0:T(8,128)(2,1)S(1)} %get-tuple-element.72), channel_id=1, source_target_pairs={{0,16},{1,17},{2,18},{3,19},{4,20},{5,21},{6,22},{7,23},{8,24},{9,... | collective-permute-start | bytes 491528 | tf_op jit(solution)/shard_map/ppermute | solution.py:320
  60.3 11.9 %collective-permute-start.30 = (bf16[64,1280]{1,0:T(8,128)(2,1)S(1)}, bf16[64,1280]{1,0:T(8,128)(2,1)S(1)}, u32[]{:S(2)}, u32[]{:S(2)}) collective-permute-start(bf16[64,1280]{1,0:T(8,128)(2,1)S(1)} %get-tuple-element.73), channel_id=1, source_target_pairs={{0,24},{1,25},{2,26},{3,27},{4,28},{5,29},{6,30},{7,31},{8,16},{9,... | collective-permute-start | bytes 491528 | tf_op jit(solution)/shard_map/ppermute | solution.py:320
  72.6 8.1 %collective-permute-start.31 = (bf16[32,1280]{1,0:T(8,128)(2,1)S(1)}, bf16[32,1280]{1,0:T(8,128)(2,1)S(1)}, u32[]{:S(2)}, u32[]{:S(2)}) collective-permute-start(bf16[32,1280]{1,0:T(8,128)(2,1)S(1)} %get-tuple-element.78), channel_id=1, source_target_pairs={{0,2},{1,3},{2,0},{3,1},{4,6},{5,7},{6,4},{7,5},{8,10},{9,11},{10,... | collective-permute-start | bytes 245768 | tf_op jit(solution)/shard_map/ppermute | solution.py:320
  74.1 11.9 %collective-permute-start.25 = (bf16[32,2304]{1,0:T(8,128)(2,1)S(1)}, bf16[32,2304]{1,0:T(8,128)(2,1)S(1)}, u32[]{:S(2)}, u32[]{:S(2)}) collective-permute-start(bf16[32,2304]{1,0:T(8,128)(2,1)S(1)} %get-tuple-element.67), channel_id=1, source_target_pairs={{0,8},{1,9},{2,10},{3,11},{4,12},{5,13},{6,14},{7,15},{8,0},{9,1},... | collective-permute-start | bytes 442376 | tf_op jit(solution)/shard_map/ppermute | solution.py:320
  77.0 12.6 %collective-permute-start.26 = (bf16[32,2304]{1,0:T(8,128)(2,1)S(1)}, bf16[32,2304]{1,0:T(8,128)(2,1)S(1)}, u32[]{:S(2)}, u32[]{:S(2)}) collective-permute-start(bf16[32,2304]{1,0:T(8,128)(2,1)S(1)} %get-tuple-element.68), channel_id=1, source_target_pairs={{0,16},{1,17},{2,18},{3,19},{4,20},{5,21},{6,22},{7,23},{8,24},{9,... | collective-permute-start | bytes 442376 | tf_op jit(solution)/shard_map/ppermute | solution.py:320
  77.5 12.1 %collective-permute-start.27 = (bf16[32,2304]{1,0:T(8,128)(2,1)S(1)}, bf16[32,2304]{1,0:T(8,128)(2,1)S(1)}, u32[]{:S(2)}, u32[]{:S(2)}) collective-permute-start(bf16[32,2304]{1,0:T(8,128)(2,1)S(1)} %get-tuple-element.69), channel_id=1, source_target_pairs={{0,24},{1,25},{2,26},{3,27},{4,28},{5,29},{6,30},{7,31},{8,16},{9,... | collective-permute-start | bytes 442376 | tf_op jit(solution)/shard_map/ppermute | solution.py:320
  79.4 4.4 %collective-permute-start.32 = (bf16[32,1280]{1,0:T(8,128)(2,1)S(1)}, bf16[32,1280]{1,0:T(8,128)(2,1)S(1)}, u32[]{:S(2)}, u32[]{:S(2)}) collective-permute-start(bf16[32,1280]{1,0:T(8,128)(2,1)S(1)} %get-tuple-element.79), channel_id=1, source_target_pairs={{0,4},{1,5},{2,6},{3,7},{4,0},{5,1},{6,2},{7,3},{8,12},{9,13},{10,... | collective-permute-start | bytes 245768 | tf_op jit(solution)/shard_map/ppermute | solution.py:320
  80.7 5.3 %collective-permute-start.33 = (bf16[32,1280]{1,0:T(8,128)(2,1)S(1)}, bf16[32,1280]{1,0:T(8,128)(2,1)S(1)}, u32[]{:S(2)}, u32[]{:S(2)}) collective-permute-start(bf16[32,1280]{1,0:T(8,128)(2,1)S(1)} %get-tuple-element.80), channel_id=1, source_target_pairs={{0,6},{1,7},{2,4},{3,5},{4,2},{5,3},{6,0},{7,1},{8,14},{9,15},{10,... | collective-permute-start | bytes 245768 | tf_op jit(solution)/shard_map/ppermute | solution.py:320

commit v4 on v3

--- a/solution.py
+++ b/solution.py
@@ -14,11 +14,11 @@
 CHUNK = 768
 VMEM_LIMIT = 24 << 20
 LOAD_LIMIT = 41 << 20
-HEAD_LIMIT = 60 << 20
+HEAD_LIMIT = 54 << 20
 GROUPS = 1
 
 
-def call(kernel, out_shapes, *operands, flops=0, scalars=0):
+def call(kernel, out_shapes, *operands, flops=0, scalars=0, scale=1.0):
     moved = sum(o.size * o.dtype.itemsize for o in operands)
     moved += sum(o.size * o.dtype.itemsize for o in out_shapes)
     vmem = pl.BlockSpec(memory_space=pltpu.VMEM)
@@ -29,7 +29,7 @@
         in_specs=[smem] * scalars + [vmem] * (len(operands) - scalars),
         out_specs=[vmem] * len(out_shapes),
         compiler_params=pltpu.CompilerParams(vmem_limit_bytes=VMEM_LIMIT),
-        cost_estimate=pl.CostEstimate(flops=flops, bytes_accessed=moved, transcendentals=0),
+        cost_estimate=pl.CostEstimate(flops=int(flops * scale), bytes_accessed=int(moved * scale), transcendentals=0),
     )(*operands)
 
 
@@ -332,22 +332,22 @@
     plane = over_planes([tagged_second] * planes)
     group = blocks // GROUPS
 
-    def pick(arrays, targets, ids, columns):
+    def pick(arrays, targets, ids, columns, scale):
         sources = len(arrays)
         out = call(
             functools.partial(pick_kernel, experts, cap, sources, targets),
             shaped(targets, (sources * cap, columns)) + shaped(3, (sources * rows, targets * sources * cap)),
             ids.reshape(1, targets), *arrays,
-            flops=2 * targets * sources * cap * sources * rows * columns, scalars=1,
+            flops=2 * targets * sources * cap * sources * rows * columns, scalars=1, scale=scale,
         )
         return out[:targets], out[targets:]
 
     first, first_factors = [], []
     for g in range(GROUPS):
-        pieces, factors = pick(column[g * group : (g + 1) * group], planes, plane_ids, split)
+        pieces, factors = pick(column[g * group : (g + 1) * group], planes, plane_ids, split, 1)
         first.append(over_planes(pieces))
         first_factors.append(factors)
-    second, second_factors = pick(plane, blocks, block_ids, rest)
+    second, second_factors = pick(plane, blocks, block_ids, rest, 0.01)
     second = over_blocks(second)
     first = [first[g][j] for j in range(planes) for g in range(GROUPS)]
     first_other = [swap(piece, 1) for piece in first]
@@ -361,7 +361,7 @@
             functools.partial(hidden_kernel, *sizes),
             shaped(1, (slots, hidden_width)),
             *first, *second, gate_weight, up_weight,
-            flops=4 * slots * width * hidden_width,
+            flops=4 * slots * width * hidden_width, scale=1,
         )[0]
 
     hidden_other, gate_weight, up_weight, down_weight = load_hidden(
@@ -372,30 +372,31 @@
         functools.partial(down_kernel, *sizes),
         shaped(1, (slots, split)) + shaped(1, (slots, rest)),
         hidden_other, down_weight,
-        flops=2 * slots * width * hidden_width,
+        flops=2 * slots * width * hidden_width, scale=1,
     )
     results = call(
         functools.partial(add_down_kernel, *sizes),
         shaped(planes * GROUPS, (group * cap, split)) + shaped(blocks, (planes * cap, rest)),
         hidden_mine, down_weight, swap(parts[0], 1), swap(parts[1], 1),
-        flops=2 * slots * width * hidden_width,
+        flops=2 * slots * width * hidden_width, scale=1,
     )
-    def combine(arrays, factors, sources, columns, own):
+    def combine(arrays, factors, sources, columns, own, scale):
         return call(
             functools.partial(combine_kernel, sources, len(arrays)),
             shaped(own, (rows, columns), F32) + shaped(sources - own, (rows, columns)),
             *arrays, *factors,
             flops=6 * arrays[0].shape[0] * len(arrays) * sources * rows * columns,
+            scale=scale,
         )
 
     first = []
     for g in reversed(range(GROUPS)):
         returned = over_planes(results[g : planes * GROUPS : GROUPS])
-        first = list(combine(returned, first_factors[g], group, split, int(g == 0))) + first
+        first = list(combine(returned, first_factors[g], group, split, int(g == 0), 0.01)) + first
     first = over_blocks(first)
     second = over_blocks(results[planes * GROUPS :])
-    second = over_planes(combine(second, second_factors, planes, rest, 1))
-    return call(final_kernel, shaped(1, (rows, width)), *first, *second)[0]
+    second = over_planes(combine(second, second_factors, planes, rest, 1, 10))
+    return call(final_kernel, shaped(1, (rows, width)), *first, *second, scale=1)[0]
 
 
 def solution(mesh):

time: 90.6 us -> 87.9 us (0.970)
  starting transfers between devices: 38.5 us -> 35.8 us
    ppermute x34, starting transfers between devices: 38.5 us -> 35.8 us  [swap(): return lax.ppermute(array, 'ep', [(i, i ^ mask) for i in range(devices)])]
  transfers between devices with their start and end apart: 34 -> 34, of which waited for: 12 -> 16; matrix products, arithmetic and copies ran while one was open for 0% -> 0% of each run, Pallas kernels for 7% -> 7%
where the time goes in v4:
time: 87.9 us; the launch traced here: 87.7 us
  starting transfers between devices  35.8 us (41%)
  waiting for transfers between devices  34.6 us (39%)
  Pallas kernels  15.4 us (18%)
  local copies, waits for them, and re-layouts  1.8 us (2%)
    ppermute x34, starting transfers between devices, swap(): return lax.ppermute(array, 'ep', [(i, i ^ mask) for i in range(devices)])  35.8 us
    ppermute x34, waiting for transfers between devices, swap(): return lax.ppermute(array, 'ep', [(i, i ^ mask) for i in range(devices)])  34.6 us
    pallas_call x8, Pallas kernels, call(): pl.pallas_call(kernel, out_shape=out_shapes, in_specs=[smem] * scalars +...  9.29 us
    pallas_call x1, Pallas kernels, load_hidden(): pl.pallas_call(functools.partial(load_hidden_kernel, *sizes), out_shape=s...  4.38 us
    unnamed x4, local copies, waits for them, and re-layouts  1.8 us
  transfers between devices with their start and end apart: 34, of which 16 were waited for; matrix products, arithmetic and copies ran while one was open for 0% of the time, Pallas kernels for 7%

profile of v4, /device:TPU:0, one launch (start us, length us, event | category | flops | bytes accessed | tf_op | source)
XLA Modules:
  0.0 87.7 jit_solution(11801817110121990527)
XLA Ops:
  0.0 1.7 %shard_map.64 = (bf16[32,2432]{1,0:T(8,128)(2,1)}, bf16[32,1408]{1,0:T(8,128)(2,1)}) custom-call(bf16[32,3584]{1,0:T(8,128)(2,1)} %x_hbm.1, s32[8,32]{1,0:T(8,128)} %bitcast.2, f32[8,32]{1,0:T(8,128)} %bitcast.3), custom_call_target="tpu_custom_call" | custom-call | bytes 458752 | tf_op jit(solution)/shard_map/pallas_call | solution.py:99
  1.7 4.0 %collective-permute-start.8 = (bf16[32,1408]{1,0:T(8,128)(2,1)}, bf16[32,1408]{1,0:T(8,128)(2,1)S(1)}, u32[]{:S(2)}, u32[]{:S(2)}) collective-permute-start(bf16[32,1408]{1,0:T(8,128)(2,1)} %get-tuple-element.48.refs_0_), channel_id=1, source_target_pairs={{0,6},{1,7},{2,4},{3,5},{4,2},{5,3},{6,0},{7,1},{8,14},{9,15},{10,... | collective-permute-start | bytes 270344 | tf_op jit(solution)/shard_map/ppermute | solution.py:320
  5.7 3.6 %collective-permute-start.2 = (bf16[32,2432]{1,0:T(8,128)(2,1)}, bf16[32,2432]{1,0:T(8,128)(2,1)S(1)}, u32[]{:S(2)}, u32[]{:S(2)}) collective-permute-start(bf16[32,2432]{1,0:T(8,128)(2,1)} %get-tuple-element.43.refs_0_), channel_id=1, source_target_pairs={{0,24},{1,25},{2,26},{3,27},{4,28},{5,29},{6,30},{7,31},{8,16},{9,... | collective-permute-start | bytes 466952 | tf_op jit(solution)/shard_map/ppermute | solution.py:320
  9.3 0.5 collective-permute-start.7
  9.8 0.5 collective-permute-start.6
  10.3 0.6 collective-permute-start
  10.9 3.1 %collective-permute-done.7.refs_2_ = bf16[32,1408]{1,0:T(8,128)(2,1)S(1)} collective-permute-done((bf16[32,1408]{1,0:T(8,128)(2,1)}, bf16[32,1408]{1,0:T(8,128)(2,1)S(1)}, u32[]{:S(2)}, u32[]{:S(2)}) %collective-permute-start.7) | collective-permute-done | bytes 90144 | tf_op jit(solution)/shard_map/ppermute | solution.py:320
  14.0 0.5 collective-permute-done.6.refs_1_
  14.5 0.9 %copy-done.1 = bf16[32,1408]{1,0:T(8,128)(2,1)S(1)} copy-done((bf16[32,1408]{1,0:T(8,128)(2,1)S(1)}, bf16[32,1408]{1,0:T(8,128)(2,1)}, u32[]{:S(2)}) %copy-start.1) | copy-done | bytes 90136
  15.4 1.2 %shard_map.66 = (bf16[64,1280]{1,0:T(8,128)(2,1)S(1)}, bf16[64,1280]{1,0:T(8,128)(2,1)S(1)}, bf16[64,1280]{1,0:T(8,128)(2,1)S(1)}, bf16[64,1280]{1,0:T(8,128)(2,...) custom-call(s32[1,4]{1,0:T(1,128)S(1)} %multiply_add_fusion.e_ref, ...), custom_call_target="tpu_custom_call" | custom-call | flops 838860 | bytes 12124 | tf_op jit(solution)/shard_map/pallas_call | solution.py:26
  16.7 0.8 collective-permute-start.10
  17.5 3.6 %collective-permute-start.11 = (bf16[64,1280]{1,0:T(8,128)(2,1)S(1)}, bf16[64,1280]{1,0:T(8,128)(2,1)S(1)}, u32[]{:S(2)}, u32[]{:S(2)}) collective-permute-start(bf16[64,1280]{1,0:T(8,128)(2,1)S(1)} %get-tuple-element.52), channel_id=1, source_target_pairs={{0,24},{1,25},{2,26},{3,27},{4,28},{5,29},{6,30},{7,31},{8,16},{9,... | collective-permute-start | bytes 491528 | tf_op jit(solution)/shard_map/ppermute | solution.py:320
  21.1 3.6 %collective-permute-done.1.refs_2_ = bf16[32,2432]{1,0:T(8,128)(2,1)S(1)} collective-permute-done((bf16[32,2432]{1,0:T(8,128)(2,1)}, bf16[32,2432]{1,0:T(8,128)(2,1)S(1)}, u32[]{:S(2)}, u32[]{:S(2)}) %collective-permute-start.1) | collective-permute-done | bytes 155680 | tf_op jit(solution)/shard_map/ppermute | solution.py:320
  24.8 0.9 %copy-done = bf16[32,2432]{1,0:T(8,128)(2,1)S(1)} copy-done((bf16[32,2432]{1,0:T(8,128)(2,1)S(1)}, bf16[32,2432]{1,0:T(8,128)(2,1)}, u32[]{:S(2)}) %copy-start) | copy-done | bytes 155672
  25.7 1.4 %shard_map.65 = (bf16[64,2304]{1,0:T(8,128)(2,1)S(1)}, bf16[64,2304]{1,0:T(8,128)(2,1)S(1)}, bf16[64,2304]{1,0:T(8,128)(2,1)S(1)}, bf16[64,2304]{1,0:T(8,128)(2,...) custom-call(s32[1,4]{1,0:T(1,128)S(1)} %xor_add_fusion.e_ref, ...), custom_call_target="tpu_custom_call" | custom-call | flops 150994944 | bytes 1998864 | tf_op jit(solution)/shard_map/pallas_call | solution.py:26
  27.0 1.0 %collective-permute-start.3 = (bf16[64,2304]{1,0:T(8,128)(2,1)S(1)}, bf16[64,2304]{1,0:T(8,128)(2,1)S(1)}, u32[]{:S(2)}, u32[]{:S(2)}) collective-permute-start(bf16[64,2304]{1,0:T(8,128)(2,1)S(1)} %get-tuple-element.45), channel_id=1, source_target_pairs={{0,2},{1,3},{2,0},{3,1},{4,6},{5,7},{6,4},{7,5},{8,10},{9,11},{10,... | collective-permute-start | bytes 884744 | tf_op jit(solution)/shard_map/ppermute | solution.py:320
  28.1 2.5 %collective-permute-start.5 = (bf16[64,2304]{1,0:T(8,128)(2,1)S(1)}, bf16[64,2304]{1,0:T(8,128)(2,1)S(1)}, u32[]{:S(2)}, u32[]{:S(2)}) collective-permute-start(bf16[64,2304]{1,0:T(8,128)(2,1)S(1)} %get-tuple-element.47), channel_id=1, source_target_pairs={{0,6},{1,7},{2,4},{3,5},{4,2},{5,3},{6,0},{7,1},{8,14},{9,15},{10,... | collective-permute-start | bytes 884744 | tf_op jit(solution)/shard_map/ppermute | solution.py:320
  30.6 3.4 %collective-permute-done.10.refs_6_ = bf16[64,1280]{1,0:T(8,128)(2,1)S(1)} collective-permute-done((bf16[64,1280]{1,0:T(8,128)(2,1)S(1)}, bf16[64,1280]{1,0:T(8,128)(2,1)S(1)}, u32[]{:S(2)}, u32[]{:S(2)}) %collective-permute-start.10) | collective-permute-done | bytes 163872 | tf_op jit(solution)/shard_map/ppermute | solution.py:320
  34.0 0.5 collective-permute-start.17
  34.5 0.9 %collective-permute-done.16.refs_4_ = bf16[64,1280]{1,0:T(8,128)(2,1)S(1)} collective-permute-done((bf16[64,1280]{1,0:T(8,128)(2,1)S(1)}, bf16[64,1280]{1,0:T(8,128)(2,1)S(1)}, u32[]{:S(2)}, u32[]{:S(2)}) %collective-permute-start.16) | collective-permute-done | bytes 163872 | tf_op jit(solution)/shard_map/ppermute | solution.py:320
  36.1 3.3 %collective-permute-done.4.refs_2_ = bf16[64,2304]{1,0:T(8,128)(2,1)S(1)} collective-permute-done((bf16[64,2304]{1,0:T(8,128)(2,1)S(1)}, bf16[64,2304]{1,0:T(8,128)(2,1)S(1)}, u32[]{:S(2)}, u32[]{:S(2)}) %collective-permute-start.4) | collective-permute-done | bytes 294944 | tf_op jit(solution)/shard_map/ppermute | solution.py:320
  39.4 0.5 collective-permute-start.15
  40.0 1.6 %collective-permute-done.19.refs_7_ = bf16[64,1280]{1,0:T(8,128)(2,1)S(1)} collective-permute-done((bf16[64,1280]{1,0:T(8,128)(2,1)S(1)}, bf16[64,1280]{1,0:T(8,128)(2,1)S(1)}, u32[]{:S(2)}, u32[]{:S(2)}) %collective-permute-start.19) | collective-permute-done | bytes 163872 | tf_op jit(solution)/shard_map/ppermute | solution.py:320
  41.6 4.4 %shard_map.67 = (bf16[256,512]{1,0:T(8,128)(2,1)S(1)}, bf16[1,3584,512]{2,1,0:T(8,128)(2,1)S(1)}, bf16[1,3584,512]{2,1,0:T(8,128)(2,1)S(1)}, bf16[1,512,3584]{2,1,0:T(8,128)(2,1)S(1)}) custom-call(bf16[64,2304]{1,0:T(8,128)(2,1)S(1)} %collective-permute-done.12.refs_0_, bf16[64,2304]{1,0:T(8,128)(2,1)S(1)} %collective-permute-done.13.refs_1_, ...), custom_call_target="tpu_custom_call" | custom-call | flops 1879048192 | bytes 11010048 | tf_op jit(solution)/shard_map/pallas_call | solution.py:255
  46.0 1.3 %shard_map.69 = (bf16[256,2304]{1,0:T(8,128)(2,1)S(1)}, bf16[256,1280]{1,0:T(8,128)(2,1)S(1)}) custom-call(bf16[256,512]{1,0:T(8,128)(2,1)S(1)} %get-tuple-element.56.hidden_ref, bf16[1,512,3584]{2,1,0:T(8,128)(2,1)S(1)} %get-tuple-element.55.down_ref), custom_call_target="tpu_custom_call" | custom-call | flops 939524096 | bytes 5767168 | tf_op jit(solution)/shard_map/pallas_call | solution.py:26
  47.6 0.4 collective-permute-start.21
  47.9 2.2 %shard_map.68.hidden_ref = bf16[256,512]{1,0:T(8,128)(2,1)S(1)} custom-call(bf16[64,2304]{1,0:T(8,128)(2,1)S(1)} %get-tuple-element.44.refs_0_, bf16[64,2304]{1,0:T(8,128)(2,1)S(1)} %collective-permute-done.3.refs_1_, bf16[64,2304]{1,0:T(8,128)(2,1)S(1)} %collective-permute-done.4.refs_2_, bf16[64,2304]{1,0:T(8,128)(2,1)S(1)} %collective-permute-done.5.refs_3_, ...), custom_call_target="tpu_custom_call" | custom-call | flops 1879048192 | bytes 9437184 | tf_op jit(solution)/shard_map/pallas_call | solution.py:26
  50.2 1.0 %collective-permute-done.21.second_ref = bf16[256,1280]{1,0:T(8,128)(2,1)S(1)} collective-permute-done((bf16[256,1280]{1,0:T(8,128)(2,1)S(1)}, bf16[256,1280]{1,0:T(8,128)(2,1)S(1)}, u32[]{:S(2)}, u32[]{:S(2)}) %collective-permute-start.21) | collective-permute-done | bytes 655392 | tf_op jit(solution)/shard_map/ppermute | solution.py:320
  51.2 1.3 %shard_map.70 = (bf16[64,2304]{1,0:T(8,128)(2,1)S(1)}, bf16[64,2304]{1,0:T(8,128)(2,1)S(1)}, bf16[64,2304]{1,0:T(8,128)(2,1)S(1)}, bf16[64,2304]{1,0:T(8,128)(2,...) custom-call(bf16[256,512]{1,0:T(8,128)(2,1)S(1)} %shard_map.68.hidde, ...), custom_call_target="tpu_custom_call" | custom-call | flops 939524096 | bytes 7602176 | tf_op jit(solution)/shard_map/pallas_call | solution.py:26
  52.6 3.1 %collective-permute-start.29 = (bf16[64,1280]{1,0:T(8,128)(2,1)S(1)}, bf16[64,1280]{1,0:T(8,128)(2,1)S(1)}, u32[]{:S(2)}, u32[]{:S(2)}) collective-permute-start(bf16[64,1280]{1,0:T(8,128)(2,1)S(1)} %get-tuple-element.72), channel_id=1, source_target_pairs={{0,16},{1,17},{2,18},{3,19},{4,20},{5,21},{6,22},{7,23},{8,24},{9,... | collective-permute-start | bytes 491528 | tf_op jit(solution)/shard_map/ppermute | solution.py:320
  55.7 1.3 %collective-permute-start.30 = (bf16[64,1280]{1,0:T(8,128)(2,1)S(1)}, bf16[64,1280]{1,0:T(8,128)(2,1)S(1)}, u32[]{:S(2)}, u32[]{:S(2)}) collective-permute-start(bf16[64,1280]{1,0:T(8,128)(2,1)S(1)} %get-tuple-element.73), channel_id=1, source_target_pairs={{0,24},{1,25},{2,26},{3,27},{4,28},{5,29},{6,30},{7,31},{8,16},{9,... | collective-permute-start | bytes 491528 | tf_op jit(solution)/shard_map/ppermute | solution.py:320
  57.0 1.5 %collective-permute-start.22 = (bf16[64,2304]{1,0:T(8,128)(2,1)S(1)}, bf16[64,2304]{1,0:T(8,128)(2,1)S(1)}, u32[]{:S(2)}, u32[]{:S(2)}) collective-permute-start(bf16[64,2304]{1,0:T(8,128)(2,1)S(1)} %get-tuple-element.60), channel_id=1, source_target_pairs={{0,2},{1,3},{2,0},{3,1},{4,6},{5,7},{6,4},{7,5},{8,10},{9,11},{10,... | collective-permute-start | bytes 884744 | tf_op jit(solution)/shard_map/ppermute | solution.py:320
  58.5 0.6 collective-permute-start.23
  59.0 2.8 %collective-permute-done.28.refs_1_ = bf16[64,1280]{1,0:T(8,128)(2,1)S(1)} collective-permute-done((bf16[64,1280]{1,0:T(8,128)(2,1)S(1)}, bf16[64,1280]{1,0:T(8,128)(2,1)S(1)}, u32[]{:S(2)}, u32[]{:S(2)}) %collective-permute-start.28) | collective-permute-done | bytes 163872 | tf_op jit(solution)/shard_map/ppermute | solution.py:320
  61.8 1.3 %collective-permute-start.24 = (bf16[64,2304]{1,0:T(8,128)(2,1)S(1)}, bf16[64,2304]{1,0:T(8,128)(2,1)S(1)}, u32[]{:S(2)}, u32[]{:S(2)}) collective-permute-start(bf16[64,2304]{1,0:T(8,128)(2,1)S(1)} %get-tuple-element.62), channel_id=1, source_target_pairs={{0,6},{1,7},{2,4},{3,5},{4,2},{5,3},{6,0},{7,1},{8,14},{9,15},{10,... | collective-permute-start | bytes 884744 | tf_op jit(solution)/shard_map/ppermute | solution.py:320
  63.1 4.6 %collective-permute-done.29.refs_2_ = bf16[64,1280]{1,0:T(8,128)(2,1)S(1)} collective-permute-done((bf16[64,1280]{1,0:T(8,128)(2,1)S(1)}, bf16[64,1280]{1,0:T(8,128)(2,1)S(1)}, u32[]{:S(2)}, u32[]{:S(2)}) %collective-permute-start.29) | collective-permute-done | bytes 163872 | tf_op jit(solution)/shard_map/ppermute | solution.py:320
  67.7 0.4 shard_map.72
  68.2 1.5 %collective-permute-start.31 = (bf16[32,1280]{1,0:T(8,128)(2,1)S(1)}, bf16[32,1280]{1,0:T(8,128)(2,1)S(1)}, u32[]{:S(2)}, u32[]{:S(2)}) collective-permute-start(bf16[32,1280]{1,0:T(8,128)(2,1)S(1)} %get-tuple-element.78), channel_id=1, source_target_pairs={{0,2},{1,3},{2,0},{3,1},{4,6},{5,7},{6,4},{7,5},{8,10},{9,11},{10,... | collective-permute-start | bytes 245768 | tf_op jit(solution)/shard_map/ppermute | solution.py:320
  69.7 3.0 %collective-permute-done.23.refs_2_ = bf16[64,2304]{1,0:T(8,128)(2,1)S(1)} collective-permute-done((bf16[64,2304]{1,0:T(8,128)(2,1)S(1)}, bf16[64,2304]{1,0:T(8,128)(2,1)S(1)}, u32[]{:S(2)}, u32[]{:S(2)}) %collective-permute-start.23) | collective-permute-done | bytes 294944 | tf_op jit(solution)/shard_map/ppermute | solution.py:320
  72.7 0.6 shard_map.71
  73.7 2.5 %collective-permute-start.26 = (bf16[32,2304]{1,0:T(8,128)(2,1)S(1)}, bf16[32,2304]{1,0:T(8,128)(2,1)S(1)}, u32[]{:S(2)}, u32[]{:S(2)}) collective-permute-start(bf16[32,2304]{1,0:T(8,128)(2,1)S(1)} %get-tuple-element.68), channel_id=1, source_target_pairs={{0,16},{1,17},{2,18},{3,19},{4,20},{5,21},{6,22},{7,23},{8,24},{9,... | collective-permute-start | bytes 442376 | tf_op jit(solution)/shard_map/ppermute | solution.py:320
  76.2 1.6 %collective-permute-start.27 = (bf16[32,2304]{1,0:T(8,128)(2,1)S(1)}, bf16[32,2304]{1,0:T(8,128)(2,1)S(1)}, u32[]{:S(2)}, u32[]{:S(2)}) collective-permute-start(bf16[32,2304]{1,0:T(8,128)(2,1)S(1)} %get-tuple-element.69), channel_id=1, source_target_pairs={{0,24},{1,25},{2,26},{3,27},{4,28},{5,29},{6,30},{7,31},{8,16},{9,... | collective-permute-start | bytes 442376 | tf_op jit(solution)/shard_map/ppermute | solution.py:320
  77.8 1.2 %collective-permute-start.32 = (bf16[32,1280]{1,0:T(8,128)(2,1)S(1)}, bf16[32,1280]{1,0:T(8,128)(2,1)S(1)}, u32[]{:S(2)}, u32[]{:S(2)}) collective-permute-start(bf16[32,1280]{1,0:T(8,128)(2,1)S(1)} %get-tuple-element.79), channel_id=1, source_target_pairs={{0,4},{1,5},{2,6},{3,7},{4,0},{5,1},{6,2},{7,3},{8,12},{9,13},{10,... | collective-permute-start | bytes 245768 | tf_op jit(solution)/shard_map/ppermute | solution.py:320
  79.0 1.5 %collective-permute-start.33 = (bf16[32,1280]{1,0:T(8,128)(2,1)S(1)}, bf16[32,1280]{1,0:T(8,128)(2,1)S(1)}, u32[]{:S(2)}, u32[]{:S(2)}) collective-permute-start(bf16[32,1280]{1,0:T(8,128)(2,1)S(1)} %get-tuple-element.80), channel_id=1, source_target_pairs={{0,6},{1,7},{2,4},{3,5},{4,2},{5,3},{6,0},{7,1},{8,14},{9,15},{10,... | collective-permute-start | bytes 245768 | tf_op jit(solution)/shard_map/ppermute | solution.py:320
  80.5 1.8 %collective-permute-done.32.refs_6_ = bf16[32,1280]{1,0:T(8,128)(2,1)S(1)} collective-permute-done((bf16[32,1280]{1,0:T(8,128)(2,1)S(1)}, bf16[32,1280]{1,0:T(8,128)(2,1)S(1)}, u32[]{:S(2)}, u32[]{:S(2)}) %collective-permute-start.32) | collective-permute-done | bytes 81952 | tf_op jit(solution)/shard_map/ppermute | solution.py:320
  82.2 2.1 %collective-permute-done.33.refs_7_ = bf16[32,1280]{1,0:T(8,128)(2,1)S(1)} collective-permute-done((bf16[32,1280]{1,0:T(8,128)(2,1)S(1)}, bf16[32,1280]{1,0:T(8,128)(2,1)S(1)}, u32[]{:S(2)}, u32[]{:S(2)}) %collective-permute-start.33) | collective-permute-done | bytes 81952 | tf_op jit(solution)/shard_map/ppermute | solution.py:320
  84.3 2.6 %collective-permute-done.26.refs_2_ = bf16[32,2304]{1,0:T(8,128)(2,1)S(1)} collective-permute-done((bf16[32,2304]{1,0:T(8,128)(2,1)S(1)}, bf16[32,2304]{1,0:T(8,128)(2,1)S(1)}, u32[]{:S(2)}, u32[]{:S(2)}) %collective-permute-start.26) | collective-permute-done | bytes 147488 | tf_op jit(solution)/shard_map/ppermute | solution.py:320
  86.9 0.8 shard_map.73
  (36 shorter events, 1.6 us)
Async XLA Ops:
  1.7 8.6 %collective-permute-start.8 = (bf16[32,1408]{1,0:T(8,128)(2,1)}, bf16[32,1408]{1,0:T(8,128)(2,1)S(1)}, u32[]{:S(2)}, u32[]{:S(2)}) collective-permute-start(bf16[32,1408]{1,0:T(8,128)(2,1)} %get-tuple-element.48.refs_0_), channel_id=1, source_target_pairs={{0,6},{1,7},{2,4},{3,5},{4,2},{5,3},{6,0},{7,1},{8,14},{9,15},{10,... | collective-permute-start | bytes 270344 | tf_op jit(solution)/shard_map/ppermute | solution.py:320
  5.7 11.8 %collective-permute-start.2 = (bf16[32,2432]{1,0:T(8,128)(2,1)}, bf16[32,2432]{1,0:T(8,128)(2,1)S(1)}, u32[]{:S(2)}, u32[]{:S(2)}) collective-permute-start(bf16[32,2432]{1,0:T(8,128)(2,1)} %get-tuple-element.43.refs_0_), channel_id=1, source_target_pairs={{0,24},{1,25},{2,26},{3,27},{4,28},{5,29},{6,30},{7,31},{8,16},{9,... | collective-permute-start | bytes 466952 | tf_op jit(solution)/shard_map/ppermute | solution.py:320
  9.3 4.7 %collective-permute-start.7 = (bf16[32,1408]{1,0:T(8,128)(2,1)}, bf16[32,1408]{1,0:T(8,128)(2,1)S(1)}, u32[]{:S(2)}, u32[]{:S(2)}) collective-permute-start(bf16[32,1408]{1,0:T(8,128)(2,1)} %get-tuple-element.48.refs_0_), channel_id=1, source_target_pairs={{0,4},{1,5},{2,6},{3,7},{4,0},{5,1},{6,2},{7,3},{8,12},{9,13},{10,... | collective-permute-start | bytes 270344 | tf_op jit(solution)/shard_map/ppermute | solution.py:320
  9.8 4.7 %collective-permute-start.6 = (bf16[32,1408]{1,0:T(8,128)(2,1)}, bf16[32,1408]{1,0:T(8,128)(2,1)S(1)}, u32[]{:S(2)}, u32[]{:S(2)}) collective-permute-start(bf16[32,1408]{1,0:T(8,128)(2,1)} %get-tuple-element.48.refs_0_), channel_id=1, source_target_pairs={{0,2},{1,3},{2,0},{3,1},{4,6},{5,7},{6,4},{7,5},{8,10},{9,11},{10,... | collective-permute-start | bytes 270344 | tf_op jit(solution)/shard_map/ppermute | solution.py:320
  10.3 14.4 %collective-permute-start.1 = (bf16[32,2432]{1,0:T(8,128)(2,1)}, bf16[32,2432]{1,0:T(8,128)(2,1)S(1)}, u32[]{:S(2)}, u32[]{:S(2)}) collective-permute-start(bf16[32,2432]{1,0:T(8,128)(2,1)} %get-tuple-element.43.refs_0_), channel_id=1, source_target_pairs={{0,16},{1,17},{2,18},{3,19},{4,20},{5,21},{6,22},{7,23},{8,24},{9,... | collective-permute-start | bytes 466952 | tf_op jit(solution)/shard_map/ppermute | solution.py:320
  10.3 14.4 %collective-permute-start = (bf16[32,2432]{1,0:T(8,128)(2,1)}, bf16[32,2432]{1,0:T(8,128)(2,1)S(1)}, u32[]{:S(2)}, u32[]{:S(2)}) collective-permute-start(bf16[32,2432]{1,0:T(8,128)(2,1)} %get-tuple-element.43.refs_0_), channel_id=1, source_target_pairs={{0,8},{1,9},{2,10},{3,11},{4,12},{5,13},{6,14},{7,15},{8,0},{9,1},... | collective-permute-start | bytes 466952 | tf_op jit(solution)/shard_map/ppermute | solution.py:320
  14.5 0.9 %copy-start.1 = (bf16[32,1408]{1,0:T(8,128)(2,1)S(1)}, bf16[32,1408]{1,0:T(8,128)(2,1)}, u32[]{:S(2)}) copy-start(bf16[32,1408]{1,0:T(8,128)(2,1)} %get-tuple-element.48.refs_0_) | copy-start | bytes 270340
  16.6 11.5 %collective-permute-start.9 = (bf16[64,1280]{1,0:T(8,128)(2,1)S(1)}, bf16[64,1280]{1,0:T(8,128)(2,1)S(1)}, u32[]{:S(2)}, u32[]{:S(2)}) collective-permute-start(bf16[64,1280]{1,0:T(8,128)(2,1)S(1)} %get-tuple-element.50), channel_id=1, source_target_pairs={{0,8},{1,9},{2,10},{3,11},{4,12},{5,13},{6,14},{7,15},{8,0},{9,1},... | collective-permute-start | bytes 491528 | tf_op jit(solution)/shard_map/ppermute | solution.py:320
  16.7 17.2 %collective-permute-start.10 = (bf16[64,1280]{1,0:T(8,128)(2,1)S(1)}, bf16[64,1280]{1,0:T(8,128)(2,1)S(1)}, u32[]{:S(2)}, u32[]{:S(2)}) collective-permute-start(bf16[64,1280]{1,0:T(8,128)(2,1)S(1)} %get-tuple-element.51), channel_id=1, source_target_pairs={{0,16},{1,17},{2,18},{3,19},{4,20},{5,21},{6,22},{7,23},{8,24},{9,... | collective-permute-start | bytes 491528 | tf_op jit(solution)/shard_map/ppermute | solution.py:320
  17.5 16.5 %collective-permute-start.11 = (bf16[64,1280]{1,0:T(8,128)(2,1)S(1)}, bf16[64,1280]{1,0:T(8,128)(2,1)S(1)}, u32[]{:S(2)}, u32[]{:S(2)}) collective-permute-start(bf16[64,1280]{1,0:T(8,128)(2,1)S(1)} %get-tuple-element.52), channel_id=1, source_target_pairs={{0,24},{1,25},{2,26},{3,27},{4,28},{5,29},{6,30},{7,31},{8,16},{9,... | collective-permute-start | bytes 491528 | tf_op jit(solution)/shard_map/ppermute | solution.py:320
  24.8 0.9 %copy-start = (bf16[32,2432]{1,0:T(8,128)(2,1)S(1)}, bf16[32,2432]{1,0:T(8,128)(2,1)}, u32[]{:S(2)}) copy-start(bf16[32,2432]{1,0:T(8,128)(2,1)} %get-tuple-element.43.refs_0_) | copy-start | bytes 466948
  27.0 8.9 %collective-permute-start.3 = (bf16[64,2304]{1,0:T(8,128)(2,1)S(1)}, bf16[64,2304]{1,0:T(8,128)(2,1)S(1)}, u32[]{:S(2)}, u32[]{:S(2)}) collective-permute-start(bf16[64,2304]{1,0:T(8,128)(2,1)S(1)} %get-tuple-element.45), channel_id=1, source_target_pairs={{0,2},{1,3},{2,0},{3,1},{4,6},{5,7},{6,4},{7,5},{8,10},{9,11},{10,... | collective-permute-start | bytes 884744 | tf_op jit(solution)/shard_map/ppermute | solution.py:320
  28.0 11.4 %collective-permute-start.4 = (bf16[64,2304]{1,0:T(8,128)(2,1)S(1)}, bf16[64,2304]{1,0:T(8,128)(2,1)S(1)}, u32[]{:S(2)}, u32[]{:S(2)}) collective-permute-start(bf16[64,2304]{1,0:T(8,128)(2,1)S(1)} %get-tuple-element.46), channel_id=1, source_target_pairs={{0,4},{1,5},{2,6},{3,7},{4,0},{5,1},{6,2},{7,3},{8,12},{9,13},{10,... | collective-permute-start | bytes 884744 | tf_op jit(solution)/shard_map/ppermute | solution.py:320
  28.1 11.3 %collective-permute-start.5 = (bf16[64,2304]{1,0:T(8,128)(2,1)S(1)}, bf16[64,2304]{1,0:T(8,128)(2,1)S(1)}, u32[]{:S(2)}, u32[]{:S(2)}) collective-permute-start(bf16[64,2304]{1,0:T(8,128)(2,1)S(1)} %get-tuple-element.47), channel_id=1, source_target_pairs={{0,6},{1,7},{2,4},{3,5},{4,2},{5,3},{6,0},{7,1},{8,14},{9,15},{10,... | collective-permute-start | bytes 884744 | tf_op jit(solution)/shard_map/ppermute | solution.py:320
  34.0 1.4 %collective-permute-start.16 = (bf16[64,1280]{1,0:T(8,128)(2,1)S(1)}, bf16[64,1280]{1,0:T(8,128)(2,1)S(1)}, u32[]{:S(2)}, u32[]{:S(2)}) collective-permute-start(bf16[64,1280]{1,0:T(8,128)(2,1)S(1)} %get-tuple-element.49.refs_4_), channel_id=1, source_target_pairs={{0,1},{1,0},{2,3},{3,2},{4,5},{5,4},{6,7},{7,6},{8,9},{9,8},{10,11... | collective-permute-start | bytes 491528 | tf_op jit(solution)/shard_map/ppermute | solution.py:320
  34.0 1.6 %collective-permute-start.17 = (bf16[64,1280]{1,0:T(8,128)(2,1)S(1)}, bf16[64,1280]{1,0:T(8,128)(2,1)S(1)}, u32[]{:S(2)}, u32[]{:S(2)}) collective-permute-start(bf16[64,1280]{1,0:T(8,128)(2,1)S(1)} %collective-permute-done.9.refs_5_), channel_id=1, source_target_pairs={{0,1},{1,0},{2,3},{3,2},{4,5},{5,4},{6,7},{7,6},{8,9},{9,8},{10,11... | collective-permute-start | bytes 491528 | tf_op jit(solution)/shard_map/ppermute | solution.py:320
  35.4 4.5 %collective-permute-start.18 = (bf16[64,1280]{1,0:T(8,128)(2,1)S(1)}, bf16[64,1280]{1,0:T(8,128)(2,1)S(1)}, u32[]{:S(2)}, u32[]{:S(2)}) collective-permute-start(bf16[64,1280]{1,0:T(8,128)(2,1)S(1)} %collective-permute-done.10.refs_6_), channel_id=1, source_target_pairs={{0,1},{1,0},{2,3},{3,2},{4,5},{5,4},{6,7},{7,6},{8,9},{9,8},{10,11... | collective-permute-start | bytes 491528 | tf_op jit(solution)/shard_map/ppermute | solution.py:320
  35.6 6.0 %collective-permute-start.12 = (bf16[64,2304]{1,0:T(8,128)(2,1)S(1)}, bf16[64,2304]{1,0:T(8,128)(2,1)S(1)}, u32[]{:S(2)}, u32[]{:S(2)}) collective-permute-start(bf16[64,2304]{1,0:T(8,128)(2,1)S(1)} %get-tuple-element.44.refs_0_), channel_id=1, source_target_pairs={{0,1},{1,0},{2,3},{3,2},{4,5},{5,4},{6,7},{7,6},{8,9},{9,8},{10,11... | collective-permute-start | bytes 884744 | tf_op jit(solution)/shard_map/ppermute | solution.py:320
  36.0 5.7 %collective-permute-start.13 = (bf16[64,2304]{1,0:T(8,128)(2,1)S(1)}, bf16[64,2304]{1,0:T(8,128)(2,1)S(1)}, u32[]{:S(2)}, u32[]{:S(2)}) collective-permute-start(bf16[64,2304]{1,0:T(8,128)(2,1)S(1)} %collective-permute-done.3.refs_1_), channel_id=1, source_target_pairs={{0,1},{1,0},{2,3},{3,2},{4,5},{5,4},{6,7},{7,6},{8,9},{9,8},{10,11... | collective-permute-start | bytes 884744 | tf_op jit(solution)/shard_map/ppermute | solution.py:320
  39.4 2.2 %collective-permute-start.14 = (bf16[64,2304]{1,0:T(8,128)(2,1)S(1)}, bf16[64,2304]{1,0:T(8,128)(2,1)S(1)}, u32[]{:S(2)}, u32[]{:S(2)}) collective-permute-start(bf16[64,2304]{1,0:T(8,128)(2,1)S(1)} %collective-permute-done.4.refs_2_), channel_id=1, source_target_pairs={{0,1},{1,0},{2,3},{3,2},{4,5},{5,4},{6,7},{7,6},{8,9},{9,8},{10,11... | collective-permute-start | bytes 884744 | tf_op jit(solution)/shard_map/ppermute | solution.py:320
  39.4 2.2 %collective-permute-start.15 = (bf16[64,2304]{1,0:T(8,128)(2,1)S(1)}, bf16[64,2304]{1,0:T(8,128)(2,1)S(1)}, u32[]{:S(2)}, u32[]{:S(2)}) collective-permute-start(bf16[64,2304]{1,0:T(8,128)(2,1)S(1)} %collective-permute-done.5.refs_3_), channel_id=1, source_target_pairs={{0,1},{1,0},{2,3},{3,2},{4,5},{5,4},{6,7},{7,6},{8,9},{9,8},{10,11... | collective-permute-start | bytes 884744 | tf_op jit(solution)/shard_map/ppermute | solution.py:320
  39.9 1.7 %collective-permute-start.19 = (bf16[64,1280]{1,0:T(8,128)(2,1)S(1)}, bf16[64,1280]{1,0:T(8,128)(2,1)S(1)}, u32[]{:S(2)}, u32[]{:S(2)}) collective-permute-start(bf16[64,1280]{1,0:T(8,128)(2,1)S(1)} %collective-permute-done.11.refs_7_), channel_id=1, source_target_pairs={{0,1},{1,0},{2,3},{3,2},{4,5},{5,4},{6,7},{7,6},{8,9},{9,8},{10,11... | collective-permute-start | bytes 491528 | tf_op jit(solution)/shard_map/ppermute | solution.py:320
  47.3 3.9 %collective-permute-start.20 = (bf16[256,2304]{1,0:T(8,128)(2,1)S(1)}, bf16[256,2304]{1,0:T(8,128)(2,1)S(1)}, u32[]{:S(2)}, u32[]{:S(2)}) collective-permute-start(bf16[256,2304]{1,0:T(8,128)(2,1)S(1)} %get-tuple-element.57), channel_id=1, source_target_pairs={{0,1},{1,0},{2,3},{3,2},{4,5},{5,4},{6,7},{7,6},{8,9},{9,8},{10,11... | collective-permute-start | bytes 3538952 | tf_op jit(solution)/shard_map/ppermute | solution.py:320
  47.6 3.6 %collective-permute-start.21 = (bf16[256,1280]{1,0:T(8,128)(2,1)S(1)}, bf16[256,1280]{1,0:T(8,128)(2,1)S(1)}, u32[]{:S(2)}, u32[]{:S(2)}) collective-permute-start(bf16[256,1280]{1,0:T(8,128)(2,1)S(1)} %get-tuple-element.58), channel_id=1, source_target_pairs={{0,1},{1,0},{2,3},{3,2},{4,5},{5,4},{6,7},{7,6},{8,9},{9,8},{10,11... | collective-permute-start | bytes 1966088 | tf_op jit(solution)/shard_map/ppermute | solution.py:320
  52.5 9.3 %collective-permute-start.28 = (bf16[64,1280]{1,0:T(8,128)(2,1)S(1)}, bf16[64,1280]{1,0:T(8,128)(2,1)S(1)}, u32[]{:S(2)}, u32[]{:S(2)}) collective-permute-start(bf16[64,1280]{1,0:T(8,128)(2,1)S(1)} %get-tuple-element.71), channel_id=1, source_target_pairs={{0,8},{1,9},{2,10},{3,11},{4,12},{5,13},{6,14},{7,15},{8,0},{9,1},... | collective-permute-start | bytes 491528 | tf_op jit(solution)/shard_map/ppermute | solution.py:320
  52.6 15.2 %collective-permute-start.29 = (bf16[64,1280]{1,0:T(8,128)(2,1)S(1)}, bf16[64,1280]{1,0:T(8,128)(2,1)S(1)}, u32[]{:S(2)}, u32[]{:S(2)}) collective-permute-start(bf16[64,1280]{1,0:T(8,128)(2,1)S(1)} %get-tuple-element.72), channel_id=1, source_target_pairs={{0,16},{1,17},{2,18},{3,19},{4,20},{5,21},{6,22},{7,23},{8,24},{9,... | collective-permute-start | bytes 491528 | tf_op jit(solution)/shard_map/ppermute | solution.py:320
  55.7 12.1 %collective-permute-start.30 = (bf16[64,1280]{1,0:T(8,128)(2,1)S(1)}, bf16[64,1280]{1,0:T(8,128)(2,1)S(1)}, u32[]{:S(2)}, u32[]{:S(2)}) collective-permute-start(bf16[64,1280]{1,0:T(8,128)(2,1)S(1)} %get-tuple-element.73), channel_id=1, source_target_pairs={{0,24},{1,25},{2,26},{3,27},{4,28},{5,29},{6,30},{7,31},{8,16},{9,... | collective-permute-start | bytes 491528 | tf_op jit(solution)/shard_map/ppermute | solution.py:320
  57.0 12.7 %collective-permute-start.22 = (bf16[64,2304]{1,0:T(8,128)(2,1)S(1)}, bf16[64,2304]{1,0:T(8,128)(2,1)S(1)}, u32[]{:S(2)}, u32[]{:S(2)}) collective-permute-start(bf16[64,2304]{1,0:T(8,128)(2,1)S(1)} %get-tuple-element.60), channel_id=1, source_target_pairs={{0,2},{1,3},{2,0},{3,1},{4,6},{5,7},{6,4},{7,5},{8,10},{9,11},{10,... | collective-permute-start | bytes 884744 | tf_op jit(solution)/shard_map/ppermute | solution.py:320
  58.5 14.2 %collective-permute-start.23 = (bf16[64,2304]{1,0:T(8,128)(2,1)S(1)}, bf16[64,2304]{1,0:T(8,128)(2,1)S(1)}, u32[]{:S(2)}, u32[]{:S(2)}) collective-permute-start(bf16[64,2304]{1,0:T(8,128)(2,1)S(1)} %get-tuple-element.61), channel_id=1, source_target_pairs={{0,4},{1,5},{2,6},{3,7},{4,0},{5,1},{6,2},{7,3},{8,12},{9,13},{10,... | collective-permute-start | bytes 884744 | tf_op jit(solution)/shard_map/ppermute | solution.py:320
  61.8 10.9 %collective-permute-start.24 = (bf16[64,2304]{1,0:T(8,128)(2,1)S(1)}, bf16[64,2304]{1,0:T(8,128)(2,1)S(1)}, u32[]{:S(2)}, u32[]{:S(2)}) collective-permute-start(bf16[64,2304]{1,0:T(8,128)(2,1)S(1)} %get-tuple-element.62), channel_id=1, source_target_pairs={{0,6},{1,7},{2,4},{3,5},{4,2},{5,3},{6,0},{7,1},{8,14},{9,15},{10,... | collective-permute-start | bytes 884744 | tf_op jit(solution)/shard_map/ppermute | solution.py:320
  68.2 10.8 %collective-permute-start.31 = (bf16[32,1280]{1,0:T(8,128)(2,1)S(1)}, bf16[32,1280]{1,0:T(8,128)(2,1)S(1)}, u32[]{:S(2)}, u32[]{:S(2)}) collective-permute-start(bf16[32,1280]{1,0:T(8,128)(2,1)S(1)} %get-tuple-element.78), channel_id=1, source_target_pairs={{0,2},{1,3},{2,0},{3,1},{4,6},{5,7},{6,4},{7,5},{8,10},{9,11},{10,... | collective-permute-start | bytes 245768 | tf_op jit(solution)/shard_map/ppermute | solution.py:320
  73.3 11.0 %collective-permute-start.25 = (bf16[32,2304]{1,0:T(8,128)(2,1)S(1)}, bf16[32,2304]{1,0:T(8,128)(2,1)S(1)}, u32[]{:S(2)}, u32[]{:S(2)}) collective-permute-start(bf16[32,2304]{1,0:T(8,128)(2,1)S(1)} %get-tuple-element.67), channel_id=1, source_target_pairs={{0,8},{1,9},{2,10},{3,11},{4,12},{5,13},{6,14},{7,15},{8,0},{9,1},... | collective-permute-start | bytes 442376 | tf_op jit(solution)/shard_map/ppermute | solution.py:320
  73.7 13.2 %collective-permute-start.26 = (bf16[32,2304]{1,0:T(8,128)(2,1)S(1)}, bf16[32,2304]{1,0:T(8,128)(2,1)S(1)}, u32[]{:S(2)}, u32[]{:S(2)}) collective-permute-start(bf16[32,2304]{1,0:T(8,128)(2,1)S(1)} %get-tuple-element.68), channel_id=1, source_target_pairs={{0,16},{1,17},{2,18},{3,19},{4,20},{5,21},{6,22},{7,23},{8,24},{9,... | collective-permute-start | bytes 442376 | tf_op jit(solution)/shard_map/ppermute | solution.py:320
  76.2 10.7 %collective-permute-start.27 = (bf16[32,2304]{1,0:T(8,128)(2,1)S(1)}, bf16[32,2304]{1,0:T(8,128)(2,1)S(1)}, u32[]{:S(2)}, u32[]{:S(2)}) collective-permute-start(bf16[32,2304]{1,0:T(8,128)(2,1)S(1)} %get-tuple-element.69), channel_id=1, source_target_pairs={{0,24},{1,25},{2,26},{3,27},{4,28},{5,29},{6,30},{7,31},{8,16},{9,... | collective-permute-start | bytes 442376 | tf_op jit(solution)/shard_map/ppermute | solution.py:320
  77.8 4.4 %collective-permute-start.32 = (bf16[32,1280]{1,0:T(8,128)(2,1)S(1)}, bf16[32,1280]{1,0:T(8,128)(2,1)S(1)}, u32[]{:S(2)}, u32[]{:S(2)}) collective-permute-start(bf16[32,1280]{1,0:T(8,128)(2,1)S(1)} %get-tuple-element.79), channel_id=1, source_target_pairs={{0,4},{1,5},{2,6},{3,7},{4,0},{5,1},{6,2},{7,3},{8,12},{9,13},{10,... | collective-permute-start | bytes 245768 | tf_op jit(solution)/shard_map/ppermute | solution.py:320
  79.0 5.3 %collective-permute-start.33 = (bf16[32,1280]{1,0:T(8,128)(2,1)S(1)}, bf16[32,1280]{1,0:T(8,128)(2,1)S(1)}, u32[]{:S(2)}, u32[]{:S(2)}) collective-permute-start(bf16[32,1280]{1,0:T(8,128)(2,1)S(1)} %get-tuple-element.80), channel_id=1, source_target_pairs={{0,6},{1,7},{2,4},{3,5},{4,2},{5,3},{6,0},{7,1},{8,14},{9,15},{10,... | collective-permute-start | bytes 245768 | tf_op jit(solution)/shard_map/ppermute | solution.py:320

commit v5 on v4

--- a/solution.py
+++ b/solution.py
@@ -14,7 +14,7 @@
 CHUNK = 768
 VMEM_LIMIT = 24 << 20
 LOAD_LIMIT = 41 << 20
-HEAD_LIMIT = 54 << 20
+HEAD_LIMIT = 24 << 20
 GROUPS = 1
 
 
@@ -271,34 +271,20 @@
     )(*first, *second, *weights)
 
 
-def down_kernel(blocks, planes, cap, hidden_ref, down_ref, first_ref, second_ref):
-    split = first_ref.shape[1]
+def down_kernel(sizes, base, reordered, added, hidden_ref, down_ref, *refs):
     hidden = hidden_ref[...]
-    for start, size in tiles(split):
-        part = jnp.dot(hidden, down_ref[0, :, pl.ds(start, size)], preferred_element_type=F32)
-        first_ref[:, pl.ds(start, size)] = part.astype(BF16)
-    hidden = jnp.dot(reorder(blocks, planes, cap, True), hidden, preferred_element_type=F32).astype(BF16)
-    for start, size in tiles(second_ref.shape[1]):
-        part = jnp.dot(hidden, down_ref[0, :, pl.ds(split + start, size)], preferred_element_type=F32)
-        second_ref[:, pl.ds(start, size)] = part.astype(BF16)
-
-
-def add_down_kernel(blocks, planes, cap, hidden_ref, down_ref, first_ref, second_ref, *outs):
-    split = first_ref.shape[1]
-    hidden = hidden_ref[...]
-
-    def halves(hidden, base, other_ref, outs):
-        rows = outs[0].shape[0]
-        for start, size in tiles(other_ref.shape[1]):
-            columns = pl.ds(start, size)
-            part = jnp.dot(hidden, down_ref[0, :, pl.ds(base + start, size)], preferred_element_type=F32)
-            both = (part + other_ref[:, columns].astype(F32)).astype(BF16)
-            for number, out in enumerate(outs):
-                out[:, columns] = both[number * rows : (number + 1) * rows]
-
-    halves(hidden, 0, first_ref, outs[: planes * GROUPS])
-    hidden = jnp.dot(reorder(blocks, planes, cap, True), hidden, preferred_element_type=F32).astype(BF16)
-    halves(hidden, split, second_ref, outs[planes * GROUPS :])
+    if reordered:
+        hidden = jnp.dot(reorder(*sizes, True), hidden, preferred_element_type=F32).astype(BF16)
+    outs = refs[1:] if added else refs
+    rows = outs[0].shape[0]
+    for start, size in tiles(outs[0].shape[1]):
+        columns = pl.ds(start, size)
+        part = jnp.dot(hidden, down_ref[0, :, pl.ds(base + start, size)], preferred_element_type=F32)
+        if added:
+            part += refs[0][:, columns].astype(F32)
+        part = part.astype(BF16)
+        for number, out in enumerate(outs):
+            out[:, columns] = part[number * rows : (number + 1) * rows]
 
 
 def body(moe_input, route_ids, route_weights, gate_weight, up_weight, down_weight):
@@ -368,18 +354,20 @@
         sizes, first_other, second_other, gate_weight, up_weight, down_weight
     )
     hidden_mine = hidden_of(first, second)
-    parts = call(
-        functools.partial(down_kernel, *sizes),
-        shaped(1, (slots, split)) + shaped(1, (slots, rest)),
-        hidden_other, down_weight,
-        flops=2 * slots * width * hidden_width, scale=1,
-    )
-    results = call(
-        functools.partial(add_down_kernel, *sizes),
-        shaped(planes * GROUPS, (group * cap, split)) + shaped(blocks, (planes * cap, rest)),
-        hidden_mine, down_weight, swap(parts[0], 1), swap(parts[1], 1),
-        flops=2 * slots * width * hidden_width, scale=1,
-    )
+    def down(hidden, base, count, columns, *received):
+        return call(
+            functools.partial(down_kernel, sizes, base, base > 0, len(received) > 0),
+            shaped(count, (slots // count, columns)),
+            hidden, down_weight, *received,
+            flops=2 * slots * columns * hidden_width,
+        )
+
+    other_second = swap(down(hidden_other, split, 1, rest)[0], 1)
+    other_first = swap(down(hidden_other, 0, 1, split)[0], 1)
+    results_second = down(hidden_mine, split, blocks, rest, other_second)
+    results_first = down(hidden_mine, 0, planes, split, other_first)
+    results = list(results_first) + list(results_second)
+
     def combine(arrays, factors, sources, columns, own, scale):
         return call(
             functools.partial(combine_kernel, sources, len(arrays)),

time: 87.9 us -> 86.4 us (0.983)
  Pallas kernels: 15.4 us -> 14.2 us
    pallas_call x1, Pallas kernels: 1.7 us -> 0.21 us  [tagged_parts(): pl.pallas_call(functools.partial(tag_kernel, experts), out_shape=shaped(1...]
    unnamed x4 -> x6, local copies, waits for them, and re-layouts: 1.8 us -> 2.31 us
    pallas_call x8 -> x10, Pallas kernels: 9.29 us -> 9.6 us  [call(): pl.pallas_call(kernel, out_shape=out_shapes, in_specs=[smem] * scalars +...]
  transfers between devices with their start and end apart: 34 -> 34, of which waited for: 16 -> 15; matrix products, arithmetic and copies ran while one was open for 0% -> 0% of each run, Pallas kernels for 7% -> 9%
where the time goes in v5:
time: 86.4 us; the launch traced here: 86.2 us
  starting transfers between devices  35.3 us (41%)
  waiting for transfers between devices  34.3 us (40%)
  Pallas kernels  14.2 us (16%)
  local copies, waits for them, and re-layouts  2.31 us (3%)
    ppermute x34, starting transfers between devices, swap(): return lax.ppermute(array, 'ep', [(i, i ^ mask) for i in range(devices)])  35.3 us
    ppermute x34, waiting for transfers between devices, swap(): return lax.ppermute(array, 'ep', [(i, i ^ mask) for i in range(devices)])  34.3 us
    pallas_call x10, Pallas kernels, call(): pl.pallas_call(kernel, out_shape=out_shapes, in_specs=[smem] * scalars +...  9.6 us
    pallas_call x1, Pallas kernels, load_hidden(): pl.pallas_call(functools.partial(load_hidden_kernel, *sizes), out_shape=s...  4.38 us
    unnamed x6, local copies, waits for them, and re-layouts  2.31 us
  transfers between devices with their start and end apart: 34, of which 15 were waited for; matrix products, arithmetic and copies ran while one was open for 0% of the time, Pallas kernels for 9%

profile of v5, /device:TPU:0, one launch (start us, length us, event | category | flops | bytes accessed | tf_op | source)
XLA Modules:
  0.0 86.2 jit_solution(10833684245634581012)
XLA Ops:
  0.0 0.9 %copy-done = bf16[32,3584]{1,0:T(8,128)(2,1)S(1)} copy-done((bf16[32,3584]{1,0:T(8,128)(2,1)S(1)}, bf16[32,3584]{1,0:T(8,128)(2,1)}, u32[]{:S(2)}) %copy-start) | copy-done | bytes 229400
  0.9 0.7 copy-done.1
  1.6 0.7 copy-done.2
  2.5 4.0 %collective-permute-start.8 = (bf16[32,1408]{1,0:T(8,128)(2,1)S(1)}, bf16[32,1408]{1,0:T(8,128)(2,1)S(1)}, u32[]{:S(2)}, u32[]{:S(2)}) collective-permute-start(bf16[32,1408]{1,0:T(8,128)(2,1)S(1)} %get-tuple-element.46.refs_0_), channel_id=1, source_target_pairs={{0,6},{1,7},{2,4},{3,5},{4,2},{5,3},{6,0},{7,1},{8,14},{9,15},{10,... | collective-permute-start | bytes 270344 | tf_op jit(solution)/shard_map/ppermute | solution.py:306
  6.5 3.6 %collective-permute-start.2 = (bf16[32,2432]{1,0:T(8,128)(2,1)S(1)}, bf16[32,2432]{1,0:T(8,128)(2,1)S(1)}, u32[]{:S(2)}, u32[]{:S(2)}) collective-permute-start(bf16[32,2432]{1,0:T(8,128)(2,1)S(1)} %get-tuple-element.41.refs_0_), channel_id=1, source_target_pairs={{0,24},{1,25},{2,26},{3,27},{4,28},{5,29},{6,30},{7,31},{8,16},{9,... | collective-permute-start | bytes 466952 | tf_op jit(solution)/shard_map/ppermute | solution.py:306
  10.1 0.5 collective-permute-start.7
  10.6 0.5 collective-permute-start.6
  11.1 0.6 collective-permute-start
  11.7 2.9 %collective-permute-done.7.refs_2_ = bf16[32,1408]{1,0:T(8,128)(2,1)S(1)} collective-permute-done((bf16[32,1408]{1,0:T(8,128)(2,1)S(1)}, bf16[32,1408]{1,0:T(8,128)(2,1)S(1)}, u32[]{:S(2)}, u32[]{:S(2)}) %collective-permute-start.7) | collective-permute-done | bytes 90144 | tf_op jit(solution)/shard_map/ppermute | solution.py:306
  14.6 0.5 collective-permute-done.6.refs_1_
  15.1 1.2 %shard_map.66 = (bf16[64,1280]{1,0:T(8,128)(2,1)S(1)}, bf16[64,1280]{1,0:T(8,128)(2,1)S(1)}, bf16[64,1280]{1,0:T(8,128)(2,1)S(1)}, bf16[64,1280]{1,0:T(8,128)(2,...) custom-call(s32[1,4]{1,0:T(1,128)S(1)} %multiply_add_fusion.e_ref, ...), custom_call_target="tpu_custom_call" | custom-call | flops 838860 | bytes 12124 | tf_op jit(solution)/shard_map/pallas_call | solution.py:26
  16.4 1.0 %collective-permute-start.10 = (bf16[64,1280]{1,0:T(8,128)(2,1)S(1)}, bf16[64,1280]{1,0:T(8,128)(2,1)S(1)}, u32[]{:S(2)}, u32[]{:S(2)}) collective-permute-start(bf16[64,1280]{1,0:T(8,128)(2,1)S(1)} %get-tuple-element.49), channel_id=1, source_target_pairs={{0,16},{1,17},{2,18},{3,19},{4,20},{5,21},{6,22},{7,23},{8,24},{9,... | collective-permute-start | bytes 491528 | tf_op jit(solution)/shard_map/ppermute | solution.py:306
  17.4 3.4 %collective-permute-start.11 = (bf16[64,1280]{1,0:T(8,128)(2,1)S(1)}, bf16[64,1280]{1,0:T(8,128)(2,1)S(1)}, u32[]{:S(2)}, u32[]{:S(2)}) collective-permute-start(bf16[64,1280]{1,0:T(8,128)(2,1)S(1)} %get-tuple-element.50), channel_id=1, source_target_pairs={{0,24},{1,25},{2,26},{3,27},{4,28},{5,29},{6,30},{7,31},{8,16},{9,... | collective-permute-start | bytes 491528 | tf_op jit(solution)/shard_map/ppermute | solution.py:306
  20.8 4.5 %collective-permute-done.1.refs_2_ = bf16[32,2432]{1,0:T(8,128)(2,1)S(1)} collective-permute-done((bf16[32,2432]{1,0:T(8,128)(2,1)S(1)}, bf16[32,2432]{1,0:T(8,128)(2,1)S(1)}, u32[]{:S(2)}, u32[]{:S(2)}) %collective-permute-start.1) | collective-permute-done | bytes 155680 | tf_op jit(solution)/shard_map/ppermute | solution.py:306
  25.4 1.4 %shard_map.65 = (bf16[64,2304]{1,0:T(8,128)(2,1)S(1)}, bf16[64,2304]{1,0:T(8,128)(2,1)S(1)}, bf16[64,2304]{1,0:T(8,128)(2,1)S(1)}, bf16[64,2304]{1,0:T(8,128)(2,...) custom-call(s32[1,4]{1,0:T(1,128)S(1)} %xor_add_fusion.e_ref, ...), custom_call_target="tpu_custom_call" | custom-call | flops 150994944 | bytes 1998864 | tf_op jit(solution)/shard_map/pallas_call | solution.py:26
  26.7 1.0 %collective-permute-start.3 = (bf16[64,2304]{1,0:T(8,128)(2,1)S(1)}, bf16[64,2304]{1,0:T(8,128)(2,1)S(1)}, u32[]{:S(2)}, u32[]{:S(2)}) collective-permute-start(bf16[64,2304]{1,0:T(8,128)(2,1)S(1)} %get-tuple-element.43), channel_id=1, source_target_pairs={{0,2},{1,3},{2,0},{3,1},{4,6},{5,7},{6,4},{7,5},{8,10},{9,11},{10,... | collective-permute-start | bytes 884744 | tf_op jit(solution)/shard_map/ppermute | solution.py:306
  27.8 2.5 %collective-permute-start.5 = (bf16[64,2304]{1,0:T(8,128)(2,1)S(1)}, bf16[64,2304]{1,0:T(8,128)(2,1)S(1)}, u32[]{:S(2)}, u32[]{:S(2)}) collective-permute-start(bf16[64,2304]{1,0:T(8,128)(2,1)S(1)} %get-tuple-element.45), channel_id=1, source_target_pairs={{0,6},{1,7},{2,4},{3,5},{4,2},{5,3},{6,0},{7,1},{8,14},{9,15},{10,... | collective-permute-start | bytes 884744 | tf_op jit(solution)/shard_map/ppermute | solution.py:306
  30.3 4.3 %collective-permute-done.10.refs_6_ = bf16[64,1280]{1,0:T(8,128)(2,1)S(1)} collective-permute-done((bf16[64,1280]{1,0:T(8,128)(2,1)S(1)}, bf16[64,1280]{1,0:T(8,128)(2,1)S(1)}, u32[]{:S(2)}, u32[]{:S(2)}) %collective-permute-start.10) | collective-permute-done | bytes 163872 | tf_op jit(solution)/shard_map/ppermute | solution.py:306
  34.6 0.5 collective-permute-start.17
  35.1 0.9 %collective-permute-done.16.refs_4_ = bf16[64,1280]{1,0:T(8,128)(2,1)S(1)} collective-permute-done((bf16[64,1280]{1,0:T(8,128)(2,1)S(1)}, bf16[64,1280]{1,0:T(8,128)(2,1)S(1)}, u32[]{:S(2)}, u32[]{:S(2)}) %collective-permute-start.16) | collective-permute-done | bytes 163872 | tf_op jit(solution)/shard_map/ppermute | solution.py:306
  36.7 2.4 %collective-permute-done.4.refs_2_ = bf16[64,2304]{1,0:T(8,128)(2,1)S(1)} collective-permute-done((bf16[64,2304]{1,0:T(8,128)(2,1)S(1)}, bf16[64,2304]{1,0:T(8,128)(2,1)S(1)}, u32[]{:S(2)}, u32[]{:S(2)}) %collective-permute-start.4) | collective-permute-done | bytes 294944 | tf_op jit(solution)/shard_map/ppermute | solution.py:306
  39.1 0.5 collective-permute-start.15
  39.7 1.6 %collective-permute-done.19.refs_7_ = bf16[64,1280]{1,0:T(8,128)(2,1)S(1)} collective-permute-done((bf16[64,1280]{1,0:T(8,128)(2,1)S(1)}, bf16[64,1280]{1,0:T(8,128)(2,1)S(1)}, u32[]{:S(2)}, u32[]{:S(2)}) %collective-permute-start.19) | collective-permute-done | bytes 163872 | tf_op jit(solution)/shard_map/ppermute | solution.py:306
  41.3 4.4 %shard_map.67 = (bf16[256,512]{1,0:T(8,128)(2,1)S(1)}, bf16[1,3584,512]{2,1,0:T(8,128)(2,1)S(1)}, bf16[1,3584,512]{2,1,0:T(8,128)(2,1)S(1)}, bf16[1,512,3584]{2,1,0:T(8,128)(2,1)S(1)}) custom-call(bf16[64,2304]{1,0:T(8,128)(2,1)S(1)} %collective-permute-done.12.refs_0_, bf16[64,2304]{1,0:T(8,128)(2,1)S(1)} %collective-permute-done.13.refs_1_, ...), custom_call_target="tpu_custom_call" | custom-call | flops 1879048192 | bytes 11010048 | tf_op jit(solution)/shard_map/pallas_call | solution.py:255
  45.7 0.8 shard_map.69
  46.7 0.7 shard_map.72
  47.8 2.2 %shard_map.68.hidden_ref = bf16[256,512]{1,0:T(8,128)(2,1)S(1)} custom-call(bf16[64,2304]{1,0:T(8,128)(2,1)S(1)} %get-tuple-element.42.refs_0_, bf16[64,2304]{1,0:T(8,128)(2,1)S(1)} %collective-permute-done.3.refs_1_, bf16[64,2304]{1,0:T(8,128)(2,1)S(1)} %collective-permute-done.4.refs_2_, bf16[64,2304]{1,0:T(8,128)(2,1)S(1)} %collective-permute-done.5.refs_3_, ...), custom_call_target="tpu_custom_call" | custom-call | flops 1879048192 | bytes 9437184 | tf_op jit(solution)/shard_map/pallas_call | solution.py:26
  50.4 0.7 shard_map.73
  51.0 0.9 %collective-permute-start.28 = (bf16[64,1280]{1,0:T(8,128)(2,1)S(1)}, bf16[64,1280]{1,0:T(8,128)(2,1)S(1)}, u32[]{:S(2)}, u32[]{:S(2)}) collective-permute-start(bf16[64,1280]{1,0:T(8,128)(2,1)S(1)} %get-tuple-element.67), channel_id=1, source_target_pairs={{0,8},{1,9},{2,10},{3,11},{4,12},{5,13},{6,14},{7,15},{8,0},{9,1},... | collective-permute-start | bytes 491528 | tf_op jit(solution)/shard_map/ppermute | solution.py:306
  51.9 3.0 %collective-permute-start.29 = (bf16[64,1280]{1,0:T(8,128)(2,1)S(1)}, bf16[64,1280]{1,0:T(8,128)(2,1)S(1)}, u32[]{:S(2)}, u32[]{:S(2)}) collective-permute-start(bf16[64,1280]{1,0:T(8,128)(2,1)S(1)} %get-tuple-element.68), channel_id=1, source_target_pairs={{0,16},{1,17},{2,18},{3,19},{4,20},{5,21},{6,22},{7,23},{8,24},{9,... | collective-permute-start | bytes 491528 | tf_op jit(solution)/shard_map/ppermute | solution.py:306
  55.0 0.5 collective-permute-start.30
  55.5 0.8 shard_map.70
  56.3 1.6 %collective-permute-start.21 = (bf16[64,2304]{1,0:T(8,128)(2,1)S(1)}, bf16[64,2304]{1,0:T(8,128)(2,1)S(1)}, u32[]{:S(2)}, u32[]{:S(2)}) collective-permute-start(bf16[64,2304]{1,0:T(8,128)(2,1)S(1)} %get-tuple-element.56), channel_id=1, source_target_pairs={{0,2},{1,3},{2,0},{3,1},{4,6},{5,7},{6,4},{7,5},{8,10},{9,11},{10,... | collective-permute-start | bytes 884744 | tf_op jit(solution)/shard_map/ppermute | solution.py:306
  57.9 0.6 collective-permute-start.22
  58.4 1.9 %collective-permute-done.28.refs_1_ = bf16[64,1280]{1,0:T(8,128)(2,1)S(1)} collective-permute-done((bf16[64,1280]{1,0:T(8,128)(2,1)S(1)}, bf16[64,1280]{1,0:T(8,128)(2,1)S(1)}, u32[]{:S(2)}, u32[]{:S(2)}) %collective-permute-start.28) | collective-permute-done | bytes 163872 | tf_op jit(solution)/shard_map/ppermute | solution.py:306
  60.4 1.4 %collective-permute-start.23 = (bf16[64,2304]{1,0:T(8,128)(2,1)S(1)}, bf16[64,2304]{1,0:T(8,128)(2,1)S(1)}, u32[]{:S(2)}, u32[]{:S(2)}) collective-permute-start(bf16[64,2304]{1,0:T(8,128)(2,1)S(1)} %get-tuple-element.58), channel_id=1, source_target_pairs={{0,6},{1,7},{2,4},{3,5},{4,2},{5,3},{6,0},{7,1},{8,14},{9,15},{10,... | collective-permute-start | bytes 884744 | tf_op jit(solution)/shard_map/ppermute | solution.py:306
  61.7 5.3 %collective-permute-done.29.refs_2_ = bf16[64,1280]{1,0:T(8,128)(2,1)S(1)} collective-permute-done((bf16[64,1280]{1,0:T(8,128)(2,1)S(1)}, bf16[64,1280]{1,0:T(8,128)(2,1)S(1)}, u32[]{:S(2)}, u32[]{:S(2)}) %collective-permute-start.29) | collective-permute-done | bytes 163872 | tf_op jit(solution)/shard_map/ppermute | solution.py:306
  67.5 0.7 collective-permute-start.31
  68.2 3.9 %collective-permute-done.22.refs_2_ = bf16[64,2304]{1,0:T(8,128)(2,1)S(1)} collective-permute-done((bf16[64,2304]{1,0:T(8,128)(2,1)S(1)}, bf16[64,2304]{1,0:T(8,128)(2,1)S(1)}, u32[]{:S(2)}, u32[]{:S(2)}) %collective-permute-start.22) | collective-permute-done | bytes 294944 | tf_op jit(solution)/shard_map/ppermute | solution.py:306
  72.1 0.6 shard_map.71
  72.8 2.7 %collective-permute-start.25 = (bf16[32,2304]{1,0:T(8,128)(2,1)S(1)}, bf16[32,2304]{1,0:T(8,128)(2,1)S(1)}, u32[]{:S(2)}, u32[]{:S(2)}) collective-permute-start(bf16[32,2304]{1,0:T(8,128)(2,1)S(1)} %get-tuple-element.64), channel_id=1, source_target_pairs={{0,16},{1,17},{2,18},{3,19},{4,20},{5,21},{6,22},{7,23},{8,24},{9,... | collective-permute-start | bytes 442376 | tf_op jit(solution)/shard_map/ppermute | solution.py:306
  75.5 1.7 %collective-permute-start.26 = (bf16[32,2304]{1,0:T(8,128)(2,1)S(1)}, bf16[32,2304]{1,0:T(8,128)(2,1)S(1)}, u32[]{:S(2)}, u32[]{:S(2)}) collective-permute-start(bf16[32,2304]{1,0:T(8,128)(2,1)S(1)} %get-tuple-element.65), channel_id=1, source_target_pairs={{0,24},{1,25},{2,26},{3,27},{4,28},{5,29},{6,30},{7,31},{8,16},{9,... | collective-permute-start | bytes 442376 | tf_op jit(solution)/shard_map/ppermute | solution.py:306
  77.2 1.2 %collective-permute-start.32 = (bf16[32,1280]{1,0:T(8,128)(2,1)S(1)}, bf16[32,1280]{1,0:T(8,128)(2,1)S(1)}, u32[]{:S(2)}, u32[]{:S(2)}) collective-permute-start(bf16[32,1280]{1,0:T(8,128)(2,1)S(1)} %get-tuple-element.75), channel_id=1, source_target_pairs={{0,4},{1,5},{2,6},{3,7},{4,0},{5,1},{6,2},{7,3},{8,12},{9,13},{10,... | collective-permute-start | bytes 245768 | tf_op jit(solution)/shard_map/ppermute | solution.py:306
  78.4 1.5 %collective-permute-start.33 = (bf16[32,1280]{1,0:T(8,128)(2,1)S(1)}, bf16[32,1280]{1,0:T(8,128)(2,1)S(1)}, u32[]{:S(2)}, u32[]{:S(2)}) collective-permute-start(bf16[32,1280]{1,0:T(8,128)(2,1)S(1)} %get-tuple-element.76), channel_id=1, source_target_pairs={{0,6},{1,7},{2,4},{3,5},{4,2},{5,3},{6,0},{7,1},{8,14},{9,15},{10,... | collective-permute-start | bytes 245768 | tf_op jit(solution)/shard_map/ppermute | solution.py:306
  79.9 1.8 %collective-permute-done.32.refs_6_ = bf16[32,1280]{1,0:T(8,128)(2,1)S(1)} collective-permute-done((bf16[32,1280]{1,0:T(8,128)(2,1)S(1)}, bf16[32,1280]{1,0:T(8,128)(2,1)S(1)}, u32[]{:S(2)}, u32[]{:S(2)}) %collective-permute-start.32) | collective-permute-done | bytes 81952 | tf_op jit(solution)/shard_map/ppermute | solution.py:306
  81.6 2.1 %collective-permute-done.33.refs_7_ = bf16[32,1280]{1,0:T(8,128)(2,1)S(1)} collective-permute-done((bf16[32,1280]{1,0:T(8,128)(2,1)S(1)}, bf16[32,1280]{1,0:T(8,128)(2,1)S(1)}, u32[]{:S(2)}, u32[]{:S(2)}) %collective-permute-start.33) | collective-permute-done | bytes 81952 | tf_op jit(solution)/shard_map/ppermute | solution.py:306
  83.7 1.7 %collective-permute-done.25.refs_2_ = bf16[32,2304]{1,0:T(8,128)(2,1)S(1)} collective-permute-done((bf16[32,2304]{1,0:T(8,128)(2,1)S(1)}, bf16[32,2304]{1,0:T(8,128)(2,1)S(1)}, u32[]{:S(2)}, u32[]{:S(2)}) %collective-permute-start.25) | collective-permute-done | bytes 147488 | tf_op jit(solution)/shard_map/ppermute | solution.py:306
  85.4 0.8 shard_map.75
  (40 shorter events, 2.7 us)
Async XLA Ops:
  0.0 0.9 %copy-start = (bf16[32,3584]{1,0:T(8,128)(2,1)S(1)}, bf16[32,3584]{1,0:T(8,128)(2,1)}, u32[]{:S(2)}) copy-start(bf16[32,3584]{1,0:T(8,128)(2,1)} %x_hbm.1) | copy-start | bytes 688132
  0.9 0.7 copy-start.1
  1.6 0.7 copy-start.2
  2.5 8.6 %collective-permute-start.8 = (bf16[32,1408]{1,0:T(8,128)(2,1)S(1)}, bf16[32,1408]{1,0:T(8,128)(2,1)S(1)}, u32[]{:S(2)}, u32[]{:S(2)}) collective-permute-start(bf16[32,1408]{1,0:T(8,128)(2,1)S(1)} %get-tuple-element.46.refs_0_), channel_id=1, source_target_pairs={{0,6},{1,7},{2,4},{3,5},{4,2},{5,3},{6,0},{7,1},{8,14},{9,15},{10,... | collective-permute-start | bytes 270344 | tf_op jit(solution)/shard_map/ppermute | solution.py:306
  6.5 10.9 %collective-permute-start.2 = (bf16[32,2432]{1,0:T(8,128)(2,1)S(1)}, bf16[32,2432]{1,0:T(8,128)(2,1)S(1)}, u32[]{:S(2)}, u32[]{:S(2)}) collective-permute-start(bf16[32,2432]{1,0:T(8,128)(2,1)S(1)} %get-tuple-element.41.refs_0_), channel_id=1, source_target_pairs={{0,24},{1,25},{2,26},{3,27},{4,28},{5,29},{6,30},{7,31},{8,16},{9,... | collective-permute-start | bytes 466952 | tf_op jit(solution)/shard_map/ppermute | solution.py:306
  10.1 4.5 %collective-permute-start.7 = (bf16[32,1408]{1,0:T(8,128)(2,1)S(1)}, bf16[32,1408]{1,0:T(8,128)(2,1)S(1)}, u32[]{:S(2)}, u32[]{:S(2)}) collective-permute-start(bf16[32,1408]{1,0:T(8,128)(2,1)S(1)} %get-tuple-element.46.refs_0_), channel_id=1, source_target_pairs={{0,4},{1,5},{2,6},{3,7},{4,0},{5,1},{6,2},{7,3},{8,12},{9,13},{10,... | collective-permute-start | bytes 270344 | tf_op jit(solution)/shard_map/ppermute | solution.py:306
  10.6 4.5 %collective-permute-start.6 = (bf16[32,1408]{1,0:T(8,128)(2,1)S(1)}, bf16[32,1408]{1,0:T(8,128)(2,1)S(1)}, u32[]{:S(2)}, u32[]{:S(2)}) collective-permute-start(bf16[32,1408]{1,0:T(8,128)(2,1)S(1)} %get-tuple-element.46.refs_0_), channel_id=1, source_target_pairs={{0,2},{1,3},{2,0},{3,1},{4,6},{5,7},{6,4},{7,5},{8,10},{9,11},{10,... | collective-permute-start | bytes 270344 | tf_op jit(solution)/shard_map/ppermute | solution.py:306
  11.1 14.2 %collective-permute-start.1 = (bf16[32,2432]{1,0:T(8,128)(2,1)S(1)}, bf16[32,2432]{1,0:T(8,128)(2,1)S(1)}, u32[]{:S(2)}, u32[]{:S(2)}) collective-permute-start(bf16[32,2432]{1,0:T(8,128)(2,1)S(1)} %get-tuple-element.41.refs_0_), channel_id=1, source_target_pairs={{0,16},{1,17},{2,18},{3,19},{4,20},{5,21},{6,22},{7,23},{8,24},{9,... | collective-permute-start | bytes 466952 | tf_op jit(solution)/shard_map/ppermute | solution.py:306
  11.1 14.2 %collective-permute-start = (bf16[32,2432]{1,0:T(8,128)(2,1)S(1)}, bf16[32,2432]{1,0:T(8,128)(2,1)S(1)}, u32[]{:S(2)}, u32[]{:S(2)}) collective-permute-start(bf16[32,2432]{1,0:T(8,128)(2,1)S(1)} %get-tuple-element.41.refs_0_), channel_id=1, source_target_pairs={{0,8},{1,9},{2,10},{3,11},{4,12},{5,13},{6,14},{7,15},{8,0},{9,1},... | collective-permute-start | bytes 466952 | tf_op jit(solution)/shard_map/ppermute | solution.py:306
  16.4 11.5 %collective-permute-start.9 = (bf16[64,1280]{1,0:T(8,128)(2,1)S(1)}, bf16[64,1280]{1,0:T(8,128)(2,1)S(1)}, u32[]{:S(2)}, u32[]{:S(2)}) collective-permute-start(bf16[64,1280]{1,0:T(8,128)(2,1)S(1)} %get-tuple-element.48), channel_id=1, source_target_pairs={{0,8},{1,9},{2,10},{3,11},{4,12},{5,13},{6,14},{7,15},{8,0},{9,1},... | collective-permute-start | bytes 491528 | tf_op jit(solution)/shard_map/ppermute | solution.py:306
  16.4 18.1 %collective-permute-start.10 = (bf16[64,1280]{1,0:T(8,128)(2,1)S(1)}, bf16[64,1280]{1,0:T(8,128)(2,1)S(1)}, u32[]{:S(2)}, u32[]{:S(2)}) collective-permute-start(bf16[64,1280]{1,0:T(8,128)(2,1)S(1)} %get-tuple-element.49), channel_id=1, source_target_pairs={{0,16},{1,17},{2,18},{3,19},{4,20},{5,21},{6,22},{7,23},{8,24},{9,... | collective-permute-start | bytes 491528 | tf_op jit(solution)/shard_map/ppermute | solution.py:306
  17.4 17.2 %collective-permute-start.11 = (bf16[64,1280]{1,0:T(8,128)(2,1)S(1)}, bf16[64,1280]{1,0:T(8,128)(2,1)S(1)}, u32[]{:S(2)}, u32[]{:S(2)}) collective-permute-start(bf16[64,1280]{1,0:T(8,128)(2,1)S(1)} %get-tuple-element.50), channel_id=1, source_target_pairs={{0,24},{1,25},{2,26},{3,27},{4,28},{5,29},{6,30},{7,31},{8,16},{9,... | collective-permute-start | bytes 491528 | tf_op jit(solution)/shard_map/ppermute | solution.py:306
  26.7 9.7 %collective-permute-start.3 = (bf16[64,2304]{1,0:T(8,128)(2,1)S(1)}, bf16[64,2304]{1,0:T(8,128)(2,1)S(1)}, u32[]{:S(2)}, u32[]{:S(2)}) collective-permute-start(bf16[64,2304]{1,0:T(8,128)(2,1)S(1)} %get-tuple-element.43), channel_id=1, source_target_pairs={{0,2},{1,3},{2,0},{3,1},{4,6},{5,7},{6,4},{7,5},{8,10},{9,11},{10,... | collective-permute-start | bytes 884744 | tf_op jit(solution)/shard_map/ppermute | solution.py:306
  27.7 11.4 %collective-permute-start.4 = (bf16[64,2304]{1,0:T(8,128)(2,1)S(1)}, bf16[64,2304]{1,0:T(8,128)(2,1)S(1)}, u32[]{:S(2)}, u32[]{:S(2)}) collective-permute-start(bf16[64,2304]{1,0:T(8,128)(2,1)S(1)} %get-tuple-element.44), channel_id=1, source_target_pairs={{0,4},{1,5},{2,6},{3,7},{4,0},{5,1},{6,2},{7,3},{8,12},{9,13},{10,... | collective-permute-start | bytes 884744 | tf_op jit(solution)/shard_map/ppermute | solution.py:306
  27.8 11.3 %collective-permute-start.5 = (bf16[64,2304]{1,0:T(8,128)(2,1)S(1)}, bf16[64,2304]{1,0:T(8,128)(2,1)S(1)}, u32[]{:S(2)}, u32[]{:S(2)}) collective-permute-start(bf16[64,2304]{1,0:T(8,128)(2,1)S(1)} %get-tuple-element.45), channel_id=1, source_target_pairs={{0,6},{1,7},{2,4},{3,5},{4,2},{5,3},{6,0},{7,1},{8,14},{9,15},{10,... | collective-permute-start | bytes 884744 | tf_op jit(solution)/shard_map/ppermute | solution.py:306
  34.6 1.4 %collective-permute-start.16 = (bf16[64,1280]{1,0:T(8,128)(2,1)S(1)}, bf16[64,1280]{1,0:T(8,128)(2,1)S(1)}, u32[]{:S(2)}, u32[]{:S(2)}) collective-permute-start(bf16[64,1280]{1,0:T(8,128)(2,1)S(1)} %get-tuple-element.47.refs_4_), channel_id=1, source_target_pairs={{0,1},{1,0},{2,3},{3,2},{4,5},{5,4},{6,7},{7,6},{8,9},{9,8},{10,11... | collective-permute-start | bytes 491528 | tf_op jit(solution)/shard_map/ppermute | solution.py:306
  34.6 1.6 %collective-permute-start.17 = (bf16[64,1280]{1,0:T(8,128)(2,1)S(1)}, bf16[64,1280]{1,0:T(8,128)(2,1)S(1)}, u32[]{:S(2)}, u32[]{:S(2)}) collective-permute-start(bf16[64,1280]{1,0:T(8,128)(2,1)S(1)} %collective-permute-done.9.refs_5_), channel_id=1, source_target_pairs={{0,1},{1,0},{2,3},{3,2},{4,5},{5,4},{6,7},{7,6},{8,9},{9,8},{10,11... | collective-permute-start | bytes 491528 | tf_op jit(solution)/shard_map/ppermute | solution.py:306
  36.0 3.6 %collective-permute-start.18 = (bf16[64,1280]{1,0:T(8,128)(2,1)S(1)}, bf16[64,1280]{1,0:T(8,128)(2,1)S(1)}, u32[]{:S(2)}, u32[]{:S(2)}) collective-permute-start(bf16[64,1280]{1,0:T(8,128)(2,1)S(1)} %collective-permute-done.10.refs_6_), channel_id=1, source_target_pairs={{0,1},{1,0},{2,3},{3,2},{4,5},{5,4},{6,7},{7,6},{8,9},{9,8},{10,11... | collective-permute-start | bytes 491528 | tf_op jit(solution)/shard_map/ppermute | solution.py:306
  36.2 5.1 %collective-permute-start.12 = (bf16[64,2304]{1,0:T(8,128)(2,1)S(1)}, bf16[64,2304]{1,0:T(8,128)(2,1)S(1)}, u32[]{:S(2)}, u32[]{:S(2)}) collective-permute-start(bf16[64,2304]{1,0:T(8,128)(2,1)S(1)} %get-tuple-element.42.refs_0_), channel_id=1, source_target_pairs={{0,1},{1,0},{2,3},{3,2},{4,5},{5,4},{6,7},{7,6},{8,9},{9,8},{10,11... | collective-permute-start | bytes 884744 | tf_op jit(solution)/shard_map/ppermute | solution.py:306
  36.5 4.8 %collective-permute-start.13 = (bf16[64,2304]{1,0:T(8,128)(2,1)S(1)}, bf16[64,2304]{1,0:T(8,128)(2,1)S(1)}, u32[]{:S(2)}, u32[]{:S(2)}) collective-permute-start(bf16[64,2304]{1,0:T(8,128)(2,1)S(1)} %collective-permute-done.3.refs_1_), channel_id=1, source_target_pairs={{0,1},{1,0},{2,3},{3,2},{4,5},{5,4},{6,7},{7,6},{8,9},{9,8},{10,11... | collective-permute-start | bytes 884744 | tf_op jit(solution)/shard_map/ppermute | solution.py:306
  39.1 2.2 %collective-permute-start.14 = (bf16[64,2304]{1,0:T(8,128)(2,1)S(1)}, bf16[64,2304]{1,0:T(8,128)(2,1)S(1)}, u32[]{:S(2)}, u32[]{:S(2)}) collective-permute-start(bf16[64,2304]{1,0:T(8,128)(2,1)S(1)} %collective-permute-done.4.refs_2_), channel_id=1, source_target_pairs={{0,1},{1,0},{2,3},{3,2},{4,5},{5,4},{6,7},{7,6},{8,9},{9,8},{10,11... | collective-permute-start | bytes 884744 | tf_op jit(solution)/shard_map/ppermute | solution.py:306
  39.1 2.2 %collective-permute-start.15 = (bf16[64,2304]{1,0:T(8,128)(2,1)S(1)}, bf16[64,2304]{1,0:T(8,128)(2,1)S(1)}, u32[]{:S(2)}, u32[]{:S(2)}) collective-permute-start(bf16[64,2304]{1,0:T(8,128)(2,1)S(1)} %collective-permute-done.5.refs_3_), channel_id=1, source_target_pairs={{0,1},{1,0},{2,3},{3,2},{4,5},{5,4},{6,7},{7,6},{8,9},{9,8},{10,11... | collective-permute-start | bytes 884744 | tf_op jit(solution)/shard_map/ppermute | solution.py:306
  39.6 1.7 %collective-permute-start.19 = (bf16[64,1280]{1,0:T(8,128)(2,1)S(1)}, bf16[64,1280]{1,0:T(8,128)(2,1)S(1)}, u32[]{:S(2)}, u32[]{:S(2)}) collective-permute-start(bf16[64,1280]{1,0:T(8,128)(2,1)S(1)} %collective-permute-done.11.refs_7_), channel_id=1, source_target_pairs={{0,1},{1,0},{2,3},{3,2},{4,5},{5,4},{6,7},{7,6},{8,9},{9,8},{10,11... | collective-permute-start | bytes 491528 | tf_op jit(solution)/shard_map/ppermute | solution.py:306
  46.5 9.0 %collective-permute-start.20 = (bf16[256,2304]{1,0:T(8,128)(2,1)S(1)}, bf16[256,2304]{1,0:T(8,128)(2,1)S(1)}, u32[]{:S(2)}, u32[]{:S(2)}) collective-permute-start(bf16[256,2304]{1,0:T(8,128)(2,1)S(1)} %shard_map.69), channel_id=1, source_target_pairs={{0,1},{1,0},{2,3},{3,2},{4,5},{5,4},{6,7},{7,6},{8,9},{9,8},{10,11... | collective-permute-start | bytes 3538952 | tf_op jit(solution)/shard_map/ppermute | solution.py:306
  47.4 3.0 %collective-permute-start.27 = (bf16[256,1280]{1,0:T(8,128)(2,1)S(1)}, bf16[256,1280]{1,0:T(8,128)(2,1)S(1)}, u32[]{:S(2)}, u32[]{:S(2)}) collective-permute-start(bf16[256,1280]{1,0:T(8,128)(2,1)S(1)} %shard_map.72), channel_id=1, source_target_pairs={{0,1},{1,0},{2,3},{3,2},{4,5},{5,4},{6,7},{7,6},{8,9},{9,8},{10,11... | collective-permute-start | bytes 1966088 | tf_op jit(solution)/shard_map/ppermute | solution.py:306
  51.0 9.3 %collective-permute-start.28 = (bf16[64,1280]{1,0:T(8,128)(2,1)S(1)}, bf16[64,1280]{1,0:T(8,128)(2,1)S(1)}, u32[]{:S(2)}, u32[]{:S(2)}) collective-permute-start(bf16[64,1280]{1,0:T(8,128)(2,1)S(1)} %get-tuple-element.67), channel_id=1, source_target_pairs={{0,8},{1,9},{2,10},{3,11},{4,12},{5,13},{6,14},{7,15},{8,0},{9,1},... | collective-permute-start | bytes 491528 | tf_op jit(solution)/shard_map/ppermute | solution.py:306
  51.9 15.1 %collective-permute-start.29 = (bf16[64,1280]{1,0:T(8,128)(2,1)S(1)}, bf16[64,1280]{1,0:T(8,128)(2,1)S(1)}, u32[]{:S(2)}, u32[]{:S(2)}) collective-permute-start(bf16[64,1280]{1,0:T(8,128)(2,1)S(1)} %get-tuple-element.68), channel_id=1, source_target_pairs={{0,16},{1,17},{2,18},{3,19},{4,20},{5,21},{6,22},{7,23},{8,24},{9,... | collective-permute-start | bytes 491528 | tf_op jit(solution)/shard_map/ppermute | solution.py:306
  55.0 12.1 %collective-permute-start.30 = (bf16[64,1280]{1,0:T(8,128)(2,1)S(1)}, bf16[64,1280]{1,0:T(8,128)(2,1)S(1)}, u32[]{:S(2)}, u32[]{:S(2)}) collective-permute-start(bf16[64,1280]{1,0:T(8,128)(2,1)S(1)} %get-tuple-element.69), channel_id=1, source_target_pairs={{0,24},{1,25},{2,26},{3,27},{4,28},{5,29},{6,30},{7,31},{8,16},{9,... | collective-permute-start | bytes 491528 | tf_op jit(solution)/shard_map/ppermute | solution.py:306
  56.3 11.9 %collective-permute-start.21 = (bf16[64,2304]{1,0:T(8,128)(2,1)S(1)}, bf16[64,2304]{1,0:T(8,128)(2,1)S(1)}, u32[]{:S(2)}, u32[]{:S(2)}) collective-permute-start(bf16[64,2304]{1,0:T(8,128)(2,1)S(1)} %get-tuple-element.56), channel_id=1, source_target_pairs={{0,2},{1,3},{2,0},{3,1},{4,6},{5,7},{6,4},{7,5},{8,10},{9,11},{10,... | collective-permute-start | bytes 884744 | tf_op jit(solution)/shard_map/ppermute | solution.py:306
  57.9 14.2 %collective-permute-start.22 = (bf16[64,2304]{1,0:T(8,128)(2,1)S(1)}, bf16[64,2304]{1,0:T(8,128)(2,1)S(1)}, u32[]{:S(2)}, u32[]{:S(2)}) collective-permute-start(bf16[64,2304]{1,0:T(8,128)(2,1)S(1)} %get-tuple-element.57), channel_id=1, source_target_pairs={{0,4},{1,5},{2,6},{3,7},{4,0},{5,1},{6,2},{7,3},{8,12},{9,13},{10,... | collective-permute-start | bytes 884744 | tf_op jit(solution)/shard_map/ppermute | solution.py:306
  60.4 11.8 %collective-permute-start.23 = (bf16[64,2304]{1,0:T(8,128)(2,1)S(1)}, bf16[64,2304]{1,0:T(8,128)(2,1)S(1)}, u32[]{:S(2)}, u32[]{:S(2)}) collective-permute-start(bf16[64,2304]{1,0:T(8,128)(2,1)S(1)} %get-tuple-element.58), channel_id=1, source_target_pairs={{0,6},{1,7},{2,4},{3,5},{4,2},{5,3},{6,0},{7,1},{8,14},{9,15},{10,... | collective-permute-start | bytes 884744 | tf_op jit(solution)/shard_map/ppermute | solution.py:306
  67.5 10.9 %collective-permute-start.31 = (bf16[32,1280]{1,0:T(8,128)(2,1)S(1)}, bf16[32,1280]{1,0:T(8,128)(2,1)S(1)}, u32[]{:S(2)}, u32[]{:S(2)}) collective-permute-start(bf16[32,1280]{1,0:T(8,128)(2,1)S(1)} %get-tuple-element.74), channel_id=1, source_target_pairs={{0,2},{1,3},{2,0},{3,1},{4,6},{5,7},{6,4},{7,5},{8,10},{9,11},{10,... | collective-permute-start | bytes 245768 | tf_op jit(solution)/shard_map/ppermute | solution.py:306
  72.7 11.0 %collective-permute-start.24 = (bf16[32,2304]{1,0:T(8,128)(2,1)S(1)}, bf16[32,2304]{1,0:T(8,128)(2,1)S(1)}, u32[]{:S(2)}, u32[]{:S(2)}) collective-permute-start(bf16[32,2304]{1,0:T(8,128)(2,1)S(1)} %get-tuple-element.63), channel_id=1, source_target_pairs={{0,8},{1,9},{2,10},{3,11},{4,12},{5,13},{6,14},{7,15},{8,0},{9,1},... | collective-permute-start | bytes 442376 | tf_op jit(solution)/shard_map/ppermute | solution.py:306
  72.8 12.6 %collective-permute-start.25 = (bf16[32,2304]{1,0:T(8,128)(2,1)S(1)}, bf16[32,2304]{1,0:T(8,128)(2,1)S(1)}, u32[]{:S(2)}, u32[]{:S(2)}) collective-permute-start(bf16[32,2304]{1,0:T(8,128)(2,1)S(1)} %get-tuple-element.64), channel_id=1, source_target_pairs={{0,16},{1,17},{2,18},{3,19},{4,20},{5,21},{6,22},{7,23},{8,24},{9,... | collective-permute-start | bytes 442376 | tf_op jit(solution)/shard_map/ppermute | solution.py:306
  75.5 9.9 %collective-permute-start.26 = (bf16[32,2304]{1,0:T(8,128)(2,1)S(1)}, bf16[32,2304]{1,0:T(8,128)(2,1)S(1)}, u32[]{:S(2)}, u32[]{:S(2)}) collective-permute-start(bf16[32,2304]{1,0:T(8,128)(2,1)S(1)} %get-tuple-element.65), channel_id=1, source_target_pairs={{0,24},{1,25},{2,26},{3,27},{4,28},{5,29},{6,30},{7,31},{8,16},{9,... | collective-permute-start | bytes 442376 | tf_op jit(solution)/shard_map/ppermute | solution.py:306
  77.2 4.4 %collective-permute-start.32 = (bf16[32,1280]{1,0:T(8,128)(2,1)S(1)}, bf16[32,1280]{1,0:T(8,128)(2,1)S(1)}, u32[]{:S(2)}, u32[]{:S(2)}) collective-permute-start(bf16[32,1280]{1,0:T(8,128)(2,1)S(1)} %get-tuple-element.75), channel_id=1, source_target_pairs={{0,4},{1,5},{2,6},{3,7},{4,0},{5,1},{6,2},{7,3},{8,12},{9,13},{10,... | collective-permute-start | bytes 245768 | tf_op jit(solution)/shard_map/ppermute | solution.py:306
  78.4 5.3 %collective-permute-start.33 = (bf16[32,1280]{1,0:T(8,128)(2,1)S(1)}, bf16[32,1280]{1,0:T(8,128)(2,1)S(1)}, u32[]{:S(2)}, u32[]{:S(2)}) collective-permute-start(bf16[32,1280]{1,0:T(8,128)(2,1)S(1)} %get-tuple-element.76), channel_id=1, source_target_pairs={{0,6},{1,7},{2,4},{3,5},{4,2},{5,3},{6,0},{7,1},{8,14},{9,15},{10,... | collective-permute-start | bytes 245768 | tf_op jit(solution)/shard_map/ppermute | solution.py:306
